TPU v7x, 256 devices: a whole 4x4x8 slice. The times are simulated.
256 devices in a mesh: dp: 8 (over y, core), seq: 32 (over x, z).
Axes of the slice: x: 4, y: 4, z: 8, core: 2. Of those that a mesh axis runs over, the one named last changes fastest.
Arguments:
- states: bfloat16 [8, 8192, 5120], P('dp', 'seq'), may hold values from -6 to 6
- span_start: int32 [8, 512], P('dp', 'seq'), may hold values from 0 to 8191, as said below
- span_end: int32 [8, 512], P('dp', 'seq'), may hold values from 0 to 8191, as said below
- gold: int32 [8, 512], P('dp', 'seq'), may hold values from 0 to 47
- live: int32 [8, 512], P('dp', 'seq'), may hold values 0 or 1
- start_proj: bfloat16 [5120, 1024], P('seq'), may hold values from -0.078125 to 0.078125
- end_proj: bfloat16 [5120, 1024], P('seq'), may hold values from -0.078125 to 0.078125
- biaffine: bfloat16 [48, 1024, 1024], P(None, 'seq'), may hold values from -64 to 64
Outputs:
- span_loss: float32 [8, 512], P('dp', 'seq')
- grad_start: bfloat16 [5120, 1024], P('seq')
- grad_end: bfloat16 [5120, 1024], P('seq')
- grad_biaffine: bfloat16 [48, 1024, 1024], P(None, 'seq')
Inputs may be any that keep to these rules, and one draw needn't show every extreme that they name: `span_start`: the tokens of a schema form 2 * 32 blocks of 128 tokens; index j of seq holds block j and then the mirrored block from the far end. Span s has its start and its end in one of the two blocks held by index s // 16 of seq. span_start <= span_end <= span_start + 31, both in the same block.
All inputs are finite; a program needn't handle non-finite values. No bound on the sum of `live` on one device may be relied on, other than what follows from the above.
Results may differ from a plain program's by a relative error of at most 0.012.
Values may be sent and summed in bfloat16 or wider, within the bound.
No kernel may reach another device: no remote copies, remote signals or barrier semaphores. Data moves between devices by JAX's collectives and lax.ppermute only.
A program may use at most 64 MiB of HBM per device.

v0:
```python
import jax
import jax.numpy as jnp
from jax import lax
from jax.sharding import PartitionSpec as P


def owner_sum(term_rows):
    return lax.psum_scatter(term_rows, "seq", scatter_dimension=0, tiled=True)


def span_gather(values):
    return lax.all_gather(values, "seq", axis=0, tiled=True)


def shards(states, span_start, span_end, gold, live, start_proj, end_proj, biaffine):
    seq_index = lax.axis_index("seq")
    half_rows = states.shape[1] // 2
    own_spans = span_start.shape[1]
    labels, inner_cols, full_width = biaffine.shape
    col_start = seq_index * inner_cols

    def local_rows(tokens):
        block_idx = tokens // half_rows
        return jnp.where(
            block_idx == seq_index,
            tokens - block_idx * half_rows,
            half_rows + tokens - block_idx * half_rows,
        )

    first_rows = jnp.take(states[0], local_rows(span_start[0]), axis=0)
    last_rows = jnp.take(states[0], local_rows(span_end[0]), axis=0)
    endpoints = jnp.stack([first_rows, last_rows], axis=1)
    pieces = lax.all_to_all(endpoints, "seq", split_axis=2, concat_axis=0, tiled=True)
    partial_value = jnp.stack(
        [
            jnp.dot(pieces[:, 0], start_proj, preferred_element_type=jnp.float32),
            jnp.dot(pieces[:, 1], end_proj, preferred_element_type=jnp.float32),
        ],
        axis=1,
    )
    pre_act = owner_sum(partial_value)
    activated, act_back = jax.vjp(jax.nn.gelu, pre_act)
    both_rows = span_gather(activated.astype(jnp.bfloat16))
    left_act = lax.dynamic_slice_in_dim(both_rows[:, 0], col_start, inner_cols, 1)
    right_act = both_rows[:, 1]
    flat_weight = biaffine.reshape(labels * inner_cols, full_width)
    label_image = lax.dot_general(
        right_act, flat_weight, (((1,), (1,)), ((), ())), preferred_element_type=jnp.float32
    ).reshape(-1, labels, inner_cols)
    left_wide = left_act.astype(jnp.float32)
    partial_scores = jnp.sum(label_image * left_wide[:, None, :], axis=2)
    scores = owner_sum(partial_scores)
    log_total = jax.nn.logsumexp(scores, axis=1)
    onehot = (gold[0][:, None] == jnp.arange(labels, dtype=jnp.int32)[None, :]).astype(jnp.float32)
    picked = jnp.sum(scores * onehot, axis=1)
    live_wide = live[0].astype(jnp.float32)
    span_loss = live_wide * (log_total - picked)
    softmax = jnp.exp(scores - log_total[:, None])
    slope_own = (live_wide[:, None] * (softmax - onehot) / own_spans).astype(jnp.bfloat16)
    slope_wide = span_gather(slope_own).astype(jnp.float32)
    grad_left = jnp.sum(slope_wide[:, :, None] * label_image, axis=1)
    outer_rows = (slope_wide[:, :, None] * left_wide[:, None, :]).astype(jnp.bfloat16)
    outer_rows = outer_rows.reshape(-1, labels * inner_cols)
    grad_flat = lax.dot_general(
        outer_rows, right_act, (((0,), (0,)), ((), ())), preferred_element_type=jnp.float32
    )
    grad_right = jnp.dot(outer_rows, flat_weight, preferred_element_type=jnp.float32)
    left_rows = lax.all_to_all(grad_left, "seq", split_axis=0, concat_axis=1, tiled=True)
    right_rows = owner_sum(grad_right[:, None, :])
    total_grad = jnp.concatenate([left_rows[:, None, :], right_rows], axis=1)
    lowered = act_back(total_grad)[0].astype(jnp.bfloat16)
    lowered_all = span_gather(lowered)
    grad_start = lax.dot_general(
        pieces[:, 0],
        lowered_all[:, 0],
        (((0,), (0,)), ((), ())),
        preferred_element_type=jnp.float32,
    )
    grad_end = lax.dot_general(
        pieces[:, 1],
        lowered_all[:, 1],
        (((0,), (0,)), ((), ())),
        preferred_element_type=jnp.float32,
    )
    summed = lax.psum((grad_start, grad_end, grad_flat), "dp")
    return (
        span_loss[None, :],
        summed[0].astype(jnp.bfloat16),
        summed[1].astype(jnp.bfloat16),
        summed[2].reshape(labels, inner_cols, full_width).astype(jnp.bfloat16),
    )


def solution(mesh):
    placed = (
        P("dp", "seq", None),
        P("dp", "seq"),
        P("dp", "seq"),
        P("dp", "seq"),
        P("dp", "seq"),
        P("seq", None),
        P("seq", None),
        P(None, "seq", None),
    )
    return jax.shard_map(
        shards,
        mesh=mesh,
        in_specs=placed,
        out_specs=(P("dp", "seq"), P("seq", None), P("seq", None), P(None, "seq", None)),
        check_vma=False,
    )
```

profile of v0, /device:TPU:1, one launch (start us, length us, event | category | flops | bytes accessed | tf_op | source)
XLA Modules:
  0.0 1024.5 jit_solution(16109681268115575397)
XLA Ops:
  7.2 0.8 compare_and_fusion
  8.1 2.9 gather_fusion
  11.0 2.9 gather_fusion.1
  14.1 4.0 copy.35
  18.2 8.1 reshape.115
  26.3 21.9 %all_to_all.34 = bf16[32,2,2560]{2,1,0:T(2,128)(2,1)} all-to-all(bf16[32,2,2560]{2,1,0:T(2,128)(2,1)S(1)} %reshape.115), channel_id=1, replica_groups=mesh['dp'=8,'seq'=32] {'seq'}, dimensions={0} | all-to-all | bytes 655360 | tf_op jit(solution)/shard_map/all_to_all | solution.py:33
  48.2 9.4 reshape.116
  57.6 6.0 copy.36
  63.6 1.4 convolution_bitcast_fusion
  65.5 2.2 pad_maximum_fusion
  67.9 215.7 %reduce-scatter.6.cloned.1.call-done = f32[16,2,1024]{2,0,1:T(8,128)} async-done(((f32[512,2,1024]{2,0,1:T(8,128)}), f32[16,2,1024]{2,0,1:T(8,128)}) %reduce-scatter.6.cloned.1.call-update) | async-done | bytes 131088 | tf_op jit(solution)/shard_map/reduce_scatter | solution.py:8
  283.6 1.6 multiply_convert_fusion.2
  285.4 79.0 %all-gather.3.cloned.1.call-done = bf16[512,2,1024]{2,0,1:T(8,128)(2,1)} async-done(((bf16[16,2,1024]{2,0,1:T(8,128)(2,1)}), bf16[512,2,1024]{2,0,1:T(8,128)(2,1)}) %all-gather.3.cloned.1.call-update) | async-done | bytes 2097168 | tf_op jit(solution)/shard_map/all_gather | solution.py:12
  364.4 1.3 slice.33
  366.0 5.7 multiply_reduce_fusion.1
  372.6 209.6 %reduce-scatter.10.cloned.1.call-done = f32[16,48]{1,0:T(8,128)} async-done(((f32[512,48]{1,0:T(8,128)}), f32[16,48]{1,0:T(8,128)}) %reduce-scatter.10.cloned.1.call-update) | async-done | bytes 3088
  583.9 31.9 %all_gather.10 = bf16[512,48]{1,0:T(8,128)(2,1)S(1)} all-gather(bf16[16,48]{1,0:T(8,128)(2,1)S(1)} %copy.41), channel_id=1, replica_groups=mesh['dp'=8,'seq'=32] {'seq'}, dimensions={0}, use_global_device_ids=true | all-gather | bytes 50688 | tf_op jit(solution)/shard_map/all_gather | solution.py:12
  615.9 4.0 fusion.4
  620.0 4.3 multiply_convert_fusion
  624.3 1.0 copy.43
  626.1 15.4 %all_to_all.35 = f32[32,1,512]{2,1,0:T(1,128)S(1)} all-to-all(f32[32,1,512]{2,1,0:T(1,128)} %reshape.117), channel_id=1, replica_groups=mesh['dp'=8,'seq'=32] {'seq'}, dimensions={0} | all-to-all | bytes 131072 | tf_op jit(solution)/shard_map/all_to_all | solution.py:68
  642.0 1.4 reduce
  643.5 0.9 reshape.118
  645.2 1.1 broadcast_in_dim.13
  646.3 198.5 %reduce-scatter.8.cloned.1.call-done = f32[16,1,1024]{2,0,1:T(8,128)} async-done(((f32[512,1,1024]{2,0,1:T(8,128)}), f32[16,1,1024]{2,0,1:T(8,128)}) %reduce-scatter.8.cloned.1.call-update) | async-done | bytes 65552 | tf_op jit(solution)/shard_map/reduce_scatter | solution.py:8
  844.8 0.8 constant_dynamic-update-slice_fusion
  846.4 2.4 copy.46
  848.9 4.5 fusion.10
  853.8 71.7 %all-gather.5.cloned.1.call-done = bf16[512,2,1024]{2,0,1:T(8,128)(2,1)} async-done(((bf16[16,2,1024]{2,0,1:T(8,128)(2,1)}), bf16[512,2,1024]{2,0,1:T(8,128)(2,1)}) %all-gather.5.cloned.1.call-update) | async-done | bytes 2097168 | tf_op jit(solution)/shard_map/all_gather | solution.py:12
  925.5 2.6 fusion.8
  928.1 2.6 fusion.7
  930.7 87.3 %all-reduce.2 = (bf16[160,1024]{1,0:T(8,128)(2,1)}, bf16[160,1024]{1,0:T(8,128)(2,1)}, bf16[1536,1024]{1,0:T(8,128)(2,1)}) all-reduce(f32[160,1024]{1,0:T(8,128)} %fusion.8, f32[160,1024]{1,0:T(8,128)} %fusion.7, f32[1536,1024]{1,0:T(8,128)} %fusion.10), channel_id=1, replica_groups=mesh['dp'=8,'seq'=32] {'dp'}, use_global_device_ids=true, to_apply=%region_8.10 | all-reduce | flops 1900544 | bytes 11403264 | tf_op jit(solution)/shard_map/psum | solution.py:85
  (53 shorter events, 7.4 us)
Async XLA Ops:
  7.2 358.8 %copy-start = (bf16[48,32,1024]{2,1,0:T(8,128)(2,1)S(1)}, bf16[48,32,1024]{2,1,0:T(8,128)(2,1)}, u32[]{:S(2)}) copy-start(bf16[48,32,1024]{2,1,0:T(8,128)(2,1)} %param.17) | copy-start | bytes 9437188
  7.2 276.4 %reduce-scatter.6.cloned.1.call-start = ((), (), s32[]{:S(2)}) async-start(), calls=%async_computation.5 | async-start | bytes 4325376 | tf_op jit(solution)/shard_map/reduce_scatter | solution.py:8
  48.2 15.4 %copy-start.4 = (bf16[160,1024]{1,0:T(8,128)(2,1)S(1)}, bf16[160,1024]{1,0:T(8,128)(2,1)}, u32[]{:S(2)}) copy-start(bf16[160,1024]{1,0:T(8,128)(2,1)} %param.16) | copy-start | bytes 983044
  63.6 1.5 copy-start.1
  63.6 1.5 copy-start.5
  67.8 296.6 %all-gather.3.cloned.1.call-start = ((), (), s32[]{:S(2)}) async-start(), calls=%async_computation.6 | async-start | bytes 2162688 | tf_op jit(solution)/shard_map/all_gather | solution.py:12
  285.2 296.9 %reduce-scatter.10.cloned.1.call-start = ((), (), s32[]{:S(2)}) async-start(), calls=%async_computation.9 | async-start | bytes 270336
  365.9 249.9 %copy-start.6 = (f32[512,32]{0,1:T(8,128)}, f32[512,32]{0,1:T(8,128)S(1)}, u32[]{:S(2)}) copy-start(f32[512,32]{0,1:T(8,128)S(1)} %copy.40) | copy-start | bytes 196612
  366.0 6.6 copy-start.8
  366.0 217.7 %copy-start.7 = (s32[1,16]{1,0:T(1,128)S(1)}, s32[1,16]{1,0:T(1,128)}, u32[]{:S(2)}) copy-start(s32[1,16]{1,0:T(1,128)} %param.13) | copy-start | bytes 196
  372.5 472.3 %reduce-scatter.8.cloned.1.call-start = ((), (), s32[]{:S(2)}) async-start(), calls=%async_computation.7 | async-start | bytes 2162688 | tf_op jit(solution)/shard_map/reduce_scatter | solution.py:8
  619.9 305.6 %all-gather.5.cloned.1.call-start = ((), (), s32[]{:S(2)}) async-start(), calls=%async_computation.8 | async-start | bytes 2162688 | tf_op jit(solution)/shard_map/all_gather | solution.py:12
  620.0 225.7 %copy-start.3 = (f32[16,2,1024]{2,0,1:T(8,128)S(1)}, f32[16,2,1024]{2,0,1:T(8,128)}, u32[]{:S(2)}) copy-start(f32[16,2,1024]{2,0,1:T(8,128)} %reduce-scatter.6.cloned.1.call-done) | copy-start | bytes 393220
  846.4 2.4 copy-start.2
Sparse Core Ops, SparseCore 0:
  67.9 215.5 reduce-scatter.5
  287.1 77.3 all-gather.2
  372.6 209.4 reduce-scatter.9
  620.1 224.7 reduce-scatter.7
  848.2 77.3 all-gather.4
where the time goes:
time: 1030 us; the launch traced here: 1020 us
  waiting for transfers between devices  775 us (75%)
  blocking collectives  157 us (15%)
  local copies, waits for them, and re-layouts  44.9 us (4%)
  matrix products  21.2 us (2%)
  between operations  14 us (1%)
  other arithmetic  12.9 us (1%)
    reduce_scatter x2, waiting for transfers between devices, owner_sum(): return lax.psum_scatter(term_rows, 'seq', scatter_dimension=0, tiled=True)  414 us
    unnamed x6, waiting for transfers between devices  210 us
    all_gather x2, waiting for transfers between devices, span_gather(): return lax.all_gather(values, 'seq', axis=0, tiled=True)  151 us
    psum x1, blocking collectives, shards(): summed = lax.psum((grad_start, grad_end, grad_flat), 'dp')  87.3 us
    all_gather x1, blocking collectives, span_gather(): return lax.all_gather(values, 'seq', axis=0, tiled=True)  31.9 us
    all_to_all x1, blocking collectives, shards(): lax.all_to_all(endpoints, 'seq', split_axis=2, concat_axis=0, tiled=True)  21.9 us
    unnamed x25, local copies, waits for them, and re-layouts  20.9 us
  transfers between devices with their start and end apart: 5, of which 5 were waited for; matrix products, arithmetic and copies ran while one was open for 2% of the time, Pallas kernels for 0%

commit v1 on v0

v1 whole, which is shorter than its diff:
```python
import jax
import jax.numpy as jnp
from jax import lax
from jax.sharding import PartitionSpec as P


def exchange(parts):
    return lax.all_to_all(parts, "seq", split_axis=0, concat_axis=0, tiled=True)


def spread(values, count):
    return exchange(jnp.broadcast_to(values[None], (count,) + values.shape))


def shards(states, span_start, span_end, gold, live, start_proj, end_proj, biaffine):
    seq_index = lax.axis_index("seq")
    half_rows = states.shape[1] // 2
    own = span_start.shape[1]
    labels, inner, full = biaffine.shape
    count = full // inner
    depth = start_proj.shape[0]
    spans = own * count

    def local_rows(tokens):
        block_idx = tokens // half_rows
        return jnp.where(
            block_idx == seq_index,
            tokens - block_idx * half_rows,
            half_rows + tokens - block_idx * half_rows,
        )

    picks = jnp.concatenate([local_rows(span_start[0]), local_rows(span_end[0])])
    pick_mat = (picks[:, None] == jnp.arange(2 * half_rows)[None, :]).astype(jnp.bfloat16)
    rows = jnp.dot(pick_mat, states[0], preferred_element_type=jnp.float32).astype(jnp.bfloat16)
    chunks = rows.reshape(2 * own, count, depth).transpose(1, 0, 2)
    tags = jnp.stack([gold[0], live[0]], axis=1).astype(jnp.bfloat16)
    tags = jnp.concatenate([tags, jnp.zeros_like(tags)], axis=0)
    tags = jnp.broadcast_to(tags[None], (count, 2 * own, 2))
    payload = jnp.concatenate([chunks, tags], axis=2)
    payload = jnp.pad(payload, ((0, 0), (0, 0), (0, 256 - depth - 2)))
    got = exchange(payload)
    first = got[:, :own, :depth].reshape(spans, depth)
    last = got[:, own:, :depth].reshape(spans, depth)
    gold_all = got[:, :own, depth].reshape(1, spans).astype(jnp.float32)
    live_all = got[:, :own, depth + 1].reshape(1, spans).astype(jnp.float32)

    def project(weight, piece):
        return lax.dot_general(
            weight, piece, (((0,), (1,)), ((), ())), preferred_element_type=jnp.float32
        ).astype(jnp.bfloat16).reshape(count, inner, spans)

    part = jnp.concatenate([project(start_proj, first), project(end_proj, last)], axis=1)
    pre = jnp.sum(exchange(part).astype(jnp.float32), axis=0)
    act, act_back = jax.vjp(jax.nn.gelu, pre)
    act = act.astype(jnp.bfloat16)
    left = act[:inner].astype(jnp.float32)
    right = spread(act[inner:], count).reshape(full, spans)
    flat_weight = biaffine.reshape(labels * inner, full)
    image = jnp.dot(flat_weight, right, preferred_element_type=jnp.float32).reshape(
        labels, inner, spans
    )
    part_scores = jnp.sum(image * left[None], axis=1)
    score_parts = part_scores.reshape(labels, count, own).transpose(1, 0, 2)
    own_scores = jnp.sum(exchange(score_parts), axis=0)
    scores = spread(own_scores, count).transpose(1, 0, 2).reshape(labels, spans)
    log_total = jax.nn.logsumexp(scores, axis=0, keepdims=True)
    onehot = (gold_all == jnp.arange(labels, dtype=jnp.float32)[:, None]).astype(jnp.float32)
    picked = jnp.sum(scores * onehot, axis=0, keepdims=True)
    loss_all = live_all * (log_total - picked)
    span_loss = lax.dynamic_slice_in_dim(loss_all, seq_index * own, own, 1)
    slope = (live_all * (jnp.exp(scores - log_total) - onehot) / own).astype(jnp.bfloat16)
    slope_wide = slope.astype(jnp.float32)
    grad_left = jnp.sum(slope_wide[:, None, :] * image, axis=0)
    outer = (slope_wide[:, None, :] * left[None]).astype(jnp.bfloat16).reshape(labels * inner, spans)
    grad_right_part = lax.dot_general(
        flat_weight, outer, (((0,), (0,)), ((), ())), preferred_element_type=jnp.float32
    ).astype(jnp.bfloat16)
    grad_flat = lax.dot_general(
        outer, right, (((1,), (1,)), ((), ())), preferred_element_type=jnp.float32
    )
    sum_flat = lax.psum(grad_flat, "dp").astype(jnp.bfloat16)
    grad_right = jnp.sum(
        exchange(grad_right_part.reshape(count, inner, spans)).astype(jnp.float32), axis=0
    )
    lowered = act_back(jnp.concatenate([grad_left, grad_right], axis=0))[0].astype(jnp.bfloat16)
    lowered_all = spread(lowered, count)
    low_left = lowered_all[:, :inner].reshape(full, spans)
    low_right = lowered_all[:, inner:].reshape(full, spans)

    def weight_grad(piece, low):
        return lax.dot_general(
            piece, low, (((0,), (1,)), ((), ())), preferred_element_type=jnp.float32
        )

    grads = jnp.concatenate([weight_grad(first, low_left), weight_grad(last, low_right)], axis=0)
    batch = 8
    grad_parts = grads.astype(jnp.bfloat16).reshape(batch, 2 * depth // batch, full)
    grad_parts = lax.all_to_all(grad_parts, "dp", split_axis=0, concat_axis=0, tiled=True)
    grad_own = jnp.sum(grad_parts.astype(jnp.float32), axis=0).astype(jnp.bfloat16)
    grad_full = lax.all_to_all(
        jnp.broadcast_to(grad_own[None], (batch,) + grad_own.shape),
        "dp",
        split_axis=0,
        concat_axis=0,
        tiled=True,
    ).reshape(2 * depth, full)
    return (
        span_loss,
        grad_full[:depth],
        grad_full[depth:],
        sum_flat.reshape(labels, inner, full),
    )


def solution(mesh):
    placed = (
        P("dp", "seq", None),
        P("dp", "seq"),
        P("dp", "seq"),
        P("dp", "seq"),
        P("dp", "seq"),
        P("seq", None),
        P("seq", None),
        P(None, "seq", None),
    )
    return jax.shard_map(
        shards,
        mesh=mesh,
        in_specs=placed,
        out_specs=(P("dp", "seq"), P("seq", None), P("seq", None), P(None, "seq", None)),
        check_vma=False,
    )
```

time: 1030 us -> 388 us (0.38)
  waiting for transfers between devices: 775 us -> 34.9 us
  blocking collectives: 157 us -> 238 us
  starting transfers between devices: 0.39 us -> 36 us
  between operations: 14 us -> 0.9 us
  local copies, waits for them, and re-layouts: 44.9 us -> 32 us
  other arithmetic: 12.9 us -> 23.6 us
    reduce_scatter x2 -> x0, waiting for transfers between devices: 414 us -> none  [owner_sum(): return lax.psum_scatter(term_rows, 'seq', scatter_dimension=0, tiled=True)]
    unnamed x6 -> x0, waiting for transfers between devices: 210 us -> none
    all_gather x2 -> x0, waiting for transfers between devices: 151 us -> none  [span_gather(): return lax.all_gather(values, 'seq', axis=0, tiled=True)]
    all_to_all x2 -> x4, blocking collectives: 37.4 us -> 165 us  [exchange(): return lax.all_to_all(parts, 'seq', split_axis=0, concat_axis=0, tiled=True)]
    all_to_all x0 -> x5, starting transfers between devices: none -> 36 us  [the longest x3 17.1 us: exchange(): return lax.all_to_all(parts, 'seq', split_axis=0, concat_axis=0, tiled=True)]
    all_to_all x0 -> x5, waiting for transfers between devices: none -> 34.9 us  [the longest x3 30.2 us: exchange(): return lax.all_to_all(parts, 'seq', split_axis=0, concat_axis=0, tiled=True)]
    all_gather x1 -> x0, blocking collectives: 31.9 us -> none  [span_gather(): return lax.all_gather(values, 'seq', axis=0, tiled=True)]
    psum x1, blocking collectives: 87.3 us -> 72.5 us  [shards(): sum_flat = lax.psum(grad_flat, 'dp').astype(jnp.bfloat16)]
  transfers between devices with their start and end apart: 5 -> 5, of which waited for: 5 -> 4; matrix products, arithmetic and copies ran while one was open for 2% -> 4% of each run, Pallas kernels for 0% -> 0%
where the time goes in v1:
time: 388 us; the launch traced here: 385 us
  blocking collectives  238 us (61%)
  starting transfers between devices  36 us (9%)
  waiting for transfers between devices  34.9 us (9%)
  local copies, waits for them, and re-layouts  32 us (8%)
  other arithmetic  23.6 us (6%)
  matrix products  20.4 us (5%)
    all_to_all x4, blocking collectives, exchange(): return lax.all_to_all(parts, 'seq', split_axis=0, concat_axis=0, tiled=True)  165 us
    psum x1, blocking collectives, shards(): sum_flat = lax.psum(grad_flat, 'dp').astype(jnp.bfloat16)  72.5 us
    all_to_all x3, waiting for transfers between devices, exchange(): return lax.all_to_all(parts, 'seq', split_axis=0, concat_axis=0, tiled=True)  30.2 us
    all_to_all x3, starting transfers between devices, exchange(): return lax.all_to_all(parts, 'seq', split_axis=0, concat_axis=0, tiled=True)  17.1 us
    all_to_all x1, starting transfers between devices, shards(): lax.all_to_all(grad_parts, 'dp', split_axis=0, concat_axis=0, tiled=True)  13.9 us
  transfers between devices with their start and end apart: 5, of which 4 were waited for; matrix products, arithmetic and copies ran while one was open for 4% of the time, Pallas kernels for 0%

profile of v1, /device:TPU:1, one launch (start us, length us, event | category | flops | bytes accessed | tf_op | source)
XLA Modules:
  0.0 385.4 jit_solution(3460044635847170445)
XLA Ops:
  2.4 2.3 convolution_convert_fusion
  4.7 1.5 reshape.298
  7.8 26.0 %all_to_all.45 = bf16[32,32,256]{2,1,0:T(8,128)(2,1)S(1)} all-to-all(bf16[32,32,256]{2,1,0:T(8,128)(2,1)S(1)} %fusion.6), channel_id=1, replica_groups=mesh['dp'=8,'seq'=32] {'seq'}, dimensions={0} | all-to-all | bytes 1048576 | tf_op jit(solution)/shard_map/all_to_all | solution.py:8
  35.3 1.4 fusion.3
  36.7 2.3 copy.46
  39.0 2.4 fusion.2
  41.4 2.3 copy.45
  43.7 1.7 pad_maximum_fusion
  45.3 54.4 %all_to_all.46 = bf16[32,64,512]{2,1,0:T(8,128)(2,1)S(1)} all-to-all(bf16[32,64,512]{2,1,0:T(8,128)(2,1)S(1)} %pad_maximum_fusion), channel_id=1, replica_groups=mesh['dp'=8,'seq'=32] {'seq'}, dimensions={0} | all-to-all | bytes 4194304 | tf_op jit(solution)/shard_map/all_to_all | solution.py:8
  100.2 33.1 %all_to_all.47 = bf16[32,32,512]{2,1,0:T(8,128)(2,1)S(1)} all-to-all(bf16[32,32,512]{2,1,0:T(8,128)(2,1)S(1)} %broadcast_in_dim.17), channel_id=1, replica_groups=mesh['dp'=8,'seq'=32] {'seq'}, dimensions={0} | all-to-all | bytes 2097152 | tf_op jit(solution)/shard_map/all_to_all | solution.py:8
  134.4 3.5 convolution_bitcast_fusion
  137.9 3.5 copy.47
  141.5 3.1 multiply_reduce_fusion.1
  146.5 8.4 %all-to-all-start.3 = ((f32[32,1,768]{2,1,0:T(1,128)}), f32[32,1,768]{2,1,0:T(1,128)S(1)}, u32[]{:S(2)}, u32[]{:S(2)}) async-start(f32[32,1,768]{2,1,0:T(1,128)} %reshape.319), calls=%async_computation.3 | async-start | bytes 196608 | tf_op jit(solution)/shard_map/all_to_all | solution.py:8
  158.0 5.9 %all-to-all-done.3 = f32[32,1,768]{2,1,0:T(1,128)S(1)} async-done(((f32[32,1,768]{2,1,0:T(1,128)}), f32[32,1,768]{2,1,0:T(1,128)S(1)}, u32[]{:S(2)}, u32[]{:S(2)}) %all-to-all-start.3) | async-done | bytes 98336 | tf_op jit(solution)/shard_map/all_to_all | solution.py:8
  164.5 1.5 reduce.7
  168.0 4.0 %all-to-all-start.4 = ((f32[32,1,768]{2,1,0:T(1,128)}), f32[32,1,768]{2,1,0:T(1,128)S(1)}, u32[]{:S(2)}, u32[]{:S(2)}) async-start(f32[32,1,768]{2,1,0:T(1,128)} %reshape.321), calls=%async_computation.4 | async-start | bytes 196608 | tf_op jit(solution)/shard_map/all_to_all | solution.py:8
  174.0 6.8 %all-to-all-done.4 = f32[32,1,768]{2,1,0:T(1,128)S(1)} async-done(((f32[32,1,768]{2,1,0:T(1,128)}), f32[32,1,768]{2,1,0:T(1,128)S(1)}, u32[]{:S(2)}, u32[]{:S(2)}) %all-to-all-start.4) | async-done | bytes 98336 | tf_op jit(solution)/shard_map/all_to_all | solution.py:8
  180.9 1.5 reduce.8
  184.2 1.7 fusion.9
  190.3 3.6 fusion.1
  193.9 2.3 copy.53
  196.2 4.7 %all-to-all-start.5 = ((bf16[32,32,512]{2,1,0:T(8,128)(2,1)}), bf16[32,32,512]{2,1,0:T(8,128)(2,1)}, u32[]{:S(2)}, u32[]{:S(2)}) async-start(bf16[32,32,512]{2,1,0:T(8,128)(2,1)} %bitcast.117), calls=%async_computation.5 | async-start | bytes 2097152 | tf_op jit(solution)/shard_map/all_to_all | solution.py:8
  200.9 3.6 multiply_convert_fusion
  204.5 17.5 %all-to-all-done.5 = bf16[32,32,512]{2,1,0:T(8,128)(2,1)} async-done(((bf16[32,32,512]{2,1,0:T(8,128)(2,1)}), bf16[32,32,512]{2,1,0:T(8,128)(2,1)}, u32[]{:S(2)}, u32[]{:S(2)}) %all-to-all-start.5) | async-done | bytes 1048608 | tf_op jit(solution)/shard_map/all_to_all | solution.py:8
  223.7 51.5 %all_to_all.48 = bf16[32,64,512]{2,1,0:T(8,128)(2,1)S(1)} all-to-all(bf16[32,64,512]{2,1,0:T(8,128)(2,1)S(1)} %broadcast_in_dim.22), channel_id=1, replica_groups=mesh['dp'=8,'seq'=32] {'seq'}, dimensions={0} | all-to-all | bytes 4194304 | tf_op jit(solution)/shard_map/all_to_all | solution.py:8
  278.1 13.9 %all-to-all-start.7 = ((bf16[8,40,1024]{2,1,0:T(8,128)(2,1)}), bf16[8,40,1024]{2,1,0:T(8,128)(2,1)}, u32[]{:S(2)}, u32[]{:S(2)}) async-start(bf16[8,40,1024]{2,1,0:T(8,128)(2,1)} %bitcast.123), calls=%async_computation.7 | async-start | bytes 1310720 | tf_op jit(solution)/shard_map/all_to_all | solution.py:98
  292.1 6.2 %fusion.28 = f32[1536,1024]{1,0:T(8,128)} fusion(bf16[1536,512]{1,0:T(8,128)(2,1)} %bitcast.129, bf16[1024,512]{1,0:T(8,128)(2,1)} %bitcast.131), kind=kOutput, calls=%fused_computation.88 | convolution fusion | flops 1610612736 | bytes 8912896 | tf_op jit(solution)/shard_map/dot_general | solution.py:78
  298.3 4.7 %all-to-all-done.7 = bf16[8,40,1024]{2,1,0:T(8,128)(2,1)} async-done(((bf16[8,40,1024]{2,1,0:T(8,128)(2,1)}), bf16[8,40,1024]{2,1,0:T(8,128)(2,1)}, u32[]{:S(2)}, u32[]{:S(2)}) %all-to-all-start.7) | async-done | bytes 655392 | tf_op jit(solution)/shard_map/all_to_all | solution.py:98
  305.1 4.9 %all-to-all-start.8 = ((bf16[8,40,1024]{2,1,0:T(8,128)(2,1)}), bf16[8,40,1024]{2,1,0:T(8,128)(2,1)}, u32[]{:S(2)}, u32[]{:S(2)}) async-start(bf16[8,40,1024]{2,1,0:T(8,128)(2,1)} %broadcast_in_dim.23), calls=%async_computation.8 | async-start | bytes 1310720 | tf_op jit(solution)/shard_map/all_to_all | solution.py:100
  310.1 72.5 %all-reduce.3 = bf16[1536,1024]{1,0:T(8,128)(2,1)} all-reduce(f32[1536,1024]{1,0:T(8,128)} %fusion.28), channel_id=1, replica_groups=mesh['dp'=8,'seq'=32] {'dp'}, use_global_device_ids=true, to_apply=%region_9.10 | all-reduce | flops 1572864 | bytes 9437184 | tf_op jit(solution)/shard_map/psum | solution.py:81
  383.4 1.9 fusion.26
  (83 shorter events, 29.7 us)
Async XLA Ops:
  0.6 132.7 %copy-start = (bf16[48,32,1024]{2,1,0:T(8,128)(2,1)S(1)}, bf16[48,32,1024]{2,1,0:T(8,128)(2,1)}, u32[]{:S(2)}) copy-start(bf16[48,32,1024]{2,1,0:T(8,128)(2,1)} %param.15) | copy-start | bytes 9437188
  6.1 29.2 %copy-start.9 = (bf16[160,1024]{1,0:T(8,128)(2,1)S(1)}, bf16[160,1024]{1,0:T(8,128)(2,1)}, u32[]{:S(2)}) copy-start(bf16[160,1024]{1,0:T(8,128)(2,1)} %param.14) | copy-start | bytes 983044
  33.8 0.8 copy-start.1
  34.6 0.7 copy-start.2
  34.6 9.0 %copy-start.4 = (bf16[32,16,160]{2,1,0:T(8,128)(2,1)}, bf16[32,16,160]{2,1,0:T(8,128)(2,1)S(1)}, u32[]{:S(2)}) copy-start(bf16[32,16,160]{2,1,0:T(8,128)(2,1)S(1)} %get-tuple-element.10) | copy-start | bytes 491524
  100.1 41.4 %copy-start.7 = (f32[32,512]{1,0:T(8,128)}, f32[32,512]{1,0:T(8,128)S(1)}, u32[]{:S(2)}) copy-start(f32[32,512]{1,0:T(8,128)S(1)} %get-tuple-element.14) | copy-start | bytes 196612
  133.4 1.0 copy-start.6
  146.5 17.5 %all-to-all-start.3 = ((f32[32,1,768]{2,1,0:T(1,128)}), f32[32,1,768]{2,1,0:T(1,128)S(1)}, u32[]{:S(2)}, u32[]{:S(2)}) async-start(f32[32,1,768]{2,1,0:T(1,128)} %reshape.319), calls=%async_computation.3 | async-start | bytes 196608 | tf_op jit(solution)/shard_map/all_to_all | solution.py:8
  156.1 8.4 %copy-start.10 = (f32[32,16]{1,0:T(8,128)}, f32[32,16]{1,0:T(8,128)S(1)}, u32[]{:S(2)}) copy-start(f32[32,16]{1,0:T(8,128)S(1)} %convert_reduce_fusion.2) | copy-start | bytes 6148
  157.9 6.5 %copy-start.14 = (bf16[32,16,1]{0,1,2:T(8,128)(2,1)}, bf16[32,16,1]{0,1,2:T(8,128)(2,1)S(1)}, u32[]{:S(2)}) copy-start(bf16[32,16,1]{0,1,2:T(8,128)(2,1)S(1)} %copy.54) | copy-start | bytes 3076
  168.0 12.9 %all-to-all-start.4 = ((f32[32,1,768]{2,1,0:T(1,128)}), f32[32,1,768]{2,1,0:T(1,128)S(1)}, u32[]{:S(2)}, u32[]{:S(2)}) async-start(f32[32,1,768]{2,1,0:T(1,128)} %reshape.321), calls=%async_computation.4 | async-start | bytes 196608 | tf_op jit(solution)/shard_map/all_to_all | solution.py:8
  193.9 7.0 %copy-start.8 = (f32[32,512]{1,0:T(8,128)S(1)}, f32[32,512]{1,0:T(8,128)}, u32[]{:S(2)}) copy-start(f32[32,512]{1,0:T(8,128)} %copy-done.7) | copy-start | bytes 196612
  196.2 25.8 %all-to-all-start.5 = ((bf16[32,32,512]{2,1,0:T(8,128)(2,1)}), bf16[32,32,512]{2,1,0:T(8,128)(2,1)}, u32[]{:S(2)}, u32[]{:S(2)}) async-start(bf16[32,32,512]{2,1,0:T(8,128)(2,1)} %bitcast.117), calls=%async_computation.5 | async-start | bytes 2097152 | tf_op jit(solution)/shard_map/all_to_all | solution.py:8
  275.2 1.0 copy-start.5
  275.2 1.5 copy-start.3
  275.4 16.6 %copy-start.11 = (f32[32,16]{1,0:T(8,128)S(1)}, f32[32,16]{1,0:T(8,128)}, u32[]{:S(2)}) copy-start(f32[32,16]{1,0:T(8,128)} %copy-done.10) | copy-start | bytes 6148
  278.1 24.9 %all-to-all-start.7 = ((bf16[8,40,1024]{2,1,0:T(8,128)(2,1)}), bf16[8,40,1024]{2,1,0:T(8,128)(2,1)}, u32[]{:S(2)}, u32[]{:S(2)}) async-start(bf16[8,40,1024]{2,1,0:T(8,128)(2,1)} %bitcast.123), calls=%async_computation.7 | async-start | bytes 1310720 | tf_op jit(solution)/shard_map/all_to_all | solution.py:98
  305.1 78.3 %all-to-all-start.8 = ((bf16[8,40,1024]{2,1,0:T(8,128)(2,1)}), bf16[8,40,1024]{2,1,0:T(8,128)(2,1)}, u32[]{:S(2)}, u32[]{:S(2)}) async-start(bf16[8,40,1024]{2,1,0:T(8,128)(2,1)} %broadcast_in_dim.23), calls=%async_computation.8 | async-start | bytes 1310720 | tf_op jit(solution)/shard_map/all_to_all | solution.py:100
  310.1 72.6 %copy-start.12 = (f32[32,16]{1,0:T(8,128)S(1)}, f32[32,16]{1,0:T(8,128)}, u32[]{:S(2)}) copy-start(f32[32,16]{1,0:T(8,128)} %abs_log_fusion) | copy-start | bytes 6148
  310.1 72.7 %copy-start.13 = (f32[32,16]{1,0:T(8,128)S(1)}, f32[32,16]{1,0:T(8,128)}, u32[]{:S(2)}) copy-start(f32[32,16]{1,0:T(8,128)} %get-tuple-element.4) | copy-start | bytes 6148

commit v2 on v0

v2 whole, which is shorter than its diff:
```python
import jax
import jax.numpy as jnp
from jax import lax
from jax.experimental import pallas as pl
from jax.experimental.pallas import tpu as pltpu
from jax.sharding import Mesh
from jax.sharding import PartitionSpec as P

CORES = 2
COLUMNS = 4
BF16 = jnp.bfloat16
F32 = jnp.float32


def exchange(parts, axes):
    return lax.all_to_all(parts, axes, split_axis=0, concat_axis=0, tiled=True)


def call(body, outs, args, scratch=(), smem=(), flops=0):
    moved = sum(a.size * a.dtype.itemsize for a in args)
    moved += sum(o.size * jnp.dtype(o.dtype).itemsize for o in outs)
    specs = [
        pl.BlockSpec(memory_space=pltpu.SMEM if i in smem else pltpu.VMEM)
        for i in range(len(args))
    ]
    got = pl.pallas_call(
        body,
        out_shape=tuple(outs),
        in_specs=specs,
        out_specs=tuple(pl.BlockSpec(memory_space=pltpu.VMEM) for _ in outs),
        scratch_shapes=list(scratch),
        compiler_params=pltpu.CompilerParams(vmem_limit_bytes=48 * 1024 * 1024),
        cost_estimate=pl.CostEstimate(flops=flops, bytes_accessed=moved, transcendentals=0),
    )(*args)
    return got


def dot(a, b, da, db):
    return lax.dot_general(a, b, (((da,), (db,)), ((), ())), preferred_element_type=F32)


def pick_body(nx, nz, seq_ref, start_ref, end_ref, states_ref, out_ref):
    tokens, width = states_ref.shape
    half = tokens // 2
    depth = width // (nx * nz)
    own = start_ref.shape[1]
    states = states_ref[...]
    for side, ref in enumerate((start_ref, end_ref)):
        token = ref[...]
        inside = lax.rem(token, half)
        low = (token - inside) == seq_ref[0] * half
        picks = inside + jnp.where(low, 0, half)
        spot = lax.broadcasted_iota(jnp.int32, (tokens, own), 0)
        mask = jnp.where(spot == picks, 1.0, 0.0).astype(BF16)
        rows = dot(mask, states, 0, 0)
        for z in range(nz):
            cut = [rows[:, (x * nz + z) * depth : (x * nz + z + 1) * depth] for x in range(nx)]
            out_ref[side * nz + z] = jnp.concatenate(cut, axis=1).astype(BF16)


def project_body(nx, nz, inner, weight_ref, piece_ref, out_ref):
    full = weight_ref.shape[2]
    weight = weight_ref[...].reshape(-1, full)
    piece = piece_ref[...].reshape(-1, piece_ref.shape[2])
    pre = dot(weight, piece, 0, 1).astype(BF16)
    group = pre.shape[1] // CORES
    for c in range(CORES):
        for z in range(nz):
            for x in range(nx):
                at = (x * nz + z) * inner
                out_ref[c * nz + z, x * inner : (x + 1) * inner, :] = pre[
                    at : at + inner, c * group : (c + 1) * group
                ]


def act_body(nx, nz, inner, got_ref, tags_ref, pre_ref, left_ref, right_ref):
    def total(side):
        sums = got_ref[side * nz].astype(F32)
        for z in range(1, nz):
            sums = sums + got_ref[side * nz + z].astype(F32)
        return sums

    pre_left, pre_right = total(0), total(1)
    pre_ref[0] = pre_left
    pre_ref[1] = pre_right
    left = jax.nn.gelu(pre_left).astype(BF16)
    right = jax.nn.gelu(pre_right)
    tags = tags_ref[...]
    for x in range(nx):
        left_ref[x] = left
        block = jnp.concatenate([right[x * inner : (x + 1) * inner], tags], axis=0).astype(BF16)
        for z in range(nz):
            right_ref[x * nz + z] = block


def score_body(nx, nz, inner, weight_ref, left_got, right_got, out_ref, left_ref, right_ref):
    labels = weight_ref.shape[1]
    width = weight_ref.shape[3]
    group = left_got.shape[2]
    for x in range(nx):
        left_ref[:, x * group : (x + 1) * group] = left_got[x].astype(F32)
        for z in range(nz):
            block = right_got[x * nz + z]
            right_ref[z * inner : (z + 1) * inner, x * group : (x + 1) * group] = block[:inner]
    for i in range(nx * nz):
        if i % nz >= labels // 8:
            out_ref[i] = jnp.zeros((8, group), F32)

    def step(lb, carry):
        total = jnp.zeros((8, nx * group), F32)
        for x in range(nx):
            weight = weight_ref[x, pl.ds(lb * 8, 8)].reshape(8 * inner, width)
            image = dot(weight, right_ref[...], 1, 0).reshape(8, inner, nx * group)
            left = left_ref[x * inner : (x + 1) * inner, :]
            total = total + jnp.sum(image * left[None], axis=1)
        for x in range(nx):
            out_ref[x * nz + lb] = total[:, x * group : (x + 1) * group]
        return carry

    lax.fori_loop(0, labels // 8, step, 0)


def slope_body(
    nx, nz, inner, own, weight_ref, left_ref, right_ref, right_got, score_ref,
    left_out, right_out, slope_ref, loss_ref, left_sum, right_sum,
):
    labels = weight_ref.shape[1]
    width = weight_ref.shape[3]
    group = score_ref.shape[2]
    for x in range(nx):
        lanes = slice(x * group, (x + 1) * group)
        tags = right_got[x * nz].astype(F32)[inner:]
        for z in range(1, nz):
            tags = tags + right_got[x * nz + z].astype(F32)[inner:]
        gold, live = tags[0:1], tags[1:2]
        scores = jnp.concatenate([score_ref[x * nz + b] for b in range(labels // 8)], axis=0)
        most = jnp.max(scores, axis=0, keepdims=True)
        log_total = most + jnp.log(jnp.sum(jnp.exp(scores - most), axis=0, keepdims=True))
        spot = lax.broadcasted_iota(jnp.int32, scores.shape, 0).astype(F32)
        onehot = jnp.where(spot == gold, 1.0, 0.0)
        picked = jnp.sum(scores * onehot, axis=0, keepdims=True)
        loss_ref[:, lanes] = live * (log_total - picked)
        slope = live * (jnp.exp(scores - log_total) - onehot) / own
        slope_ref[:, lanes] = slope.astype(BF16).astype(F32)
    left_sum[...] = jnp.zeros_like(left_sum)
    right_sum[...] = jnp.zeros_like(right_sum)

    def step(lb, carry):
        slope = slope_ref[pl.ds(lb * 8, 8), :]
        for x in range(nx):
            rows = slice(x * inner, (x + 1) * inner)
            weight = weight_ref[x, pl.ds(lb * 8, 8)].reshape(8 * inner, width)
            image = dot(weight, right_ref[...], 1, 0).reshape(8, inner, nx * group)
            left_sum[rows, :] += jnp.sum(image * slope[:, None, :], axis=0)
            left = left_ref[rows, :]
            outer = (slope[:, None, :] * left[None]).astype(BF16).reshape(8 * inner, nx * group)
            right_sum[...] += dot(weight, outer, 0, 0)
        return carry

    lax.fori_loop(0, labels // 8, step, 0)
    for x in range(nx):
        lanes = slice(x * group, (x + 1) * group)
        left_out[x] = left_sum[:, lanes].astype(BF16)
        for z in range(nz):
            right_out[x * nz + z] = right_sum[z * inner : (z + 1) * inner, lanes].astype(BF16)


def flat_body(nx, inner, left_ref, right_ref, slope_ref, out_ref):
    parts, _, take = out_ref.shape[:3]
    spans = left_ref.shape[1]
    for g in range(parts):
        slope = slope_ref[g * take : (g + 1) * take, :]
        for x in range(nx):
            left = left_ref[x * inner : (x + 1) * inner, :]
            outer = (slope[:, None, :] * left[None]).astype(BF16).reshape(take * inner, spans)
            out_ref[g, x] = dot(outer, right_ref[...], 1, 1).astype(BF16).reshape(out_ref.shape[2:])


def lower_body(nx, nz, inner, pre_ref, left_got, right_got, out_ref):
    grad_left = left_got[0].astype(F32)
    for x in range(1, nx):
        grad_left = grad_left + left_got[x].astype(F32)
    blocks = []
    for x in range(nx):
        block = right_got[x * nz].astype(F32)
        for z in range(1, nz):
            block = block + right_got[x * nz + z].astype(F32)
        blocks.append(block)
    grad_right = jnp.concatenate(blocks, axis=0)
    for side, grad in enumerate((grad_left, grad_right)):
        _, back = jax.vjp(jax.nn.gelu, pre_ref[side])
        lowered = back(grad)[0].astype(BF16)
        for z in range(nz):
            out_ref[side * nz + z] = lowered


def weight_body(nx, nz, inner, low_ref, piece_ref, out_ref, wide_ref):
    group = low_ref.shape[2]
    for c in range(CORES):
        for z in range(nz):
            for x in range(nx):
                at = (x * nz + z) * inner
                wide_ref[at : at + inner, c * group : (c + 1) * group] = low_ref[
                    c * nz + z, x * inner : (x + 1) * inner, :
                ]
    piece = piece_ref[...].reshape(-1, piece_ref.shape[2])
    grad = dot(piece, wide_ref[...], 0, 1)
    take = out_ref.shape[1]
    ny = out_ref.shape[0] // nx
    for y in range(ny):
        for x in range(nx):
            at = (x * ny + y) * take
            out_ref[y * nx + x] = grad[at : at + take].astype(BF16)


def build(ny, nx, nz):
    def shards(states, span_start, span_end, gold, live, start_proj, end_proj, biaffine):
        x_index, z_index = lax.axis_index("x"), lax.axis_index("z")
        seq_index = x_index * nz + z_index
        core = lax.axis_index("core")
        own = span_start.shape[1]
        labels, inner, full = biaffine.shape
        depth = start_proj.shape[0]
        group = own * nz
        spans = group * nx
        width = full // nx
        rows = nx * inner
        take = labels // (CORES * ny)
        shape = jax.ShapeDtypeStruct

        blocks = exchange(
            biaffine.reshape(labels, inner, nx, width).transpose(2, 0, 1, 3), "x"
        )
        side_proj = jnp.where(core == 0, start_proj, end_proj)
        weights = exchange(jnp.broadcast_to(side_proj[None], (nx,) + side_proj.shape), "x")

        (picked,) = call(
            lambda *refs: pick_body(nx, nz, *refs),
            [shape((CORES * nz, own, nx * depth), BF16)],
            (seq_index.reshape(1), span_start, span_end, states[0]),
            smem=(0,),
        )
        pieces = exchange(picked, ("core", "z"))

        (pre_parts,) = call(
            lambda *refs: project_body(nx, nz, inner, *refs),
            [shape((CORES * nz, rows, group), BF16)],
            (weights, pieces),
            flops=2 * full * nx * depth * group * CORES,
        )
        pre_got = exchange(pre_parts, ("core", "z"))

        tags = jnp.concatenate([gold, live], axis=0).astype(F32)
        tags = lax.dynamic_update_slice(jnp.zeros((8, group), F32), tags, (0, z_index * own))
        pre, left_pay, right_pay = call(
            lambda *refs: act_body(nx, nz, inner, *refs),
            [
                shape((2, rows, group), F32),
                shape((nx, rows, group), BF16),
                shape((nx * nz, inner + 8, group), BF16),
            ],
            (pre_got, tags),
        )
        right_got = exchange(right_pay, ("x", "z"))
        left_got = exchange(left_pay, "x")

        score_parts, left, right = call(
            lambda *refs: score_body(nx, nz, inner, *refs),
            [
                shape((nx * nz, 8, group), F32),
                shape((rows, spans), F32),
                shape((width, spans), BF16),
            ],
            (blocks, left_got, right_got),
            flops=2 * labels * rows * width * spans,
        )
        score_got = exchange(score_parts, ("x", "z"))
        score_sum = jnp.sum(score_got, axis=0)
        scores = exchange(jnp.broadcast_to(score_sum[None], score_got.shape), ("x", "z"))

        left_grad, right_grad, slope, loss = call(
            lambda *refs: slope_body(nx, nz, inner, own, *refs),
            [
                shape((nx, rows, group), BF16),
                shape((nx * nz, inner, group), BF16),
                shape((labels, spans), F32),
                shape((1, spans), F32),
            ],
            (blocks, left, right, right_got, scores),
            scratch=(pltpu.VMEM((rows, spans), F32), pltpu.VMEM((width, spans), F32)),
            flops=4 * labels * rows * width * spans,
        )
        span_loss = lax.dynamic_slice_in_dim(loss, seq_index * own, own, 1)
        right_grad_got = exchange(right_grad, ("x", "z"))
        left_grad_got = exchange(left_grad, "x")

        (flat,) = call(
            lambda *refs: flat_body(nx, inner, *refs),
            [shape((CORES * ny, nx, take, inner, width), BF16)],
            (left, right, slope),
            flops=2 * labels * rows * width * spans,
        )
        flat = exchange(flat.reshape((CORES, ny * nx) + flat.shape[2:]), "core")
        flat = jnp.sum(flat.astype(F32), axis=0).astype(BF16)
        flat = exchange(flat, "y").reshape((ny, nx) + flat.shape[1:])
        flat = jnp.sum(flat.astype(F32), axis=0).astype(BF16)
        flat = exchange(
            jnp.broadcast_to(flat[None], (ny,) + flat.shape).reshape((ny * nx,) + flat.shape[1:]),
            ("y", "x"),
        )
        flat = exchange(jnp.broadcast_to(flat[None], (CORES,) + flat.shape), "core")
        flat = flat.reshape(CORES * ny, nx, take, inner, width).transpose(0, 2, 3, 1, 4)
        grad_biaffine = flat.reshape(labels, inner, full)

        (lowered,) = call(
            lambda *refs: lower_body(nx, nz, inner, *refs),
            [shape((CORES * nz, rows, group), BF16)],
            (pre, left_grad_got, right_grad_got),
        )
        lowered_got = exchange(lowered, ("core", "z"))
        (grad_parts,) = call(
            lambda *refs: weight_body(nx, nz, inner, *refs),
            [shape((ny * nx, depth // ny, full), BF16)],
            (lowered_got, pieces),
            scratch=(pltpu.VMEM((full, CORES * group), BF16),),
            flops=2 * full * nx * depth * group * CORES,
        )
        grad_got = exchange(grad_parts, ("y", "x"))
        grad_own = jnp.sum(grad_got.astype(F32), axis=0).astype(BF16)
        grads = exchange(
            jnp.broadcast_to(grad_own[None], (ny * CORES,) + grad_own.shape), ("y", "core")
        ).reshape(ny, CORES, depth // ny, full)
        return (
            span_loss,
            grads[:, 0].reshape(depth, full),
            grads[:, 1].reshape(depth, full),
            grad_biaffine,
        )

    return shards


def solution(mesh):
    ny, nz = mesh.shape["dp"] // CORES, mesh.shape["seq"] // COLUMNS
    fine = Mesh(mesh.devices.reshape(ny, CORES, COLUMNS, nz), ("y", "core", "x", "z"))
    dp, seq = ("y", "core"), ("x", "z")
    placed = (
        P(dp, seq, None),
        P(dp, seq),
        P(dp, seq),
        P(dp, seq),
        P(dp, seq),
        P(seq, None),
        P(seq, None),
        P(None, seq, None),
    )
    return jax.shard_map(
        build(ny, COLUMNS, nz),
        mesh=fine,
        in_specs=placed,
        out_specs=(P(dp, seq), P(seq, None), P(seq, None), P(None, seq, None)),
        check_vma=False,
    )
```

time: 1030 us -> 346 us (0.34)
  waiting for transfers between devices: 775 us -> 85.1 us
  starting transfers between devices: 0.39 us -> 54.4 us
  matrix products: 21.2 us -> 0 us
  Pallas kernels: 0 us -> 16.3 us
  between operations: 14 us -> 0.83 us
  local copies, waits for them, and re-layouts: 44.9 us -> 33.6 us
    reduce_scatter x2 -> x0, waiting for transfers between devices: 414 us -> none  [owner_sum(): return lax.psum_scatter(term_rows, 'seq', scatter_dimension=0, tiled=True)]
    unnamed x6 -> x0, waiting for transfers between devices: 210 us -> none
    all_gather x2 -> x0, waiting for transfers between devices: 151 us -> none  [span_gather(): return lax.all_gather(values, 'seq', axis=0, tiled=True)]
    all_to_all x2 -> x8, blocking collectives: 37.4 us -> 147 us  [exchange(): return lax.all_to_all(parts, axes, split_axis=0, concat_axis=0, tiled=True)]
    psum x1 -> x0, blocking collectives: 87.3 us -> none  [shards(): summed = lax.psum((grad_start, grad_end, grad_flat), 'dp')]
    all_to_all x0 -> x9, waiting for transfers between devices: none -> 85.1 us  [exchange(): return lax.all_to_all(parts, axes, split_axis=0, concat_axis=0, tiled=True)]
    all_to_all x0 -> x9, starting transfers between devices: none -> 54.4 us  [exchange(): return lax.all_to_all(parts, axes, split_axis=0, concat_axis=0, tiled=True)]
    all_gather x1 -> x0, blocking collectives: 31.9 us -> none  [span_gather(): return lax.all_gather(values, 'seq', axis=0, tiled=True)]
  transfers between devices with their start and end apart: 5 -> 9, of which waited for: 5 -> 8; matrix products, arithmetic and copies ran while one was open for 2% -> 6% of each run, Pallas kernels for 0% -> 0%
where the time goes in v2:
time: 346 us; the launch traced here: 344 us
  blocking collectives  147 us (42%)
  waiting for transfers between devices  85.1 us (25%)
  starting transfers between devices  54.4 us (16%)
  local copies, waits for them, and re-layouts  33.6 us (10%)
  Pallas kernels  16.3 us (5%)
  other arithmetic  7.12 us (2%)
    all_to_all x8, blocking collectives, exchange(): return lax.all_to_all(parts, axes, split_axis=0, concat_axis=0, tiled=True)  147 us
    all_to_all x9, waiting for transfers between devices, exchange(): return lax.all_to_all(parts, axes, split_axis=0, concat_axis=0, tiled=True)  85.1 us
    all_to_all x9, starting transfers between devices, exchange(): return lax.all_to_all(parts, axes, split_axis=0, concat_axis=0, tiled=True)  54.4 us
    pallas_call x8, Pallas kernels, call(): pl.pallas_call(body, out_shape=tuple(outs), in_specs=specs, out_specs=tup...  16.3 us
    unnamed x42, local copies, waits for them, and re-layouts  10.1 us
  transfers between devices with their start and end apart: 9, of which 8 were waited for; matrix products, arithmetic and copies ran while one was open for 6% of the time, Pallas kernels for 0%

profile of v2, /device:TPU:1, one launch (start us, length us, event | category | flops | bytes accessed | tf_op | source)
XLA Modules:
  0.0 344.3 jit_solution(15641543166624303157)
XLA Ops:
  5.3 10.0 %all-to-all-start.2 = ((bf16[16,16,640]{2,1,0:T(8,128)(2,1)}), bf16[16,16,640]{2,1,0:T(8,128)(2,1)S(1)}, u32[]{:S(2)}, u32[]{:S(2)}) async-start(bf16[16,16,640]{2,1,0:T(8,128)(2,1)} %shard_map.111), calls=%async_computation.2 | async-start | bytes 655360 | tf_op jit(solution)/shard_map/all_to_all | solution.py:16
  15.4 10.6 %all-to-all-done.2.refs_1_ = bf16[16,16,640]{2,1,0:T(8,128)(2,1)S(1)} async-done(((bf16[16,16,640]{2,1,0:T(8,128)(2,1)}), bf16[16,16,640]{2,1,0:T(8,128)(2,1)S(1)}, u32[]{:S(2)}, u32[]{:S(2)}) %all-to-all-start.2) | async-done | bytes 327712 | tf_op jit(solution)/shard_map/all_to_all | solution.py:16
  26.2 20.2 %all_to_all.85.refs_0_ = bf16[4,160,1024]{2,1,0:T(8,128)(2,1)S(1)} all-to-all(bf16[4,160,1024]{2,1,0:T(8,128)(2,1)S(1)} %broadcast_in_dim.12), channel_id=1, replica_groups=mesh['y'=4,'core'=2,'x'=4,'z'=8] {'x'}, dimensions={0} | all-to-all | bytes 2621440 | tf_op jit(solution)/shard_map/all_to_all | solution.py:16
  47.9 7.4 %all-to-all-start.3 = ((bf16[16,128,128]{2,1,0:T(8,128)(2,1)}), bf16[16,128,128]{2,1,0:T(8,128)(2,1)S(1)}, u32[]{:S(2)}, u32[]{:S(2)}) async-start(bf16[16,128,128]{2,1,0:T(8,128)(2,1)} %shard_map.112), calls=%async_computation.3 | async-start | bytes 1048576 | tf_op jit(solution)/shard_map/all_to_all | solution.py:16
  55.6 14.4 %all-to-all-done.3.refs_0_ = bf16[16,128,128]{2,1,0:T(8,128)(2,1)S(1)} async-done(((bf16[16,128,128]{2,1,0:T(8,128)(2,1)}), bf16[16,128,128]{2,1,0:T(8,128)(2,1)S(1)}, u32[]{:S(2)}, u32[]{:S(2)}) %all-to-all-start.3) | async-done | bytes 524320 | tf_op jit(solution)/shard_map/all_to_all | solution.py:16
  72.1 3.3 all-to-all-start.4
  75.4 4.0 %copy.19 = bf16[48,4,4,8,256]{4,3,1,0,2:T(8,128)(2,1)} copy(bf16[48,4,4,8,256]{4,3,2,1,0:T(8,128)(2,1)} %bitcast.23) | data formatting | bytes 6291456 | tf_op jit(solution)/shard_map/reshape | solution.py:232
  80.9 39.0 %all_to_all.86.refs_0_ = bf16[4,48,32,256]{3,2,1,0:T(8,128)(2,1)S(1)} all-to-all(bf16[4,48,32,256]{3,2,1,0:T(8,128)(2,1)} %bitcast.21), channel_id=1, replica_groups=mesh['y'=4,'core'=2,'x'=4,'z'=8] {'x'}, dimensions={0} | all-to-all | bytes 6291456 | tf_op jit(solution)/shard_map/all_to_all | solution.py:16
  119.9 17.6 %all_to_all.87.refs_2_.refs_3_ = bf16[32,40,128]{2,1,0:T(8,128)(2,1)S(1)} all-to-all(bf16[32,40,128]{2,1,0:T(8,128)(2,1)S(1)} %copy-done.4), channel_id=1, replica_groups=mesh['y'=4,'core'=2,'x'=4,'z'=8] {'x','z'}, dimensions={0} | all-to-all | bytes 655360 | tf_op jit(solution)/shard_map/all_to_all | solution.py:16
  137.4 2.8 shard_map.114
  142.3 15.8 %all_to_all.88 = f32[32,8,128]{2,1,0:T(8,128)} all-to-all(f32[32,8,128]{2,1,0:T(8,128)S(1)} %get-tuple-element.18), channel_id=1, replica_groups=mesh['y'=4,'core'=2,'x'=4,'z'=8] {'x','z'}, dimensions={0} | all-to-all | bytes 262144 | tf_op jit(solution)/shard_map/all_to_all | solution.py:16
  159.1 12.6 %all_to_all.89.refs_4_ = f32[32,8,128]{2,1,0:T(8,128)S(1)} all-to-all(f32[32,8,128]{2,1,0:T(8,128)S(1)} %broadcast_in_dim.14), channel_id=1, replica_groups=mesh['y'=4,'core'=2,'x'=4,'z'=8] {'x','z'}, dimensions={0} | all-to-all | bytes 262144 | tf_op jit(solution)/shard_map/all_to_all | solution.py:16
  174.6 5.3 %shard_map.115 = (bf16[4,128,128]{2,1,0:T(8,128)(2,1)S(1)}, bf16[32,32,128]{2,1,0:T(8,128)(2,1)}, f32[48,512]{1,0:T(8,128)S(1)}, f32[1,512]{1,0:T(1,128)S(1)}) custom-call(bf16[4,48,32,256]{3,2,1,0:T(8,128)(2,1)S(1)} %all_to_all.86.refs_0_, f32[128,512]{1,0:T(8,128)S(1)} %copy-done.12, bf16[256,512]{1,0:T(8,128)(2,1)S(1)} %copy-done.15, ...), custom_call_target="tpu_custom_call" | custom-call | flops 3221225472 | bytes 4622336 | tf_op jit(solution)/shard_map/pallas_call | solution.py:26
  180.0 2.9 shard_map.118
  182.8 11.7 %all_to_all.90 = bf16[2,16,6,32,256]{4,3,2,1,0:T(8,128)(2,1)} all-to-all(bf16[2,16,6,32,256]{4,3,2,1,0:T(8,128)(2,1)S(1)} %bitcast.18), channel_id=1, replica_groups=mesh['y'=4,'core'=2,'x'=4,'z'=8] {'core'}, dimensions={0} | all-to-all | bytes 6291456 | tf_op jit(solution)/shard_map/all_to_all | solution.py:16
  194.5 7.2 %all_to_all.91.refs_1_ = bf16[4,128,128]{2,1,0:T(8,128)(2,1)S(1)} all-to-all(bf16[4,128,128]{2,1,0:T(8,128)(2,1)S(1)} %get-tuple-element.21), channel_id=1, replica_groups=mesh['y'=4,'core'=2,'x'=4,'z'=8] {'x'}, dimensions={0} | all-to-all | bytes 262144 | tf_op jit(solution)/shard_map/all_to_all | solution.py:16
  201.7 3.9 %all-to-all-start.9 = ((bf16[32,32,128]{2,1,0:T(8,128)(2,1)}), bf16[32,32,128]{2,1,0:T(8,128)(2,1)S(1)}, u32[]{:S(2)}, u32[]{:S(2)}) async-start(bf16[32,32,128]{2,1,0:T(8,128)(2,1)} %get-tuple-element.22), calls=%async_computation.9 | async-start | bytes 524288 | tf_op jit(solution)/shard_map/all_to_all | solution.py:16
  205.6 4.2 %reduce_sum.47 = bf16[16,6,32,256]{3,2,1,0:T(8,128)(2,1)} reduce(bf16[2,16,6,32,256]{4,3,2,1,0:T(8,128)(2,1)} %all_to_all.90, bf16[]{:T(256)} %constant.30.clone.1), dimensions={0}, to_apply=%region_2.3 | reduce | flops 786432 | bytes 4718594 | tf_op jit(solution)/shard_map/reduce_sum | solution.py:304
  209.8 5.4 %all-to-all-done.9.refs_2_ = bf16[32,32,128]{2,1,0:T(8,128)(2,1)S(1)} async-done(((bf16[32,32,128]{2,1,0:T(8,128)(2,1)}), bf16[32,32,128]{2,1,0:T(8,128)(2,1)S(1)}, u32[]{:S(2)}, u32[]{:S(2)}) %all-to-all-start.9) | async-done | bytes 262176 | tf_op jit(solution)/shard_map/all_to_all | solution.py:16
  215.2 4.2 %all-to-all-start.14 = ((bf16[16,6,32,256]{3,2,1,0:T(8,128)(2,1)}), bf16[16,6,32,256]{3,2,1,0:T(8,128)(2,1)S(1)}, u32[]{:S(2)}, u32[]{:S(2)}) async-start(bf16[16,6,32,256]{3,2,1,0:T(8,128)(2,1)} %reduce_sum.47), calls=%async_computation.14 | async-start | bytes 3145728 | tf_op jit(solution)/shard_map/all_to_all | solution.py:16
  220.4 15.5 %all-to-all-done.14 = bf16[16,6,32,256]{3,2,1,0:T(8,128)(2,1)S(1)} async-done(((bf16[16,6,32,256]{3,2,1,0:T(8,128)(2,1)}), bf16[16,6,32,256]{3,2,1,0:T(8,128)(2,1)S(1)}, u32[]{:S(2)}, u32[]{:S(2)}) %all-to-all-start.14) | async-done | bytes 1572896 | tf_op jit(solution)/shard_map/all_to_all | solution.py:16
  235.9 10.3 %all-to-all-start.10 = ((bf16[16,128,128]{2,1,0:T(8,128)(2,1)}), bf16[16,128,128]{2,1,0:T(8,128)(2,1)S(1)}, u32[]{:S(2)}, u32[]{:S(2)}) async-start(bf16[16,128,128]{2,1,0:T(8,128)(2,1)} %shard_map.116), calls=%async_computation.10 | async-start | bytes 1048576 | tf_op jit(solution)/shard_map/all_to_all | solution.py:16
  246.5 14.4 %all-to-all-done.10.refs_0_ = bf16[16,128,128]{2,1,0:T(8,128)(2,1)S(1)} async-done(((bf16[16,128,128]{2,1,0:T(8,128)(2,1)}), bf16[16,128,128]{2,1,0:T(8,128)(2,1)S(1)}, u32[]{:S(2)}, u32[]{:S(2)}) %all-to-all-start.10) | async-done | bytes 524320 | tf_op jit(solution)/shard_map/all_to_all | solution.py:16
  262.3 4.4 %all-to-all-start.15 = ((bf16[16,6,32,256]{3,2,1,0:T(8,128)(2,1)}), bf16[16,6,32,256]{3,2,1,0:T(8,128)(2,1)}, u32[]{:S(2)}, u32[]{:S(2)}) async-start(bf16[16,6,32,256]{3,2,1,0:T(8,128)(2,1)} %bitcast.8), calls=%async_computation.15 | async-start | bytes 3145728 | tf_op jit(solution)/shard_map/all_to_all | solution.py:16
  267.3 22.2 %all-to-all-done.15 = bf16[16,6,32,256]{3,2,1,0:T(8,128)(2,1)} async-done(((bf16[16,6,32,256]{3,2,1,0:T(8,128)(2,1)}), bf16[16,6,32,256]{3,2,1,0:T(8,128)(2,1)}, u32[]{:S(2)}, u32[]{:S(2)}) %all-to-all-start.15) | async-done | bytes 1572896 | tf_op jit(solution)/shard_map/all_to_all | solution.py:16
  289.5 22.9 %all_to_all.92 = bf16[16,40,1024]{2,1,0:T(8,128)(2,1)} all-to-all(bf16[16,40,1024]{2,1,0:T(8,128)(2,1)S(1)} %shard_map.117), channel_id=1, replica_groups=mesh['y'=4,'core'=2,'x'=4,'z'=8] {'y','x'}, dimensions={0} | all-to-all | bytes 2621440 | tf_op jit(solution)/shard_map/all_to_all | solution.py:16
  312.4 3.5 %broadcast_in_dim.17 = bf16[2,16,6,32,256]{4,3,2,1,0:T(8,128)(2,1)} broadcast(bf16[16,6,32,256]{3,2,1,0:T(8,128)(2,1)} %all-to-all-done.15), dimensions={1,2,3,4} | broadcast | bytes 4718592 | tf_op jit(solution)/shard_map/broadcast_in_dim | solution.py:311
  316.0 6.5 %all-to-all-start.16 = ((bf16[2,16,6,32,256]{4,3,2,1,0:T(8,128)(2,1)}), bf16[2,16,6,32,256]{4,3,2,1,0:T(8,128)(2,1)S(1)}, u32[]{:S(2)}, u32[]{:S(2)}) async-start(bf16[2,16,6,32,256]{4,3,2,1,0:T(8,128)(2,1)} %broadcast_in_dim.17), calls=%async_computation.16 | async-start | bytes 6291456 | tf_op jit(solution)/shard_map/all_to_all | solution.py:16
  326.6 4.5 %all-to-all-start.12 = ((bf16[8,40,1024]{2,1,0:T(8,128)(2,1)}), bf16[8,40,1024]{2,1,0:T(8,128)(2,1)}, u32[]{:S(2)}, u32[]{:S(2)}) async-start(bf16[8,40,1024]{2,1,0:T(8,128)(2,1)} %broadcast_in_dim.15), calls=%async_computation.12 | async-start | bytes 1310720 | tf_op jit(solution)/shard_map/all_to_all | solution.py:16
  331.6 4.7 %copy.16 = bf16[8,6,32,4,256]{4,3,2,1,0:T(4,128)(2,1)} copy(bf16[8,6,32,4,256]{4,2,1,3,0:T(8,128)(2,1)S(1)} %bitcast.20) | data formatting | bytes 6291456 | tf_op jit(solution)/shard_map/transpose | solution.py:312
  336.3 6.1 %reshape.44 = bf16[48,32,1024]{2,1,0:T(8,128)(2,1)} reshape(bf16[8,6,32,4,256]{4,3,2,1,0:T(4,128)(2,1)} %copy.16) | data formatting | bytes 6291456 | tf_op jit(solution)/shard_map/reshape | solution.py:313
  342.4 1.9 fusion
  (62 shorter events, 24.1 us)
Async XLA Ops:
  0.6 1.7 copy-start
  2.4 0.7 copy-start.9
  3.0 0.7 copy-start.10
  3.7 11.6 %copy-start.17 = (bf16[160,1024]{1,0:T(8,128)(2,1)S(1)}, bf16[160,1024]{1,0:T(8,128)(2,1)}, u32[]{:S(2)}) copy-start(bf16[160,1024]{1,0:T(8,128)(2,1)} %param.13) | copy-start | bytes 983044
  3.7 11.6 %copy-start.18 = (bf16[160,1024]{1,0:T(8,128)(2,1)S(1)}, bf16[160,1024]{1,0:T(8,128)(2,1)}, u32[]{:S(2)}) copy-start(bf16[160,1024]{1,0:T(8,128)(2,1)} %param.14) | copy-start | bytes 983044
  5.3 20.7 %all-to-all-start.2 = ((bf16[16,16,640]{2,1,0:T(8,128)(2,1)}), bf16[16,16,640]{2,1,0:T(8,128)(2,1)S(1)}, u32[]{:S(2)}, u32[]{:S(2)}) async-start(bf16[16,16,640]{2,1,0:T(8,128)(2,1)} %shard_map.111), calls=%async_computation.2 | async-start | bytes 655360 | tf_op jit(solution)/shard_map/all_to_all | solution.py:16
  26.2 29.1 %copy-start.19 = (s32[1,16]{1,0:T(1,128)S(1)}, s32[1,16]{1,0:T(1,128)}, u32[]{:S(2)}) copy-start(s32[1,16]{1,0:T(1,128)} %param.12) | copy-start | bytes 196
  26.2 29.1 %copy-start.20 = (s32[1,16]{1,0:T(1,128)S(1)}, s32[1,16]{1,0:T(1,128)}, u32[]{:S(2)}) copy-start(s32[1,16]{1,0:T(1,128)} %param.11) | copy-start | bytes 196
  47.9 22.1 %all-to-all-start.3 = ((bf16[16,128,128]{2,1,0:T(8,128)(2,1)}), bf16[16,128,128]{2,1,0:T(8,128)(2,1)S(1)}, u32[]{:S(2)}, u32[]{:S(2)}) async-start(bf16[16,128,128]{2,1,0:T(8,128)(2,1)} %shard_map.112), calls=%async_computation.3 | async-start | bytes 1048576 | tf_op jit(solution)/shard_map/all_to_all | solution.py:16
  70.7 0.7 copy-start.3
  71.5 0.6 copy-start.7
  72.1 8.1 %all-to-all-start.4 = ((bf16[4,128,128]{2,1,0:T(8,128)(2,1)}), bf16[4,128,128]{2,1,0:T(8,128)(2,1)S(1)}, u32[]{:S(2)}, u32[]{:S(2)}) async-start(bf16[4,128,128]{2,1,0:T(8,128)(2,1)} %get-tuple-element.14), calls=%async_computation.4 | async-start | bytes 262144 | tf_op jit(solution)/shard_map/all_to_all | solution.py:16
  80.2 0.7 copy-start.5
  80.9 39.0 %copy-start.4 = (bf16[32,40,128]{2,1,0:T(8,128)(2,1)S(1)}, bf16[32,40,128]{2,1,0:T(8,128)(2,1)}, u32[]{:S(2)}) copy-start(bf16[32,40,128]{2,1,0:T(8,128)(2,1)} %copy-done.3) | copy-start | bytes 983044
  80.9 56.5 %copy-start.6 = (bf16[4,128,128]{2,1,0:T(8,128)(2,1)S(1)}, bf16[4,128,128]{2,1,0:T(8,128)(2,1)}, u32[]{:S(2)}) copy-start(bf16[4,128,128]{2,1,0:T(8,128)(2,1)} %copy-done.5) | copy-start | bytes 393220
  140.2 0.7 copy-start.1
  140.9 0.7 copy-start.11
  141.6 0.7 copy-start.14
  171.8 1.0 copy-start.2
  172.7 0.9 copy-start.12
  173.7 0.9 copy-start.15
  174.6 5.3 %copy-start.13 = (f32[128,512]{1,0:T(8,128)S(1)}, f32[128,512]{1,0:T(8,128)}, u32[]{:S(2)}) copy-start(f32[128,512]{1,0:T(8,128)} %copy-done.11) | copy-start | bytes 786436
  174.6 5.3 %copy-start.16 = (bf16[256,512]{1,0:T(8,128)(2,1)S(1)}, bf16[256,512]{1,0:T(8,128)(2,1)}, u32[]{:S(2)}) copy-start(bf16[256,512]{1,0:T(8,128)(2,1)} %copy-done.14) | copy-start | bytes 786436
  201.7 13.5 %all-to-all-start.9 = ((bf16[32,32,128]{2,1,0:T(8,128)(2,1)}), bf16[32,32,128]{2,1,0:T(8,128)(2,1)S(1)}, u32[]{:S(2)}, u32[]{:S(2)}) async-start(bf16[32,32,128]{2,1,0:T(8,128)(2,1)} %get-tuple-element.22), calls=%async_computation.9 | async-start | bytes 524288 | tf_op jit(solution)/shard_map/all_to_all | solution.py:16
  205.6 13.8 %copy-start.8 = (f32[2,128,128]{2,1,0:T(8,128)S(1)}, f32[2,128,128]{2,1,0:T(8,128)}, u32[]{:S(2)}) copy-start(f32[2,128,128]{2,1,0:T(8,128)} %copy-done.7) | copy-start | bytes 393220
  215.2 20.7 %all-to-all-start.14 = ((bf16[16,6,32,256]{3,2,1,0:T(8,128)(2,1)}), bf16[16,6,32,256]{3,2,1,0:T(8,128)(2,1)S(1)}, u32[]{:S(2)}, u32[]{:S(2)}) async-start(bf16[16,6,32,256]{3,2,1,0:T(8,128)(2,1)} %reduce_sum.47), calls=%async_computation.14 | async-start | bytes 3145728 | tf_op jit(solution)/shard_map/all_to_all | solution.py:16
  235.9 25.1 %all-to-all-start.10 = ((bf16[16,128,128]{2,1,0:T(8,128)(2,1)}), bf16[16,128,128]{2,1,0:T(8,128)(2,1)S(1)}, u32[]{:S(2)}, u32[]{:S(2)}) async-start(bf16[16,128,128]{2,1,0:T(8,128)(2,1)} %shard_map.116), calls=%async_computation.10 | async-start | bytes 1048576 | tf_op jit(solution)/shard_map/all_to_all | solution.py:16
  262.3 27.2 %all-to-all-start.15 = ((bf16[16,6,32,256]{3,2,1,0:T(8,128)(2,1)}), bf16[16,6,32,256]{3,2,1,0:T(8,128)(2,1)}, u32[]{:S(2)}, u32[]{:S(2)}) async-start(bf16[16,6,32,256]{3,2,1,0:T(8,128)(2,1)} %bitcast.8), calls=%async_computation.15 | async-start | bytes 3145728 | tf_op jit(solution)/shard_map/all_to_all | solution.py:16
  316.0 9.7 %all-to-all-start.16 = ((bf16[2,16,6,32,256]{4,3,2,1,0:T(8,128)(2,1)}), bf16[2,16,6,32,256]{4,3,2,1,0:T(8,128)(2,1)S(1)}, u32[]{:S(2)}, u32[]{:S(2)}) async-start(bf16[2,16,6,32,256]{4,3,2,1,0:T(8,128)(2,1)} %broadcast_in_dim.17), calls=%async_computation.16 | async-start | bytes 6291456 | tf_op jit(solution)/shard_map/all_to_all | solution.py:16
  326.6 15.8 %all-to-all-start.12 = ((bf16[8,40,1024]{2,1,0:T(8,128)(2,1)}), bf16[8,40,1024]{2,1,0:T(8,128)(2,1)}, u32[]{:S(2)}, u32[]{:S(2)}) async-start(bf16[8,40,1024]{2,1,0:T(8,128)(2,1)} %broadcast_in_dim.15), calls=%async_computation.12 | async-start | bytes 1310720 | tf_op jit(solution)/shard_map/all_to_all | solution.py:16

commit v3 on v2

v3 whole, which is shorter than its diff:
```python
import jax
import jax.numpy as jnp
from jax import lax
from jax.experimental import pallas as pl
from jax.experimental.pallas import tpu as pltpu
from jax.sharding import Mesh
from jax.sharding import PartitionSpec as P

CORES = 2
COLUMNS = 4
TAGS = 16
BF16 = jnp.bfloat16
F32 = jnp.float32


def exchange(parts, axes):
    return lax.all_to_all(parts, axes, split_axis=0, concat_axis=0, tiled=True)


def call(body, outs, args, scratch=(), smem=(), flops=0):
    moved = sum(a.size * a.dtype.itemsize for a in args)
    moved += sum(o.size * jnp.dtype(o.dtype).itemsize for o in outs)
    specs = [
        pl.BlockSpec(memory_space=pltpu.SMEM if i in smem else pltpu.VMEM)
        for i in range(len(args))
    ]
    got = pl.pallas_call(
        body,
        out_shape=tuple(outs),
        in_specs=specs,
        out_specs=tuple(pl.BlockSpec(memory_space=pltpu.VMEM) for _ in outs),
        scratch_shapes=list(scratch),
        compiler_params=pltpu.CompilerParams(vmem_limit_bytes=48 * 1024 * 1024),
        cost_estimate=pl.CostEstimate(flops=flops, bytes_accessed=moved, transcendentals=0),
    )(*args)
    return got


def dot(a, b, da, db):
    return lax.dot_general(a, b, (((da,), (db,)), ((), ())), preferred_element_type=F32)


def pick_body(nx, nz, seq_ref, start_ref, end_ref, states_ref, out_ref):
    tokens, width = states_ref.shape
    half = tokens // 2
    depth = width // (nx * nz)
    own = start_ref.shape[1]
    states = states_ref[...]
    for side, ref in enumerate((start_ref, end_ref)):
        token = ref[...]
        inside = lax.rem(token, half)
        low = (token - inside) == seq_ref[0] * half
        picks = inside + jnp.where(low, 0, half)
        spot = lax.broadcasted_iota(jnp.int32, (tokens, own), 0)
        mask = jnp.where(spot == picks, 1.0, 0.0).astype(BF16)
        rows = dot(mask, states, 0, 0)
        for z in range(nz):
            cut = [rows[:, (x * nz + z) * depth : (x * nz + z + 1) * depth] for x in range(nx)]
            out_ref[side * nz + z] = jnp.concatenate(cut, axis=1).astype(BF16)


def project_body(nx, nz, inner, weight_ref, piece_ref, out_ref):
    full = weight_ref.shape[2]
    weight = weight_ref[...].reshape(-1, full)
    piece = piece_ref[...].reshape(-1, piece_ref.shape[2])
    pre = dot(weight, piece, 0, 1).astype(BF16)
    group = pre.shape[1] // CORES
    for c in range(CORES):
        for z in range(nz):
            for x in range(nx):
                at = (x * nz + z) * inner
                out_ref[c * nz + z, x * inner : (x + 1) * inner, :] = pre[
                    at : at + inner, c * group : (c + 1) * group
                ]


def act_body(nx, nz, got_ref, tags_ref, pre_ref, left_ref, right_ref):
    def total(side):
        sums = got_ref[side * nz].astype(F32)
        for z in range(1, nz):
            sums = sums + got_ref[side * nz + z].astype(F32)
        return sums

    pre_left, pre_right = total(0), total(1)
    pre_ref[0] = pre_left
    pre_ref[1] = pre_right
    left_ref[...] = jax.nn.gelu(pre_left).astype(BF16)
    block = jnp.concatenate([jax.nn.gelu(pre_right), tags_ref[...]], axis=0).astype(BF16)
    for z in range(nz):
        right_ref[z] = block


def spread_body(nx, nz, inner, left_ref, got_ref, out_ref):
    full = nx * nz * inner
    rows = nx * inner
    tags = got_ref[0].astype(F32)[rows:]
    for z in range(1, nz):
        tags = tags + got_ref[z].astype(F32)[rows:]
    tags = tags.astype(BF16)
    for to in range(nx):
        for z in range(nz):
            for x in range(nx):
                at = (x * nz + z) * inner
                out_ref[to, at : at + inner, :] = got_ref[z, x * inner : (x + 1) * inner, :]
        out_ref[to, full : full + inner, :] = left_ref[to * inner : (to + 1) * inner, :]
        out_ref[to, full + inner : full + inner + TAGS, :] = tags


def score_body(nx, nz, inner, weight_ref, got_ref, out_ref, left_ref, right_ref, tags_ref):
    labels, _, full = weight_ref.shape
    group = got_ref.shape[2]
    for x in range(nx):
        lanes = slice(x * group, (x + 1) * group)
        right_ref[:, lanes] = got_ref[x, :full, :]
        left_ref[:, lanes] = got_ref[x, full : full + inner, :].astype(F32)
        tags_ref[:, lanes] = got_ref[x, full + inner : full + inner + TAGS, :].astype(F32)
    for i in range(nx * nz):
        if i % nz >= labels // 8:
            out_ref[i] = jnp.zeros((8, group), F32)

    def step(lb, carry):
        weight = weight_ref[pl.ds(lb * 8, 8)].reshape(8 * inner, full)
        image = dot(weight, right_ref[...], 1, 0).reshape(8, inner, nx * group)
        total = jnp.sum(image * left_ref[...][None], axis=1)
        for x in range(nx):
            out_ref[x * nz + lb] = total[:, x * group : (x + 1) * group]
        return carry

    lax.fori_loop(0, labels // 8, step, 0)


def slope_body(
    nx, nz, inner, own, weight_ref, left_ref, right_ref, tags_ref, score_ref,
    out_ref, outer_ref, loss_ref, slope_ref,
):
    labels, _, full = weight_ref.shape
    group = score_ref.shape[2]
    spans = nx * group
    scores = jnp.concatenate(
        [
            jnp.concatenate([score_ref[x * nz + b] for x in range(nx)], axis=1)
            for b in range(labels // 8)
        ],
        axis=0,
    )
    gold, live = tags_ref[0:1, :], tags_ref[1:2, :]
    most = jnp.max(scores, axis=0, keepdims=True)
    log_total = most + jnp.log(jnp.sum(jnp.exp(scores - most), axis=0, keepdims=True))
    spot = lax.broadcasted_iota(jnp.int32, scores.shape, 0).astype(F32)
    onehot = jnp.where(spot == gold, 1.0, 0.0)
    picked = jnp.sum(scores * onehot, axis=0, keepdims=True)
    loss_ref[...] = live * (log_total - picked)
    slope = live * (jnp.exp(scores - log_total) - onehot) / own
    slope_ref[...] = slope.astype(BF16).astype(F32)

    def step(lb, left_sum):
        slope = slope_ref[pl.ds(lb * 8, 8), :]
        weight = weight_ref[pl.ds(lb * 8, 8)].reshape(8 * inner, full)
        image = dot(weight, right_ref[...], 1, 0).reshape(8, inner, spans)
        outer = (slope[:, None, :] * left_ref[...][None]).astype(BF16)
        outer_ref[pl.ds(lb * 8 * inner, 8 * inner), :] = outer.reshape(8 * inner, spans)
        return left_sum + jnp.sum(image * slope[:, None, :], axis=0)

    left_sum = lax.fori_loop(0, labels // 8, step, jnp.zeros((inner, spans), F32)).astype(BF16)
    weight = weight_ref[...].reshape(labels * inner, full)
    right_sum = dot(weight, outer_ref[...], 0, 0).astype(BF16)
    for to in range(nx):
        lanes = slice(to * group, (to + 1) * group)
        for z in range(nz):
            for x in range(nx):
                at = (x * nz + z) * inner
                spot = (z * nx + x) * inner
                out_ref[to, spot : spot + inner, :] = right_sum[at : at + inner, lanes]
        out_ref[to, full : full + inner, :] = left_sum[:, lanes]


def flat_body(outer_ref, right_ref, out_ref):
    out_ref[...] = dot(outer_ref[...], right_ref[...], 1, 1).astype(BF16)


def fold_body(nx, nz, got_ref, out_ref):
    _, rows, _ = out_ref.shape
    for z in range(nz):
        block = got_ref[0, z * rows : (z + 1) * rows, :].astype(F32)
        for x in range(1, nx):
            block = block + got_ref[x, z * rows : (z + 1) * rows, :].astype(F32)
        out_ref[z] = block.astype(BF16)


def lower_body(ny, nx, nz, inner, pre_ref, left_got, right_got, out_ref):
    full = nx * nz * inner
    grad_left = jnp.concatenate(
        [left_got[x, full : full + inner, :].astype(F32) for x in range(nx)], axis=0
    )
    grad_right = right_got[0].astype(F32)
    for z in range(1, nz):
        grad_right = grad_right + right_got[z].astype(F32)
    take = grad_left.shape[0] // ny
    for side, grad in enumerate((grad_left, grad_right)):
        _, back = jax.vjp(jax.nn.gelu, pre_ref[side])
        lowered = back(grad)[0].astype(BF16)
        for y in range(ny):
            for z in range(nz):
                out_ref[(y * CORES + side) * nz + z] = lowered[y * take : (y + 1) * take]


def weight_body(ny, nx, nz, inner, low_ref, piece_ref, out_ref, wide_ref):
    group = low_ref.shape[2]
    for s in range(ny * CORES):
        for z in range(nz):
            wide_ref[z * inner : (z + 1) * inner, s * group : (s + 1) * group] = low_ref[s * nz + z]
    piece = piece_ref[...].reshape(-1, piece_ref.shape[3])
    grad = dot(piece, wide_ref[...], 0, 1).astype(BF16)
    depth = out_ref.shape[1]
    for x in range(nx):
        out_ref[x] = grad[x * depth : (x + 1) * depth]


def total_body(got_ref, out_ref):
    total = got_ref[0].astype(F32)
    for x in range(1, got_ref.shape[0]):
        total = total + got_ref[x].astype(F32)
    total = total.astype(BF16)
    for i in range(out_ref.shape[0]):
        out_ref[i] = total


def join_body(got_ref, start_ref, end_ref):
    width = got_ref.shape[2]
    for y in range(got_ref.shape[0] // CORES):
        start_ref[:, y * width : (y + 1) * width] = got_ref[y * CORES]
        end_ref[:, y * width : (y + 1) * width] = got_ref[y * CORES + 1]


def build(ny, nx, nz):
    def shards(states, span_start, span_end, gold, live, start_proj, end_proj, biaffine):
        x_index, z_index = lax.axis_index("x"), lax.axis_index("z")
        seq_index = x_index * nz + z_index
        core = lax.axis_index("core")
        own = span_start.shape[1]
        labels, inner, full = biaffine.shape
        depth = start_proj.shape[0]
        group = own * nz
        spans = group * nx
        width = full // ny
        rows = nx * inner
        shape = jax.ShapeDtypeStruct

        side_proj = jnp.where(core == 0, start_proj, end_proj)
        weights = lax.all_gather(side_proj, "x", axis=0)

        (picked,) = call(
            lambda *refs: pick_body(nx, nz, *refs),
            [shape((CORES * nz, own, nx * depth), BF16)],
            (seq_index.reshape(1), span_start, span_end, states[0]),
            smem=(0,),
        )
        pieces = exchange(picked, ("core", "z"))
        all_pieces = lax.all_gather(pieces, "y", axis=0)

        (pre_parts,) = call(
            lambda *refs: project_body(nx, nz, inner, *refs),
            [shape((CORES * nz, rows, group), BF16)],
            (weights, pieces),
            flops=2 * full * nx * depth * group * CORES,
        )
        pre_got = exchange(pre_parts, ("core", "z"))

        tags = jnp.concatenate([gold, live], axis=0).astype(F32)
        tags = lax.dynamic_update_slice(jnp.zeros((TAGS, group), F32), tags, (0, z_index * own))
        pre, left_own, right_pay = call(
            lambda *refs: act_body(nx, nz, *refs),
            [
                shape((2, rows, group), F32),
                shape((rows, group), BF16),
                shape((nz, rows + TAGS, group), BF16),
            ],
            (pre_got, tags),
        )
        right_column = exchange(right_pay, "z")
        (act_pay,) = call(
            lambda *refs: spread_body(nx, nz, inner, *refs),
            [shape((nx, full + inner + TAGS, group), BF16)],
            (left_own, right_column),
        )
        act_got = exchange(act_pay, "x")

        score_parts, left, right, all_tags = call(
            lambda *refs: score_body(nx, nz, inner, *refs),
            [
                shape((nx * nz, 8, group), F32),
                shape((inner, spans), F32),
                shape((full, spans), BF16),
                shape((TAGS, spans), F32),
            ],
            (biaffine, act_got),
            flops=2 * labels * inner * full * spans,
        )
        score_got = exchange(score_parts, ("x", "z"))
        score_sum = jnp.sum(score_got, axis=0)
        scores = exchange(jnp.broadcast_to(score_sum[None], score_got.shape), ("x", "z"))

        grad_pay, outer, loss = call(
            lambda *refs: slope_body(nx, nz, inner, own, *refs),
            [
                shape((nx, full + inner, group), BF16),
                shape((labels * inner, spans), BF16),
                shape((1, spans), F32),
            ],
            (biaffine, left, right, all_tags, scores),
            scratch=(pltpu.VMEM((labels, spans), F32),),
            flops=4 * labels * inner * full * spans,
        )
        span_loss = lax.dynamic_slice_in_dim(loss, seq_index * own, own, 1)
        (flat,) = call(
            flat_body,
            [shape((labels * inner, full), BF16)],
            (outer, right),
            flops=2 * labels * inner * full * spans,
        )
        grad_biaffine = lax.psum(flat, ("y", "core")).reshape(labels, inner, full)

        grad_got = exchange(grad_pay, "x")
        (fold_pay,) = call(
            lambda *refs: fold_body(nx, nz, *refs),
            [shape((nz, rows, group), BF16)],
            (grad_got,),
        )
        fold_got = exchange(fold_pay, "z")
        (lowered,) = call(
            lambda *refs: lower_body(ny, nx, nz, inner, *refs),
            [shape((ny * CORES * nz, rows // ny, group), BF16)],
            (pre, grad_got, fold_got),
        )
        lowered_got = exchange(lowered, ("y", "core", "z"))
        (grad_parts,) = call(
            lambda *refs: weight_body(ny, nx, nz, inner, *refs),
            [shape((nx, depth, width), BF16)],
            (lowered_got, all_pieces),
            scratch=(pltpu.VMEM((width, ny * CORES * group), BF16),),
            flops=2 * full * nx * depth * group * CORES,
        )
        (grad_own,) = call(
            total_body, [shape((ny * CORES, depth, width), BF16)], (exchange(grad_parts, "x"),)
        )
        grad_start, grad_end = call(
            join_body,
            [shape((depth, full), BF16), shape((depth, full), BF16)],
            (exchange(grad_own, ("y", "core")),),
        )
        return span_loss, grad_start, grad_end, grad_biaffine

    return shards


def solution(mesh):
    ny, nz = mesh.shape["dp"] // CORES, mesh.shape["seq"] // COLUMNS
    fine = Mesh(mesh.devices.reshape(ny, CORES, COLUMNS, nz), ("y", "core", "x", "z"))
    dp, seq = ("y", "core"), ("x", "z")
    placed = (
        P(dp, seq, None),
        P(dp, seq),
        P(dp, seq),
        P(dp, seq),
        P(dp, seq),
        P(seq, None),
        P(seq, None),
        P(None, seq, None),
    )
    return jax.shard_map(
        build(ny, COLUMNS, nz),
        mesh=fine,
        in_specs=placed,
        out_specs=(P(dp, seq), P(seq, None), P(seq, None), P(None, seq, None)),
        check_vma=False,
    )
```

time: 346 us -> 270 us (0.78)
  blocking collectives: 147 us -> 99.5 us
  starting transfers between devices: 54.4 us -> 31.6 us
  local copies, waits for them, and re-layouts: 33.6 us -> 13.6 us
  between operations: 0.83 us -> 15.6 us
  other arithmetic: 7.12 us -> 1.79 us
    all_to_all x8 -> x7, blocking collectives: 147 us -> 99.5 us  [exchange(): return lax.all_to_all(parts, axes, split_axis=0, concat_axis=0, tiled=True)]
    all_to_all x9 -> x4, waiting for transfers between devices: 85.1 us -> 46.7 us  [exchange(): return lax.all_to_all(parts, axes, split_axis=0, concat_axis=0, tiled=True)]
    psum x0 -> x1, waiting for transfers between devices: none -> 33.2 us  [shards(): grad_biaffine = lax.psum(flat, ('y', 'core')).reshape(labels, inner, full)]
    all_to_all x9 -> x4, starting transfers between devices: 54.4 us -> 31.5 us  [exchange(): return lax.all_to_all(parts, axes, split_axis=0, concat_axis=0, tiled=True)]
    reshape x2 -> x0, local copies, waits for them, and re-layouts: 10.1 us -> none  [the longest x1 6.06 us: shards(): grad_biaffine = flat.reshape(labels, inner, full)]
    all_gather x0 -> x2, waiting for transfers between devices: none -> 7.01 us  [the longest x1 6.98 us: shards(): weights = lax.all_gather(side_proj, 'x', axis=0)]
    reduce_sum x3 -> x0, other arithmetic: 6.13 us -> none  [the longest x2 4.56 us: shards(): flat = jnp.sum(flat.astype(F32), axis=0).astype(BF16)]
    broadcast_in_dim x5 -> x1, local copies, waits for them, and re-layouts: 5.94 us -> 0.01 us  [shards(): jnp.zeros((TAGS, group), F32)]
  transfers between devices with their start and end apart: 9 -> 7, of which waited for: 8 -> 6; matrix products, arithmetic and copies ran while one was open for 6% -> 0% of each run, Pallas kernels for 0% -> 5%
where the time goes in v3:
time: 270 us; the launch traced here: 269 us
  blocking collectives  99.5 us (37%)
  waiting for transfers between devices  87.5 us (32%)
  starting transfers between devices  31.6 us (12%)
  Pallas kernels  18.9 us (7%)
  between operations  15.6 us (6%)
  local copies, waits for them, and re-layouts  13.6 us (5%)
    all_to_all x7, blocking collectives, exchange(): return lax.all_to_all(parts, axes, split_axis=0, concat_axis=0, tiled=True)  99.5 us
    all_to_all x4, waiting for transfers between devices, exchange(): return lax.all_to_all(parts, axes, split_axis=0, concat_axis=0, tiled=True)  46.7 us
    psum x1, waiting for transfers between devices, shards(): grad_biaffine = lax.psum(flat, ('y', 'core')).reshape(labels, inner, full)  33.2 us
    all_to_all x4, starting transfers between devices, exchange(): return lax.all_to_all(parts, axes, split_axis=0, concat_axis=0, tiled=True)  31.5 us
    pallas_call x12, Pallas kernels, call(): pl.pallas_call(body, out_shape=tuple(outs), in_specs=specs, out_specs=tup...  18.9 us
    unnamed x25, local copies, waits for them, and re-layouts  12 us
    all_gather x1, waiting for transfers between devices, shards(): weights = lax.all_gather(side_proj, 'x', axis=0)  6.98 us
  transfers between devices with their start and end apart: 7, of which 6 were waited for; matrix products, arithmetic and copies ran while one was open for 0% of the time, Pallas kernels for 5%

profile of v3, /device:TPU:1, one launch (start us, length us, event | category | flops | bytes accessed | tf_op | source)
XLA Modules:
  0.0 268.6 jit_solution(2190170890844107535)
XLA Ops:
  8.1 1.7 broadcast_select_fusion
  9.8 1.7 copy-done.1
  12.9 0.9 shard_map.111
  13.8 20.5 %all_to_all.55.refs_1_ = bf16[16,16,640]{2,1,0:T(8,128)(2,1)S(1)} all-to-all(bf16[16,16,640]{2,1,0:T(8,128)(2,1)S(1)} %shard_map.111), channel_id=1, replica_groups=mesh['y'=4,'core'=2,'x'=4,'z'=8] {'core','z'}, dimensions={0} | all-to-all | bytes 655360 | tf_op jit(solution)/shard_map/all_to_all | solution.py:17
  34.3 7.0 %all-gather.5.cloned.1.call-done = bf16[640,1024]{1,0:T(8,128)(2,1)} async-done(((bf16[160,1024]{1,0:T(8,128)(2,1)}), bf16[640,1024]{1,0:T(8,128)(2,1)}) %all-gather.5.cloned.1.call-update) | async-done | bytes 1310736 | tf_op jit(solution)/shard_map/all_gather | solution.py:250
  41.3 1.3 copy-done.3
  42.6 1.4 shard_map.112
  44.1 8.9 %all-to-all-start.1 = ((bf16[16,128,128]{2,1,0:T(8,128)(2,1)}), bf16[16,128,128]{2,1,0:T(8,128)(2,1)S(1)}, u32[]{:S(2)}, u32[]{:S(2)}) async-start(bf16[16,128,128]{2,1,0:T(8,128)(2,1)} %shard_map.112), calls=%async_computation.1 | async-start | bytes 1048576 | tf_op jit(solution)/shard_map/all_to_all | solution.py:17
  53.4 14.3 %all-to-all-done.1.refs_0_ = bf16[16,128,128]{2,1,0:T(8,128)(2,1)S(1)} async-done(((bf16[16,128,128]{2,1,0:T(8,128)(2,1)}), bf16[16,128,128]{2,1,0:T(8,128)(2,1)S(1)}, u32[]{:S(2)}, u32[]{:S(2)}) %all-to-all-start.1) | async-done | bytes 524320 | tf_op jit(solution)/shard_map/all_to_all | solution.py:17
  67.8 15.9 %all_to_all.56.refs_1_ = bf16[8,144,128]{2,1,0:T(8,128)(2,1)S(1)} all-to-all(bf16[8,144,128]{2,1,0:T(8,128)(2,1)S(1)} %get-tuple-element.17), channel_id=1, replica_groups=mesh['y'=4,'core'=2,'x'=4,'z'=8] {'z'}, dimensions={0} | all-to-all | bytes 589824 | tf_op jit(solution)/shard_map/all_to_all | solution.py:17
  83.9 16.4 %all_to_all.57.refs_1_ = bf16[4,1072,128]{2,1,0:T(8,128)(2,1)S(1)} all-to-all(bf16[4,1072,128]{2,1,0:T(8,128)(2,1)S(1)} %shard_map.114), channel_id=1, replica_groups=mesh['y'=4,'core'=2,'x'=4,'z'=8] {'x'}, dimensions={0} | all-to-all | bytes 2195456 | tf_op jit(solution)/shard_map/all_to_all | solution.py:17
  100.3 2.9 %shard_map.115 = (f32[32,8,128]{2,1,0:T(8,128)S(1)}, f32[32,512]{1,0:T(8,128)S(1)}, bf16[1024,512]{1,0:T(8,128)(2,1)S(1)}, f32[16,512]{1,0:T(8,128)S(1)}) custom-call(bf16[48,32,1024]{2,1,0:T(8,128)(2,1)S(1)} %copy-done.6, bf16[4,1072,128]{2,1,0:T(8,128)(2,1)S(1)} %all_to_all.57.refs_1_), custom_call_target="tpu_custom_call" | custom-call | flops 1610612736 | bytes 5521408 | tf_op jit(solution)/shard_map/pallas_call | solution.py:27
  103.2 1.0 copy-done.7
  104.1 13.9 %all_to_all.58 = f32[32,8,128]{2,1,0:T(8,128)S(1)} all-to-all(f32[32,8,128]{2,1,0:T(8,128)S(1)} %get-tuple-element.21), channel_id=1, replica_groups=mesh['y'=4,'core'=2,'x'=4,'z'=8] {'x','z'}, dimensions={0} | all-to-all | bytes 262144 | tf_op jit(solution)/shard_map/all_to_all | solution.py:17
  118.7 3.9 %all-to-all-start.5 = ((f32[32,8,128]{2,1,0:T(8,128)}), f32[32,8,128]{2,1,0:T(8,128)S(1)}, u32[]{:S(2)}, u32[]{:S(2)}) async-start(f32[32,8,128]{2,1,0:T(8,128)} %broadcast_in_dim.10), calls=%async_computation.5 | async-start | bytes 262144 | tf_op jit(solution)/shard_map/all_to_all | solution.py:17
  123.2 8.6 %all-to-all-done.5.refs_4_ = f32[32,8,128]{2,1,0:T(8,128)S(1)} async-done(((f32[32,8,128]{2,1,0:T(8,128)}), f32[32,8,128]{2,1,0:T(8,128)S(1)}, u32[]{:S(2)}, u32[]{:S(2)}) %all-to-all-start.5) | async-done | bytes 131104 | tf_op jit(solution)/shard_map/all_to_all | solution.py:17
  131.7 1.2 copy-done.8
  133.0 6.5 %shard_map.116 = (bf16[4,1056,128]{2,1,0:T(8,128)(2,1)S(1)}, bf16[1536,512]{1,0:T(8,128)(2,1)S(1)}, f32[1,512]{1,0:T(1,128)S(1)}) custom-call(bf16[48,32,1024]{2,1,0:T(8,128)(2,1)} %refs_0_.3, f32[32,512]{1,0:T(8,128)S(1)} %get-tuple-element.18.refs_1_, bf16[1024,512]{1,0:T(8,128)(2,1)S(1)} %copy-done.8, f32[16,512]{1,0:T(8,128)S(1)} %get-tuple-element.20.refs_3_, ...), custom_call_target="tpu_custom_call" | custom-call | flops 3221225472 | bytes 7079936 | tf_op jit(solution)/shard_map/pallas_call | solution.py:27
  139.4 12.7 %all_to_all.59.refs_0_.refs_1_ = bf16[4,1056,128]{2,1,0:T(8,128)(2,1)S(1)} all-to-all(bf16[4,1056,128]{2,1,0:T(8,128)(2,1)S(1)} %get-tuple-element.24), channel_id=1, replica_groups=mesh['y'=4,'core'=2,'x'=4,'z'=8] {'x'}, dimensions={0} | all-to-all | bytes 2162688 | tf_op jit(solution)/shard_map/all_to_all | solution.py:17
  152.2 11.9 %all_to_all.60.refs_2_ = bf16[8,128,128]{2,1,0:T(8,128)(2,1)S(1)} all-to-all(bf16[8,128,128]{2,1,0:T(8,128)(2,1)S(1)} %shard_map.117), channel_id=1, replica_groups=mesh['y'=4,'core'=2,'x'=4,'z'=8] {'z'}, dimensions={0} | all-to-all | bytes 524288 | tf_op jit(solution)/shard_map/all_to_all | solution.py:17
  164.1 0.9 shard_map.118
  165.0 12.0 %all-to-all-start.8 = ((bf16[64,32,128]{2,1,0:T(8,128)(2,1)}), bf16[64,32,128]{2,1,0:T(8,128)(2,1)S(1)}, u32[]{:S(2)}, u32[]{:S(2)}) async-start(bf16[64,32,128]{2,1,0:T(8,128)(2,1)} %shard_map.118), calls=%async_computation.8 | async-start | bytes 1048576 | tf_op jit(solution)/shard_map/all_to_all | solution.py:17
  177.1 3.5 %shard_map.122 = bf16[1536,1024]{1,0:T(8,128)(2,1)} custom-call(bf16[1536,512]{1,0:T(8,128)(2,1)S(1)} %get-tuple-element.27.outer_ref, bf16[1024,512]{1,0:T(8,128)(2,1)S(1)} %copy-done.9), custom_call_target="tpu_custom_call" | custom-call | flops 1610612736 | bytes 5767168 | tf_op jit(solution)/shard_map/pallas_call | solution.py:27
  180.7 13.5 %all-to-all-done.8.refs_0_ = bf16[64,32,128]{2,1,0:T(8,128)(2,1)S(1)} async-done(((bf16[64,32,128]{2,1,0:T(8,128)(2,1)}), bf16[64,32,128]{2,1,0:T(8,128)(2,1)S(1)}, u32[]{:S(2)}, u32[]{:S(2)}) %all-to-all-start.8) | async-done | bytes 524320 | tf_op jit(solution)/shard_map/all_to_all | solution.py:17
  194.2 1.3 copy-done.2
  196.1 8.3 %all_to_all.61.got_ref = bf16[4,160,256]{2,1,0:T(8,128)(2,1)S(1)} all-to-all(bf16[4,160,256]{2,1,0:T(8,128)(2,1)S(1)} %shard_map.119), channel_id=1, replica_groups=mesh['y'=4,'core'=2,'x'=4,'z'=8] {'x'}, dimensions={0} | all-to-all | bytes 655360 | tf_op jit(solution)/shard_map/all_to_all | solution.py:17
  204.4 0.9 shard_map.120
  205.3 6.7 %all-to-all-start.10 = ((bf16[8,160,256]{2,1,0:T(8,128)(2,1)}), bf16[8,160,256]{2,1,0:T(8,128)(2,1)S(1)}, u32[]{:S(2)}, u32[]{:S(2)}) async-start(bf16[8,160,256]{2,1,0:T(8,128)(2,1)} %shard_map.120), calls=%async_computation.10 | async-start | bytes 1310720 | tf_op jit(solution)/shard_map/all_to_all | solution.py:17
  212.6 10.3 %all-to-all-done.10.got_ref = bf16[8,160,256]{2,1,0:T(8,128)(2,1)S(1)} async-done(((bf16[8,160,256]{2,1,0:T(8,128)(2,1)}), bf16[8,160,256]{2,1,0:T(8,128)(2,1)S(1)}, u32[]{:S(2)}, u32[]{:S(2)}) %all-to-all-start.10) | async-done | bytes 655392 | tf_op jit(solution)/shard_map/all_to_all | solution.py:17
  222.9 0.9 shard_map.121
  223.8 33.2 %all-reduce.2.cloned.1.call-done = bf16[48,32,1024]{2,1,0:T(8,128)(2,1)} async-done(((bf16[48,32,1024]{2,1,0:T(8,128)(2,1)}), bf16[48,32,1024]{2,1,0:T(8,128)(2,1)}) %all-reduce.2.cloned.1.call-update) | async-done | bytes 3145744 | tf_op jit(solution)/shard_map/psum | solution.py:321
  257.0 4.1 %copy.14 = bf16[48,32,1024]{2,1,0:T(8,128)(2,1)} copy(bf16[48,32,1024]{2,1,0:T(8,128)(2,1)} %all-reduce.2.cloned.1.call-done) | data formatting | bytes 6291456
  (36 shorter events, 4.7 us)
Async XLA Ops:
  8.0 33.3 %all-gather.5.cloned.1.call-start = ((), (), s32[]{:S(2)}) async-start(), calls=%async_computation.12 | async-start | bytes 1638400 | tf_op jit(solution)/shard_map/all_gather | solution.py:250
  9.8 1.7 copy-start.1
  11.6 0.7 copy-start.4
  12.2 0.7 copy-start.5
  34.3 9.7 %copy-start = (bf16[16,16,640]{2,1,0:T(8,128)(2,1)}, bf16[16,16,640]{2,1,0:T(8,128)(2,1)S(1)}, u32[]{:S(2)}) copy-start(bf16[16,16,640]{2,1,0:T(8,128)(2,1)S(1)} %all_to_all.55.refs_1_) | copy-start | bytes 983044
  41.3 1.3 copy-start.3
  42.6 10.3 %copy-start.10 = (s32[1,16]{1,0:T(1,128)S(1)}, s32[1,16]{1,0:T(1,128)}, u32[]{:S(2)}) copy-start(s32[1,16]{1,0:T(1,128)} %param.12) | copy-start | bytes 196
  42.6 10.3 %copy-start.11 = (s32[1,16]{1,0:T(1,128)S(1)}, s32[1,16]{1,0:T(1,128)}, u32[]{:S(2)}) copy-start(s32[1,16]{1,0:T(1,128)} %param.11) | copy-start | bytes 196
  44.1 23.7 %all-to-all-start.1 = ((bf16[16,128,128]{2,1,0:T(8,128)(2,1)}), bf16[16,128,128]{2,1,0:T(8,128)(2,1)S(1)}, u32[]{:S(2)}, u32[]{:S(2)}) async-start(bf16[16,128,128]{2,1,0:T(8,128)(2,1)} %shard_map.112), calls=%async_computation.1 | async-start | bytes 1048576 | tf_op jit(solution)/shard_map/all_to_all | solution.py:17
  83.8 16.5 %copy-start.6 = (bf16[48,32,1024]{2,1,0:T(8,128)(2,1)S(1)}, bf16[48,32,1024]{2,1,0:T(8,128)(2,1)}, u32[]{:S(2)}) copy-start(bf16[48,32,1024]{2,1,0:T(8,128)(2,1)} %refs_0_.3) | copy-start | bytes 9437188
  103.2 1.0 copy-start.7
  118.7 13.0 %all-to-all-start.5 = ((f32[32,8,128]{2,1,0:T(8,128)}), f32[32,8,128]{2,1,0:T(8,128)S(1)}, u32[]{:S(2)}, u32[]{:S(2)}) async-start(f32[32,8,128]{2,1,0:T(8,128)} %broadcast_in_dim.10), calls=%async_computation.5 | async-start | bytes 262144 | tf_op jit(solution)/shard_map/all_to_all | solution.py:17
  122.6 58.1 %all-gather.7.cloned.1.call-start = ((), (), s32[]{:S(2)}) async-start(), calls=%async_computation.13 | async-start | bytes 1638400 | tf_op jit(solution)/shard_map/all_gather | solution.py:259
  131.7 1.2 copy-start.8
  164.1 13.0 %copy-start.9 = (bf16[1024,512]{1,0:T(8,128)(2,1)S(1)}, bf16[1024,512]{1,0:T(8,128)(2,1)}, u32[]{:S(2)}) copy-start(bf16[1024,512]{1,0:T(8,128)(2,1)} %copy-done.7) | copy-start | bytes 3145732
  165.0 29.1 %all-to-all-start.8 = ((bf16[64,32,128]{2,1,0:T(8,128)(2,1)}), bf16[64,32,128]{2,1,0:T(8,128)(2,1)S(1)}, u32[]{:S(2)}, u32[]{:S(2)}) async-start(bf16[64,32,128]{2,1,0:T(8,128)(2,1)} %shard_map.118), calls=%async_computation.8 | async-start | bytes 1048576 | tf_op jit(solution)/shard_map/all_to_all | solution.py:17
  177.1 80.0 %all-reduce.2.cloned.1.call-start = ((), (), s32[]{:S(2)}) async-start(), calls=%async_computation.11 | async-start | bytes 6291456 | tf_op jit(solution)/shard_map/psum | solution.py:321
  194.2 1.3 copy-start.2
  205.3 17.6 %all-to-all-start.10 = ((bf16[8,160,256]{2,1,0:T(8,128)(2,1)}), bf16[8,160,256]{2,1,0:T(8,128)(2,1)S(1)}, u32[]{:S(2)}, u32[]{:S(2)}) async-start(bf16[8,160,256]{2,1,0:T(8,128)(2,1)} %shard_map.120), calls=%async_computation.10 | async-start | bytes 1310720 | tf_op jit(solution)/shard_map/all_to_all | solution.py:17
Sparse Core Ops, SparseCore 0:
  11.2 30.0 all-gather.4
  180.9 76.1 all-reduce.1
Sparse Core Ops, SparseCore 1:
  125.4 30.4 all-gather.6

commit v4 on v3

--- a/solution.py
+++ b/solution.py
@@ -8,7 +8,6 @@
 
 CORES = 2
 COLUMNS = 4
-TAGS = 16
 BF16 = jnp.bfloat16
 F32 = jnp.float32
 
@@ -17,11 +16,13 @@
     return lax.all_to_all(parts, axes, split_axis=0, concat_axis=0, tiled=True)
 
 
-def call(body, outs, args, scratch=(), smem=(), flops=0):
+def call(body, outs, args, scratch=(), smem=(), hbm=(), flops=0, room=16):
     moved = sum(a.size * a.dtype.itemsize for a in args)
     moved += sum(o.size * jnp.dtype(o.dtype).itemsize for o in outs)
     specs = [
-        pl.BlockSpec(memory_space=pltpu.SMEM if i in smem else pltpu.VMEM)
+        pl.BlockSpec(
+            memory_space=pltpu.SMEM if i in smem else pltpu.HBM if i in hbm else pltpu.VMEM
+        )
         for i in range(len(args))
     ]
     got = pl.pallas_call(
@@ -30,7 +31,7 @@
         in_specs=specs,
         out_specs=tuple(pl.BlockSpec(memory_space=pltpu.VMEM) for _ in outs),
         scratch_shapes=list(scratch),
-        compiler_params=pltpu.CompilerParams(vmem_limit_bytes=48 * 1024 * 1024),
+        compiler_params=pltpu.CompilerParams(vmem_limit_bytes=room * 1024 * 1024),
         cost_estimate=pl.CostEstimate(flops=flops, bytes_accessed=moved, transcendentals=0),
     )(*args)
     return got
@@ -40,11 +41,22 @@
     return lax.dot_general(a, b, (((da,), (db,)), ((), ())), preferred_element_type=F32)
 
 
-def pick_body(nx, nz, seq_ref, start_ref, end_ref, states_ref, out_ref):
+def pick_body(
+    nx, nz, seq_ref, start_hbm, end_hbm, states_hbm, out_ref, start_ref, end_ref, states_ref, sems
+):
     tokens, width = states_ref.shape
     half = tokens // 2
     depth = width // (nx * nz)
     own = start_ref.shape[1]
+    copies = [
+        pltpu.make_async_copy(states_hbm, states_ref, sems.at[0]),
+        pltpu.make_async_copy(start_hbm, start_ref, sems.at[1]),
+        pltpu.make_async_copy(end_hbm, end_ref, sems.at[2]),
+    ]
+    for copy in copies:
+        copy.start()
+    for copy in copies[1:] + copies[:1]:
+        copy.wait()
     states = states_ref[...]
     for side, ref in enumerate((start_ref, end_ref)):
         token = ref[...]
@@ -74,7 +86,7 @@
                 ]
 
 
-def act_body(nx, nz, got_ref, tags_ref, pre_ref, left_ref, right_ref):
+def act_body(nx, nz, got_ref, pre_ref, left_ref, right_ref):
     def total(side):
         sums = got_ref[side * nz].astype(F32)
         for z in range(1, nz):
@@ -85,37 +97,32 @@
     pre_ref[0] = pre_left
     pre_ref[1] = pre_right
     left_ref[...] = jax.nn.gelu(pre_left).astype(BF16)
-    block = jnp.concatenate([jax.nn.gelu(pre_right), tags_ref[...]], axis=0).astype(BF16)
+    block = jax.nn.gelu(pre_right).astype(BF16)
     for z in range(nz):
         right_ref[z] = block
 
 
 def spread_body(nx, nz, inner, left_ref, got_ref, out_ref):
     full = nx * nz * inner
-    rows = nx * inner
-    tags = got_ref[0].astype(F32)[rows:]
-    for z in range(1, nz):
-        tags = tags + got_ref[z].astype(F32)[rows:]
-    tags = tags.astype(BF16)
     for to in range(nx):
         for z in range(nz):
             for x in range(nx):
                 at = (x * nz + z) * inner
                 out_ref[to, at : at + inner, :] = got_ref[z, x * inner : (x + 1) * inner, :]
         out_ref[to, full : full + inner, :] = left_ref[to * inner : (to + 1) * inner, :]
-        out_ref[to, full + inner : full + inner + TAGS, :] = tags
-
-
-def score_body(nx, nz, inner, weight_ref, got_ref, out_ref, left_ref, right_ref, tags_ref):
+
+
+def score_body(nx, nz, inner, weight_ref, got_ref, tags_ref, out_ref, left_ref, right_ref):
     labels, _, full = weight_ref.shape
     group = got_ref.shape[2]
     for x in range(nx):
         lanes = slice(x * group, (x + 1) * group)
         right_ref[:, lanes] = got_ref[x, :full, :]
         left_ref[:, lanes] = got_ref[x, full : full + inner, :].astype(F32)
-        tags_ref[:, lanes] = got_ref[x, full + inner : full + inner + TAGS, :].astype(F32)
     for i in range(nx * nz):
-        if i % nz >= labels // 8:
+        if i % nz == labels // 8:
+            out_ref[i] = tags_ref[i // nz]
+        elif i % nz > labels // 8:
             out_ref[i] = jnp.zeros((8, group), F32)
 
     def step(lb, carry):
@@ -130,7 +137,7 @@
 
 
 def slope_body(
-    nx, nz, inner, own, weight_ref, left_ref, right_ref, tags_ref, score_ref,
+    nx, nz, inner, own, weight_ref, left_ref, right_ref, score_ref,
     out_ref, outer_ref, loss_ref, slope_ref,
 ):
     labels, _, full = weight_ref.shape
@@ -143,7 +150,8 @@
         ],
         axis=0,
     )
-    gold, live = tags_ref[0:1, :], tags_ref[1:2, :]
+    tags = jnp.concatenate([score_ref[x * nz + labels // 8] for x in range(nx)], axis=1)
+    gold, live = tags[0:1], tags[1:2]
     most = jnp.max(scores, axis=0, keepdims=True)
     log_total = most + jnp.log(jnp.sum(jnp.exp(scores - most), axis=0, keepdims=True))
     spot = lax.broadcasted_iota(jnp.int32, scores.shape, 0).astype(F32)
@@ -174,8 +182,10 @@
         out_ref[to, full : full + inner, :] = left_sum[:, lanes]
 
 
-def flat_body(outer_ref, right_ref, out_ref):
-    out_ref[...] = dot(outer_ref[...], right_ref[...], 1, 1).astype(BF16)
+def flat_body(outer_ref, right_ref, *outs):
+    half = outs[0].shape[0]
+    for i, out_ref in enumerate(outs):
+        out_ref[...] = dot(outer_ref[i * half : (i + 1) * half], right_ref[...], 1, 1).astype(BF16)
 
 
 def fold_body(nx, nz, got_ref, out_ref):
@@ -253,7 +263,14 @@
             lambda *refs: pick_body(nx, nz, *refs),
             [shape((CORES * nz, own, nx * depth), BF16)],
             (seq_index.reshape(1), span_start, span_end, states[0]),
+            scratch=(
+                pltpu.VMEM(span_start.shape, jnp.int32),
+                pltpu.VMEM(span_end.shape, jnp.int32),
+                pltpu.VMEM(states.shape[1:], BF16),
+                pltpu.SemaphoreType.DMA((3,)),
+            ),
             smem=(0,),
+            hbm=(1, 2, 3),
         )
         pieces = exchange(picked, ("core", "z"))
         all_pieces = lax.all_gather(pieces, "y", axis=0)
@@ -266,34 +283,35 @@
         )
         pre_got = exchange(pre_parts, ("core", "z"))
 
-        tags = jnp.concatenate([gold, live], axis=0).astype(F32)
-        tags = lax.dynamic_update_slice(jnp.zeros((TAGS, group), F32), tags, (0, z_index * own))
+        tags = jnp.concatenate([gold, live], axis=0).astype(F32)[None]
+        tags = lax.dynamic_update_slice(
+            jnp.zeros((nx, 8, group), F32), tags, (x_index, 0, z_index * own)
+        )
         pre, left_own, right_pay = call(
             lambda *refs: act_body(nx, nz, *refs),
             [
                 shape((2, rows, group), F32),
                 shape((rows, group), BF16),
-                shape((nz, rows + TAGS, group), BF16),
+                shape((nz, rows, group), BF16),
             ],
-            (pre_got, tags),
+            (pre_got,),
         )
         right_column = exchange(right_pay, "z")
         (act_pay,) = call(
             lambda *refs: spread_body(nx, nz, inner, *refs),
-            [shape((nx, full + inner + TAGS, group), BF16)],
+            [shape((nx, full + inner, group), BF16)],
             (left_own, right_column),
         )
         act_got = exchange(act_pay, "x")
 
-        score_parts, left, right, all_tags = call(
+        score_parts, left, right = call(
             lambda *refs: score_body(nx, nz, inner, *refs),
             [
                 shape((nx * nz, 8, group), F32),
                 shape((inner, spans), F32),
                 shape((full, spans), BF16),
-                shape((TAGS, spans), F32),
             ],
-            (biaffine, act_got),
+            (biaffine, act_got, tags),
             flops=2 * labels * inner * full * spans,
         )
         score_got = exchange(score_parts, ("x", "z"))
@@ -307,20 +325,22 @@
                 shape((labels * inner, spans), BF16),
                 shape((1, spans), F32),
             ],
-            (biaffine, left, right, all_tags, scores),
+            (biaffine, left, right, scores),
             scratch=(pltpu.VMEM((labels, spans), F32),),
             flops=4 * labels * inner * full * spans,
         )
         span_loss = lax.dynamic_slice_in_dim(loss, seq_index * own, own, 1)
-        (flat,) = call(
+        halves = call(
             flat_body,
-            [shape((labels * inner, full), BF16)],
+            [shape((labels * inner // 2, full), BF16)] * 2,
             (outer, right),
             flops=2 * labels * inner * full * spans,
         )
-        grad_biaffine = lax.psum(flat, ("y", "core")).reshape(labels, inner, full)
-
-        grad_got = exchange(grad_pay, "x")
+        grad_got, _ = lax.optimization_barrier((exchange(grad_pay, "x"), halves))
+        grad_biaffine = jnp.concatenate(
+            [lax.psum(half, axes) for half, axes in zip(halves, (("y", "core"), ("core", "y")))],
+            axis=0,
+        ).reshape(labels, inner, full)
         (fold_pay,) = call(
             lambda *refs: fold_body(nx, nz, *refs),
             [shape((nz, rows, group), BF16)],

time: 270 us -> 323 us (1.20)
  waiting for transfers between devices: 87.5 us -> 154 us
  blocking collectives: 99.5 us -> 80 us
  other arithmetic: 1.79 us -> 5.64 us
    psum x1 -> x2, waiting for transfers between devices: 33.2 us -> 93.3 us  [shards(): lax.psum(half, axes)]
    all_to_all x7 -> x5, blocking collectives: 99.5 us -> 80 us  [exchange(): return lax.all_to_all(parts, axes, split_axis=0, concat_axis=0, tiled=True)]
    all_to_all x4 -> x6, waiting for transfers between devices: 46.7 us -> 51.7 us  [exchange(): return lax.all_to_all(parts, axes, split_axis=0, concat_axis=0, tiled=True)]
    concatenate x0 -> x1, other arithmetic: none -> 3.85 us  [shards(): jnp.concatenate([lax.psum(half, axes) for half, axes in zip(halves, (('y'...]
    all_to_all x4 -> x6, starting transfers between devices: 31.5 us -> 33.8 us  [exchange(): return lax.all_to_all(parts, axes, split_axis=0, concat_axis=0, tiled=True)]
    unnamed x25 -> x24, local copies, waits for them, and re-layouts: 12 us -> 12 us
  transfers between devices with their start and end apart: 7 -> 10, of which waited for: 6 -> 8; matrix products, arithmetic and copies ran while one was open for 0% -> 1% of each run, Pallas kernels for 5% -> 4%
where the time goes in v4:
time: 323 us; the launch traced here: 321 us
  waiting for transfers between devices  154 us (48%)
  blocking collectives  80 us (25%)
  starting transfers between devices  33.9 us (10%)
  Pallas kernels  19.8 us (6%)
  between operations  15.4 us (5%)
  local copies, waits for them, and re-layouts  12.9 us (4%)
  other arithmetic  5.64 us (2%)
    psum x2, waiting for transfers between devices, shards(): lax.psum(half, axes)  93.3 us
    all_to_all x5, blocking collectives, exchange(): return lax.all_to_all(parts, axes, split_axis=0, concat_axis=0, tiled=True)  80 us
    all_to_all x6, waiting for transfers between devices, exchange(): return lax.all_to_all(parts, axes, split_axis=0, concat_axis=0, tiled=True)  51.7 us
    all_to_all x6, starting transfers between devices, exchange(): return lax.all_to_all(parts, axes, split_axis=0, concat_axis=0, tiled=True)  33.8 us
    pallas_call x12, Pallas kernels, call(): pl.pallas_call(body, out_shape=tuple(outs), in_specs=specs, out_specs=tup...  19.8 us
    unnamed x24, local copies, waits for them, and re-layouts  12 us
    all_gather x1, waiting for transfers between devices, shards(): weights = lax.all_gather(side_proj, 'x', axis=0)  6.77 us
  transfers between devices with their start and end apart: 10, of which 8 were waited for; matrix products, arithmetic and copies ran while one was open for 1% of the time, Pallas kernels for 4%

profile of v4, /device:TPU:1, one launch (start us, length us, event | category | flops | bytes accessed | tf_op | source)
XLA Modules:
  0.0 321.3 jit_solution(11279377963202042567)
XLA Ops:
  8.1 1.7 broadcast_select_fusion
  9.8 1.7 copy-done.1
  14.0 20.5 %all_to_all.55.refs_1_ = bf16[16,16,640]{2,1,0:T(8,128)(2,1)S(1)} all-to-all(bf16[16,16,640]{2,1,0:T(8,128)(2,1)S(1)} %shard_map.111), channel_id=1, replica_groups=mesh['y'=4,'core'=2,'x'=4,'z'=8] {'core','z'}, dimensions={0} | all-to-all | bytes 655360 | tf_op jit(solution)/shard_map/all_to_all | solution.py:16
  34.5 6.8 %all-gather.5.cloned.1.call-done = bf16[640,1024]{1,0:T(8,128)(2,1)} async-done(((bf16[160,1024]{1,0:T(8,128)(2,1)}), bf16[640,1024]{1,0:T(8,128)(2,1)}) %all-gather.5.cloned.1.call-update) | async-done | bytes 1310736 | tf_op jit(solution)/shard_map/all_gather | solution.py:260
  41.3 1.3 copy-done.3
  43.3 23.4 %all_to_all.56.refs_0_ = bf16[16,128,128]{2,1,0:T(8,128)(2,1)S(1)} all-to-all(bf16[16,128,128]{2,1,0:T(8,128)(2,1)S(1)} %shard_map.112), channel_id=1, replica_groups=mesh['y'=4,'core'=2,'x'=4,'z'=8] {'core','z'}, dimensions={0} | all-to-all | bytes 1048576 | tf_op jit(solution)/shard_map/all_to_all | solution.py:16
  66.8 15.2 %all_to_all.57.refs_1_ = bf16[8,128,128]{2,1,0:T(8,128)(2,1)S(1)} all-to-all(bf16[8,128,128]{2,1,0:T(8,128)(2,1)S(1)} %get-tuple-element.19), channel_id=1, replica_groups=mesh['y'=4,'core'=2,'x'=4,'z'=8] {'z'}, dimensions={0} | all-to-all | bytes 524288 | tf_op jit(solution)/shard_map/all_to_all | solution.py:16
  82.0 1.1 shard_map.114
  83.1 3.5 %all-to-all-start.3 = ((bf16[4,1056,128]{2,1,0:T(8,128)(2,1)}), bf16[4,1056,128]{2,1,0:T(8,128)(2,1)S(1)}, u32[]{:S(2)}, u32[]{:S(2)}) async-start(bf16[4,1056,128]{2,1,0:T(8,128)(2,1)} %shard_map.114), calls=%async_computation.3 | async-start | bytes 2162688 | tf_op jit(solution)/shard_map/all_to_all | solution.py:16
  87.0 12.8 %all-to-all-done.3.refs_1_ = bf16[4,1056,128]{2,1,0:T(8,128)(2,1)S(1)} async-done(((bf16[4,1056,128]{2,1,0:T(8,128)(2,1)}), bf16[4,1056,128]{2,1,0:T(8,128)(2,1)S(1)}, u32[]{:S(2)}, u32[]{:S(2)}) %all-to-all-start.3) | async-done | bytes 1081376 | tf_op jit(solution)/shard_map/all_to_all | solution.py:16
  99.9 1.9 copy-done.6
  101.8 3.5 %shard_map.115 = (f32[32,8,128]{2,1,0:T(8,128)}, f32[32,512]{1,0:T(8,128)S(1)}, bf16[1024,512]{1,0:T(8,128)(2,1)S(1)}) custom-call(bf16[48,32,1024]{2,1,0:T(8,128)(2,1)S(1)} %copy-done.6, bf16[4,1056,128]{2,1,0:T(8,128)(2,1)S(1)} %all-to-all-done.3.refs_1_, f32[4,8,128]{2,1,0:T(8,128)S(1)} %dynamic_update_slice.3.refs_2_), custom_call_target="tpu_custom_call" | custom-call | flops 1610612736 | bytes 5488640 | tf_op jit(solution)/shard_map/pallas_call | solution.py:28
  105.3 4.4 %all-to-all-start.4 = ((f32[32,8,128]{2,1,0:T(8,128)}), f32[32,8,128]{2,1,0:T(8,128)S(1)}, u32[]{:S(2)}, u32[]{:S(2)}) async-start(f32[32,8,128]{2,1,0:T(8,128)} %get-tuple-element.22), calls=%async_computation.4 | async-start | bytes 262144 | tf_op jit(solution)/shard_map/all_to_all | solution.py:16
  110.2 8.7 %all-to-all-done.4 = f32[32,8,128]{2,1,0:T(8,128)S(1)} async-done(((f32[32,8,128]{2,1,0:T(8,128)}), f32[32,8,128]{2,1,0:T(8,128)S(1)}, u32[]{:S(2)}, u32[]{:S(2)}) %all-to-all-start.4) | async-done | bytes 131104 | tf_op jit(solution)/shard_map/all_to_all | solution.py:16
  119.0 12.6 %all_to_all.58.refs_3_ = f32[32,8,128]{2,1,0:T(8,128)S(1)} all-to-all(f32[32,8,128]{2,1,0:T(8,128)S(1)} %broadcast_in_dim.5), channel_id=1, replica_groups=mesh['y'=4,'core'=2,'x'=4,'z'=8] {'x','z'}, dimensions={0} | all-to-all | bytes 262144 | tf_op jit(solution)/shard_map/all_to_all | solution.py:16
  131.6 1.9 copy-done.7
  133.5 5.6 %shard_map.116 = (bf16[4,1056,128]{2,1,0:T(8,128)(2,1)}, bf16[1536,512]{1,0:T(8,128)(2,1)S(1)}, f32[1,512]{1,0:T(1,128)S(1)}) custom-call(bf16[48,32,1024]{2,1,0:T(8,128)(2,1)S(1)} %copy-done.7, f32[32,512]{1,0:T(8,128)S(1)} %get-tuple-element.20.refs_1_, bf16[1024,512]{1,0:T(8,128)(2,1)S(1)} %get-tuple-element.21.refs_2_.right_ref, ...), custom_call_target="tpu_custom_call" | custom-call | flops 3221225472 | bytes 7047168 | tf_op jit(solution)/shard_map/pallas_call | solution.py:28
  139.1 1.1 copy-done.8
  140.2 3.5 %all-to-all-start.6 = ((bf16[4,1056,128]{2,1,0:T(8,128)(2,1)}), bf16[4,1056,128]{2,1,0:T(8,128)(2,1)S(1)}, u32[]{:S(2)}, u32[]{:S(2)}) async-start(bf16[4,1056,128]{2,1,0:T(8,128)(2,1)} %get-tuple-element.25), calls=%async_computation.6 | async-start | bytes 2162688 | tf_op jit(solution)/shard_map/all_to_all | solution.py:16
  143.8 1.4 copy-done.9
  145.2 3.4 %shard_map.117 = (bf16[768,1024]{1,0:T(8,128)(2,1)}, bf16[768,1024]{1,0:T(8,128)(2,1)}) custom-call(bf16[1536,512]{1,0:T(8,128)(2,1)S(1)} %copy-done.9, bf16[1024,512]{1,0:T(8,128)(2,1)S(1)} %get-tuple-element.21.refs_2_.right_ref), custom_call_target="tpu_custom_call" | custom-call | flops 1610612736 | bytes 5767168 | tf_op jit(solution)/shard_map/pallas_call | solution.py:28
  148.6 5.4 %all-to-all-done.6.refs_0_.refs_1_ = bf16[4,1056,128]{2,1,0:T(8,128)(2,1)S(1)} async-done(((bf16[4,1056,128]{2,1,0:T(8,128)(2,1)}), bf16[4,1056,128]{2,1,0:T(8,128)(2,1)S(1)}, u32[]{:S(2)}, u32[]{:S(2)}) %all-to-all-start.6) | async-done | bytes 1081376 | tf_op jit(solution)/shard_map/all_to_all | solution.py:16
  154.8 3.4 %all-to-all-start.7 = ((bf16[8,128,128]{2,1,0:T(8,128)(2,1)}), bf16[8,128,128]{2,1,0:T(8,128)(2,1)S(1)}, u32[]{:S(2)}, u32[]{:S(2)}) async-start(bf16[8,128,128]{2,1,0:T(8,128)(2,1)} %shard_map.118), calls=%async_computation.7 | async-start | bytes 524288 | tf_op jit(solution)/shard_map/all_to_all | solution.py:16
  159.0 8.5 %all-to-all-done.7.refs_2_ = bf16[8,128,128]{2,1,0:T(8,128)(2,1)S(1)} async-done(((bf16[8,128,128]{2,1,0:T(8,128)(2,1)}), bf16[8,128,128]{2,1,0:T(8,128)(2,1)S(1)}, u32[]{:S(2)}, u32[]{:S(2)}) %all-to-all-start.7) | async-done | bytes 262176 | tf_op jit(solution)/shard_map/all_to_all | solution.py:16
  168.4 12.2 %all-to-all-start.8 = ((bf16[64,32,128]{2,1,0:T(8,128)(2,1)}), bf16[64,32,128]{2,1,0:T(8,128)(2,1)S(1)}, u32[]{:S(2)}, u32[]{:S(2)}) async-start(bf16[64,32,128]{2,1,0:T(8,128)(2,1)} %shard_map.119), calls=%async_computation.8 | async-start | bytes 1048576 | tf_op jit(solution)/shard_map/all_to_all | solution.py:16
  181.4 16.3 %all-to-all-done.8.refs_0_ = bf16[64,32,128]{2,1,0:T(8,128)(2,1)S(1)} async-done(((bf16[64,32,128]{2,1,0:T(8,128)(2,1)}), bf16[64,32,128]{2,1,0:T(8,128)(2,1)S(1)}, u32[]{:S(2)}, u32[]{:S(2)}) %all-to-all-start.8) | async-done | bytes 524320 | tf_op jit(solution)/shard_map/all_to_all | solution.py:16
  197.8 1.3 copy-done.2
  199.7 8.3 %all_to_all.59.got_ref = bf16[4,160,256]{2,1,0:T(8,128)(2,1)S(1)} all-to-all(bf16[4,160,256]{2,1,0:T(8,128)(2,1)S(1)} %shard_map.120), channel_id=1, replica_groups=mesh['y'=4,'core'=2,'x'=4,'z'=8] {'x'}, dimensions={0} | all-to-all | bytes 655360 | tf_op jit(solution)/shard_map/all_to_all | solution.py:16
  208.9 6.7 %all-to-all-start.10 = ((bf16[8,160,256]{2,1,0:T(8,128)(2,1)}), bf16[8,160,256]{2,1,0:T(8,128)(2,1)S(1)}, u32[]{:S(2)}, u32[]{:S(2)}) async-start(bf16[8,160,256]{2,1,0:T(8,128)(2,1)} %shard_map.121), calls=%async_computation.10 | async-start | bytes 1310720 | tf_op jit(solution)/shard_map/all_to_all | solution.py:16
  216.1 23.7 %all-reduce.5.cloned.1.call-done = bf16[768,1024]{1,0:T(8,128)(2,1)} async-done(((bf16[768,1024]{1,0:T(8,128)(2,1)}), bf16[768,1024]{1,0:T(8,128)(2,1)}) %all-reduce.5.cloned.1.call-update) | async-done | bytes 1572880 | tf_op jit(solution)/shard_map/psum | solution.py:341
  239.8 69.6 %all-reduce.3.cloned.1.call-done = bf16[768,1024]{1,0:T(8,128)(2,1)} async-done(((bf16[768,1024]{1,0:T(8,128)(2,1)}), bf16[768,1024]{1,0:T(8,128)(2,1)}) %all-reduce.3.cloned.1.call-update) | async-done | bytes 1572880 | tf_op jit(solution)/shard_map/psum | solution.py:341
  309.4 3.9 %pad_maximum_fusion = bf16[1536,1024]{1,0:T(8,128)(2,1)} fusion(bf16[768,1024]{1,0:T(8,128)(2,1)} %all-reduce.5.cloned.1.call-done, bf16[768,1024]{1,0:T(8,128)(2,1)} %all-reduce.3.cloned.1.call-done), kind=kLoop, calls=%fused_computation | loop fusion | flops 6291456 | bytes 6291456 | tf_op jit(solution)/shard_map/concatenate | solution.py:340
  (41 shorter events, 10.5 us)
Async XLA Ops:
  8.0 33.3 %all-gather.5.cloned.1.call-start = ((), (), s32[]{:S(2)}) async-start(), calls=%async_computation.13 | async-start | bytes 1638400 | tf_op jit(solution)/shard_map/all_gather | solution.py:260
  9.8 1.7 copy-start.1
  11.6 0.7 copy-start.4
  12.2 0.7 copy-start.5
  34.5 32.2 %copy-start = (bf16[16,16,640]{2,1,0:T(8,128)(2,1)}, bf16[16,16,640]{2,1,0:T(8,128)(2,1)S(1)}, u32[]{:S(2)}) copy-start(bf16[16,16,640]{2,1,0:T(8,128)(2,1)S(1)} %all_to_all.55.refs_1_) | copy-start | bytes 983044
  41.3 1.3 copy-start.3
  82.0 4.7 %copy-start.10 = (s32[1,16]{1,0:T(1,128)S(1)}, s32[1,16]{1,0:T(1,128)}, u32[]{:S(2)}) copy-start(s32[1,16]{1,0:T(1,128)} %param.12) | copy-start | bytes 196
  82.0 4.7 %copy-start.11 = (s32[1,16]{1,0:T(1,128)S(1)}, s32[1,16]{1,0:T(1,128)}, u32[]{:S(2)}) copy-start(s32[1,16]{1,0:T(1,128)} %param.11) | copy-start | bytes 196
  83.1 16.8 %all-to-all-start.3 = ((bf16[4,1056,128]{2,1,0:T(8,128)(2,1)}), bf16[4,1056,128]{2,1,0:T(8,128)(2,1)S(1)}, u32[]{:S(2)}, u32[]{:S(2)}) async-start(bf16[4,1056,128]{2,1,0:T(8,128)(2,1)} %shard_map.114), calls=%async_computation.3 | async-start | bytes 2162688 | tf_op jit(solution)/shard_map/all_to_all | solution.py:16
  99.9 1.9 copy-start.6
  105.3 13.6 %all-to-all-start.4 = ((f32[32,8,128]{2,1,0:T(8,128)}), f32[32,8,128]{2,1,0:T(8,128)S(1)}, u32[]{:S(2)}, u32[]{:S(2)}) async-start(f32[32,8,128]{2,1,0:T(8,128)} %get-tuple-element.22), calls=%async_computation.4 | async-start | bytes 262144 | tf_op jit(solution)/shard_map/all_to_all | solution.py:16
  109.7 71.7 %all-gather.7.cloned.1.call-start = ((), (), s32[]{:S(2)}) async-start(), calls=%async_computation.14 | async-start | bytes 1638400 | tf_op jit(solution)/shard_map/all_gather | solution.py:276
  131.6 1.9 copy-start.7
  139.1 1.1 copy-start.8
  140.2 13.7 %all-to-all-start.6 = ((bf16[4,1056,128]{2,1,0:T(8,128)(2,1)}), bf16[4,1056,128]{2,1,0:T(8,128)(2,1)S(1)}, u32[]{:S(2)}, u32[]{:S(2)}) async-start(bf16[4,1056,128]{2,1,0:T(8,128)(2,1)} %get-tuple-element.25), calls=%async_computation.6 | async-start | bytes 2162688 | tf_op jit(solution)/shard_map/all_to_all | solution.py:16
  143.8 1.4 copy-start.9
  154.8 12.7 %all-to-all-start.7 = ((bf16[8,128,128]{2,1,0:T(8,128)(2,1)}), bf16[8,128,128]{2,1,0:T(8,128)(2,1)S(1)}, u32[]{:S(2)}, u32[]{:S(2)}) async-start(bf16[8,128,128]{2,1,0:T(8,128)(2,1)} %shard_map.118), calls=%async_computation.7 | async-start | bytes 524288 | tf_op jit(solution)/shard_map/all_to_all | solution.py:16
  158.2 81.6 %all-reduce.5.cloned.1.call-start = ((), (), s32[]{:S(2)}) async-start(), calls=%async_computation.12 | async-start | bytes 3145728 | tf_op jit(solution)/shard_map/psum | solution.py:341
  168.4 29.3 %all-to-all-start.8 = ((bf16[64,32,128]{2,1,0:T(8,128)(2,1)}), bf16[64,32,128]{2,1,0:T(8,128)(2,1)S(1)}, u32[]{:S(2)}, u32[]{:S(2)}) async-start(bf16[64,32,128]{2,1,0:T(8,128)(2,1)} %shard_map.119), calls=%async_computation.8 | async-start | bytes 1048576 | tf_op jit(solution)/shard_map/all_to_all | solution.py:16
  180.7 128.8 %all-reduce.3.cloned.1.call-start = ((), (), s32[]{:S(2)}) async-start(), calls=%async_computation.11 | async-start | bytes 3145728 | tf_op jit(solution)/shard_map/psum | solution.py:341
  197.8 1.3 copy-start.2
  208.9 104.4 %all-to-all-start.10 = ((bf16[8,160,256]{2,1,0:T(8,128)(2,1)}), bf16[8,160,256]{2,1,0:T(8,128)(2,1)S(1)}, u32[]{:S(2)}, u32[]{:S(2)}) async-start(bf16[8,160,256]{2,1,0:T(8,128)(2,1)} %shard_map.121), calls=%async_computation.10 | async-start | bytes 1310720 | tf_op jit(solution)/shard_map/all_to_all | solution.py:16
Sparse Core Ops, SparseCore 0:
  11.2 30.0 all-gather.4
  161.4 78.3 all-reduce.4
  242.8 66.5 all-reduce.2
Sparse Core Ops, SparseCore 1:
  112.5 29.3 all-gather.6

commit v5 on v4

--- a/solution.py
+++ b/solution.py
@@ -16,13 +16,11 @@
     return lax.all_to_all(parts, axes, split_axis=0, concat_axis=0, tiled=True)
 
 
-def call(body, outs, args, scratch=(), smem=(), hbm=(), flops=0, room=16):
+def call(body, outs, args, scratch=(), smem=(), flops=0, room=16):
     moved = sum(a.size * a.dtype.itemsize for a in args)
     moved += sum(o.size * jnp.dtype(o.dtype).itemsize for o in outs)
     specs = [
-        pl.BlockSpec(
-            memory_space=pltpu.SMEM if i in smem else pltpu.HBM if i in hbm else pltpu.VMEM
-        )
+        pl.BlockSpec(memory_space=pltpu.SMEM if i in smem else pltpu.VMEM)
         for i in range(len(args))
     ]
     got = pl.pallas_call(
@@ -41,25 +39,14 @@
     return lax.dot_general(a, b, (((da,), (db,)), ((), ())), preferred_element_type=F32)
 
 
-def pick_body(
-    nx, nz, seq_ref, start_hbm, end_hbm, states_hbm, out_ref, start_ref, end_ref, states_ref, sems
-):
+def pick_body(nx, nz, seq_ref, ends_ref, states_ref, out_ref):
     tokens, width = states_ref.shape
     half = tokens // 2
     depth = width // (nx * nz)
-    own = start_ref.shape[1]
-    copies = [
-        pltpu.make_async_copy(states_hbm, states_ref, sems.at[0]),
-        pltpu.make_async_copy(start_hbm, start_ref, sems.at[1]),
-        pltpu.make_async_copy(end_hbm, end_ref, sems.at[2]),
-    ]
-    for copy in copies:
-        copy.start()
-    for copy in copies[1:] + copies[:1]:
-        copy.wait()
+    own = ends_ref.shape[1]
     states = states_ref[...]
-    for side, ref in enumerate((start_ref, end_ref)):
-        token = ref[...]
+    for side in range(CORES):
+        token = ends_ref[side : side + 1, :]
         inside = lax.rem(token, half)
         low = (token - inside) == seq_ref[0] * half
         picks = inside + jnp.where(low, 0, half)
@@ -136,13 +123,8 @@
     lax.fori_loop(0, labels // 8, step, 0)
 
 
-def slope_body(
-    nx, nz, inner, own, weight_ref, left_ref, right_ref, score_ref,
-    out_ref, outer_ref, loss_ref, slope_ref,
-):
-    labels, _, full = weight_ref.shape
-    group = score_ref.shape[2]
-    spans = nx * group
+def slope_body(nx, nz, inner, own, labels, left_ref, score_ref, outer_ref, loss_ref, slope_ref):
+    spans = left_ref.shape[1]
     scores = jnp.concatenate(
         [
             jnp.concatenate([score_ref[x * nz + b] for x in range(nx)], axis=1)
@@ -161,12 +143,24 @@
     slope = live * (jnp.exp(scores - log_total) - onehot) / own
     slope_ref[...] = slope.astype(BF16).astype(F32)
 
+    def step(lb, carry):
+        slope = slope_ref[pl.ds(lb * 8, 8), :]
+        outer = (slope[:, None, :] * left_ref[...][None]).astype(BF16)
+        outer_ref[pl.ds(lb * 8 * inner, 8 * inner), :] = outer.reshape(8 * inner, spans)
+        return carry
+
+    lax.fori_loop(0, labels // 8, step, 0)
+
+
+def back_body(nx, nz, inner, weight_ref, right_ref, slope_ref, outer_ref, out_ref):
+    labels, _, full = weight_ref.shape
+    group = out_ref.shape[2]
+    spans = nx * group
+
     def step(lb, left_sum):
         slope = slope_ref[pl.ds(lb * 8, 8), :]
         weight = weight_ref[pl.ds(lb * 8, 8)].reshape(8 * inner, full)
         image = dot(weight, right_ref[...], 1, 0).reshape(8, inner, spans)
-        outer = (slope[:, None, :] * left_ref[...][None]).astype(BF16)
-        outer_ref[pl.ds(lb * 8 * inner, 8 * inner), :] = outer.reshape(8 * inner, spans)
         return left_sum + jnp.sum(image * slope[:, None, :], axis=0)
 
     left_sum = lax.fori_loop(0, labels // 8, step, jnp.zeros((inner, spans), F32)).astype(BF16)
@@ -182,10 +176,12 @@
         out_ref[to, full : full + inner, :] = left_sum[:, lanes]
 
 
-def flat_body(outer_ref, right_ref, *outs):
-    half = outs[0].shape[0]
-    for i, out_ref in enumerate(outs):
-        out_ref[...] = dot(outer_ref[i * half : (i + 1) * half], right_ref[...], 1, 1).astype(BF16)
+def flat_body(outer_ref, right_ref, out_ref):
+    out_ref[...] = dot(outer_ref[...], right_ref[...], 1, 1)
+
+
+def round_body(wide_ref, out_ref):
+    out_ref[...] = wide_ref[...].astype(BF16)
 
 
 def fold_body(nx, nz, got_ref, out_ref):
@@ -262,15 +258,8 @@
         (picked,) = call(
             lambda *refs: pick_body(nx, nz, *refs),
             [shape((CORES * nz, own, nx * depth), BF16)],
-            (seq_index.reshape(1), span_start, span_end, states[0]),
-            scratch=(
-                pltpu.VMEM(span_start.shape, jnp.int32),
-                pltpu.VMEM(span_end.shape, jnp.int32),
-                pltpu.VMEM(states.shape[1:], BF16),
-                pltpu.SemaphoreType.DMA((3,)),
-            ),
+            (seq_index.reshape(1), jnp.concatenate([span_start, span_end], axis=0), states[0]),
             smem=(0,),
-            hbm=(1, 2, 3),
         )
         pieces = exchange(picked, ("core", "z"))
         all_pieces = lax.all_gather(pieces, "y", axis=0)
@@ -318,29 +307,37 @@
         score_sum = jnp.sum(score_got, axis=0)
         scores = exchange(jnp.broadcast_to(score_sum[None], score_got.shape), ("x", "z"))
 
-        grad_pay, outer, loss = call(
-            lambda *refs: slope_body(nx, nz, inner, own, *refs),
+        outer, loss, slope = call(
+            lambda *refs: slope_body(nx, nz, inner, own, labels, *refs),
             [
-                shape((nx, full + inner, group), BF16),
                 shape((labels * inner, spans), BF16),
                 shape((1, spans), F32),
+                shape((labels, spans), F32),
             ],
-            (biaffine, left, right, scores),
-            scratch=(pltpu.VMEM((labels, spans), F32),),
-            flops=4 * labels * inner * full * spans,
+            (left, scores),
         )
         span_loss = lax.dynamic_slice_in_dim(loss, seq_index * own, own, 1)
-        halves = call(
+        (flat,) = call(
             flat_body,
-            [shape((labels * inner // 2, full), BF16)] * 2,
+            [shape((labels * inner, full), F32)],
             (outer, right),
             flops=2 * labels * inner * full * spans,
         )
-        grad_got, _ = lax.optimization_barrier((exchange(grad_pay, "x"), halves))
-        grad_biaffine = jnp.concatenate(
-            [lax.psum(half, axes) for half, axes in zip(halves, (("y", "core"), ("core", "y")))],
-            axis=0,
-        ).reshape(labels, inner, full)
+        flat, slope = lax.optimization_barrier((flat, slope))
+        (grad_pay,) = call(
+            lambda *refs: back_body(nx, nz, inner, *refs),
+            [shape((nx, full + inner, group), BF16)],
+            (biaffine, right, slope, outer),
+            flops=4 * labels * inner * full * spans,
+        )
+        grad_got = exchange(grad_pay, "x")
+        (grad_biaffine,) = call(
+            round_body,
+            [shape((labels * inner, full), BF16)],
+            (lax.psum(flat, ("y", "core")),),
+            room=32,
+        )
+        grad_biaffine = grad_biaffine.reshape(labels, inner, full)
         (fold_pay,) = call(
             lambda *refs: fold_body(nx, nz, *refs),
             [shape((nz, rows, group), BF16)],

time: 323 us -> 267 us (0.83)
  waiting for transfers between devices: 154 us -> 93.4 us
  blocking collectives: 80 us -> 90.1 us
  starting transfers between devices: 33.9 us -> 30.5 us
    psum x2 -> x1, waiting for transfers between devices: 93.3 us -> 20.8 us  [shards(): lax.psum(flat, ('y', 'core'))]
    all_to_all x6 -> x5, waiting for transfers between devices: 51.7 us -> 63.7 us  [exchange(): return lax.all_to_all(parts, axes, split_axis=0, concat_axis=0, tiled=True)]
    all_to_all x5 -> x6, blocking collectives: 80 us -> 90.1 us  [exchange(): return lax.all_to_all(parts, axes, split_axis=0, concat_axis=0, tiled=True)]
    all_to_all x6 -> x5, starting transfers between devices: 33.8 us -> 30.4 us  [exchange(): return lax.all_to_all(parts, axes, split_axis=0, concat_axis=0, tiled=True)]
    unnamed x24 -> x20, local copies, waits for them, and re-layouts: 12 us -> 13.6 us
    pallas_call x12 -> x14, Pallas kernels: 19.8 us -> 19.3 us  [call(): pl.pallas_call(body, out_shape=tuple(outs), in_specs=specs, out_specs=tup...]
  transfers between devices with their start and end apart: 10 -> 8, of which waited for: 8 -> 7; matrix products, arithmetic and copies ran while one was open for 1% -> 1% of each run, Pallas kernels for 4% -> 6%
where the time goes in v5:
time: 267 us; the launch traced here: 266 us
  waiting for transfers between devices  93.4 us (35%)
  blocking collectives  90.1 us (34%)
  starting transfers between devices  30.5 us (11%)
  Pallas kernels  19.3 us (7%)
  between operations  15.6 us (6%)
  local copies, waits for them, and re-layouts  14.5 us (5%)
    all_to_all x6, blocking collectives, exchange(): return lax.all_to_all(parts, axes, split_axis=0, concat_axis=0, tiled=True)  90.1 us
    all_to_all x5, waiting for transfers between devices, exchange(): return lax.all_to_all(parts, axes, split_axis=0, concat_axis=0, tiled=True)  63.7 us
    all_to_all x5, starting transfers between devices, exchange(): return lax.all_to_all(parts, axes, split_axis=0, concat_axis=0, tiled=True)  30.4 us
    psum x1, waiting for transfers between devices, shards(): lax.psum(flat, ('y', 'core'))  20.8 us
    pallas_call x14, Pallas kernels, call(): pl.pallas_call(body, out_shape=tuple(outs), in_specs=specs, out_specs=tup...  19.3 us
    unnamed x20, local copies, waits for them, and re-layouts  13.6 us
    all_gather x1, waiting for transfers between devices, shards(): weights = lax.all_gather(side_proj, 'x', axis=0)  7.61 us
  transfers between devices with their start and end apart: 8, of which 7 were waited for; matrix products, arithmetic and copies ran while one was open for 1% of the time, Pallas kernels for 6%

profile of v5, /device:TPU:1, one launch (start us, length us, event | category | flops | bytes accessed | tf_op | source)
XLA Modules:
  0.0 265.8 jit_solution(5279116079870624095)
XLA Ops:
  8.1 1.7 broadcast_select_fusion
  10.5 1.7 copy-done.3
  13.2 20.5 %all_to_all.55.refs_1_ = bf16[16,16,640]{2,1,0:T(8,128)(2,1)S(1)} all-to-all(bf16[16,16,640]{2,1,0:T(8,128)(2,1)S(1)} %shard_map.111), channel_id=1, replica_groups=mesh['y'=4,'core'=2,'x'=4,'z'=8] {'core','z'}, dimensions={0} | all-to-all | bytes 655360 | tf_op jit(solution)/shard_map/all_to_all | solution.py:16
  33.7 7.6 %all-gather.5.cloned.1.call-done = bf16[640,1024]{1,0:T(8,128)(2,1)} async-done(((bf16[160,1024]{1,0:T(8,128)(2,1)}), bf16[640,1024]{1,0:T(8,128)(2,1)}) %all-gather.5.cloned.1.call-update) | async-done | bytes 1310736 | tf_op jit(solution)/shard_map/all_gather | solution.py:256
  41.3 1.3 copy-done.5
  43.3 23.4 %all_to_all.56.refs_0_ = bf16[16,128,128]{2,1,0:T(8,128)(2,1)S(1)} all-to-all(bf16[16,128,128]{2,1,0:T(8,128)(2,1)S(1)} %shard_map.112), channel_id=1, replica_groups=mesh['y'=4,'core'=2,'x'=4,'z'=8] {'core','z'}, dimensions={0} | all-to-all | bytes 1048576 | tf_op jit(solution)/shard_map/all_to_all | solution.py:16
  67.5 4.7 %all-to-all-start.2 = ((bf16[8,128,128]{2,1,0:T(8,128)(2,1)}), bf16[8,128,128]{2,1,0:T(8,128)(2,1)S(1)}, u32[]{:S(2)}, u32[]{:S(2)}) async-start(bf16[8,128,128]{2,1,0:T(8,128)(2,1)} %get-tuple-element.18), calls=%async_computation.2 | async-start | bytes 524288 | tf_op jit(solution)/shard_map/all_to_all | solution.py:16
  72.7 10.1 %all-to-all-done.2.refs_1_ = bf16[8,128,128]{2,1,0:T(8,128)(2,1)S(1)} async-done(((bf16[8,128,128]{2,1,0:T(8,128)(2,1)}), bf16[8,128,128]{2,1,0:T(8,128)(2,1)S(1)}, u32[]{:S(2)}, u32[]{:S(2)}) %all-to-all-start.2) | async-done | bytes 262176 | tf_op jit(solution)/shard_map/all_to_all | solution.py:16
  82.8 1.1 shard_map.114
  84.0 3.5 %all-to-all-start.3 = ((bf16[4,1056,128]{2,1,0:T(8,128)(2,1)}), bf16[4,1056,128]{2,1,0:T(8,128)(2,1)S(1)}, u32[]{:S(2)}, u32[]{:S(2)}) async-start(bf16[4,1056,128]{2,1,0:T(8,128)(2,1)} %shard_map.114), calls=%async_computation.3 | async-start | bytes 2162688 | tf_op jit(solution)/shard_map/all_to_all | solution.py:16
  87.9 12.8 %all-to-all-done.3.refs_1_ = bf16[4,1056,128]{2,1,0:T(8,128)(2,1)S(1)} async-done(((bf16[4,1056,128]{2,1,0:T(8,128)(2,1)}), bf16[4,1056,128]{2,1,0:T(8,128)(2,1)S(1)}, u32[]{:S(2)}, u32[]{:S(2)}) %all-to-all-start.3) | async-done | bytes 1081376 | tf_op jit(solution)/shard_map/all_to_all | solution.py:16
  100.7 1.9 copy-done.6
  102.6 2.9 %shard_map.115 = (f32[32,8,128]{2,1,0:T(8,128)S(1)}, f32[32,512]{1,0:T(8,128)S(1)}, bf16[1024,512]{1,0:T(8,128)(2,1)S(1)}) custom-call(bf16[48,32,1024]{2,1,0:T(8,128)(2,1)S(1)} %copy-done.6, bf16[4,1056,128]{2,1,0:T(8,128)(2,1)S(1)} %all-to-all-done.3.refs_1_, f32[4,8,128]{2,1,0:T(8,128)S(1)} %dynamic_update_slice.3.refs_2_), custom_call_target="tpu_custom_call" | custom-call | flops 1610612736 | bytes 5488640 | tf_op jit(solution)/shard_map/pallas_call | solution.py:26
  105.5 13.4 %all_to_all.57 = f32[32,8,128]{2,1,0:T(8,128)S(1)} all-to-all(f32[32,8,128]{2,1,0:T(8,128)S(1)} %get-tuple-element.20), channel_id=1, replica_groups=mesh['y'=4,'core'=2,'x'=4,'z'=8] {'x','z'}, dimensions={0} | all-to-all | bytes 262144 | tf_op jit(solution)/shard_map/all_to_all | solution.py:16
  118.9 12.7 %all_to_all.58.refs_1_ = f32[32,8,128]{2,1,0:T(8,128)S(1)} all-to-all(f32[32,8,128]{2,1,0:T(8,128)S(1)} %broadcast_in_dim.5), channel_id=1, replica_groups=mesh['y'=4,'core'=2,'x'=4,'z'=8] {'x','z'}, dimensions={0} | all-to-all | bytes 262144 | tf_op jit(solution)/shard_map/all_to_all | solution.py:16
  132.0 1.8 shard_map.117
  133.8 2.6 copy-done
  136.4 1.9 copy-done.7
  138.3 5.5 %shard_map.118 = bf16[4,1056,128]{2,1,0:T(8,128)(2,1)} custom-call(bf16[48,32,1024]{2,1,0:T(8,128)(2,1)S(1)} %copy-done.7, bf16[1024,512]{1,0:T(8,128)(2,1)S(1)} %get-tuple-element.23.right_ref.refs_1_, f32[48,512]{1,0:T(8,128)S(1)} %get-tuple-element.26.refs_2_, bf16[1536,512]{1,0:T(8,128)(2,1)S(1)} %get-tuple-element.24.outer_ref.refs_3_), custom_call_target="tpu_custom_call" | custom-call | flops 3221225472 | bytes 6946816 | tf_op jit(solution)/shard_map/pallas_call | solution.py:26
  143.7 3.5 %all-to-all-start.6 = ((bf16[4,1056,128]{2,1,0:T(8,128)(2,1)}), bf16[4,1056,128]{2,1,0:T(8,128)(2,1)S(1)}, u32[]{:S(2)}, u32[]{:S(2)}) async-start(bf16[4,1056,128]{2,1,0:T(8,128)(2,1)} %shard_map.118), calls=%async_computation.6 | async-start | bytes 2162688 | tf_op jit(solution)/shard_map/all_to_all | solution.py:16
  148.0 9.6 %all-to-all-done.6.refs_0_.refs_1_ = bf16[4,1056,128]{2,1,0:T(8,128)(2,1)S(1)} async-done(((bf16[4,1056,128]{2,1,0:T(8,128)(2,1)}), bf16[4,1056,128]{2,1,0:T(8,128)(2,1)S(1)}, u32[]{:S(2)}, u32[]{:S(2)}) %all-to-all-start.6) | async-done | bytes 1081376 | tf_op jit(solution)/shard_map/all_to_all | solution.py:16
  157.8 11.7 %all_to_all.59.refs_2_ = bf16[8,128,128]{2,1,0:T(8,128)(2,1)S(1)} all-to-all(bf16[8,128,128]{2,1,0:T(8,128)(2,1)S(1)} %shard_map.119), channel_id=1, replica_groups=mesh['y'=4,'core'=2,'x'=4,'z'=8] {'z'}, dimensions={0} | all-to-all | bytes 524288 | tf_op jit(solution)/shard_map/all_to_all | solution.py:16
  169.5 0.9 shard_map.120
  170.5 12.0 %all-to-all-start.8 = ((bf16[64,32,128]{2,1,0:T(8,128)(2,1)}), bf16[64,32,128]{2,1,0:T(8,128)(2,1)S(1)}, u32[]{:S(2)}, u32[]{:S(2)}) async-start(bf16[64,32,128]{2,1,0:T(8,128)(2,1)} %shard_map.120), calls=%async_computation.8 | async-start | bytes 1048576 | tf_op jit(solution)/shard_map/all_to_all | solution.py:16
  182.5 17.1 %all-to-all-done.8.refs_0_ = bf16[64,32,128]{2,1,0:T(8,128)(2,1)S(1)} async-done(((bf16[64,32,128]{2,1,0:T(8,128)(2,1)}), bf16[64,32,128]{2,1,0:T(8,128)(2,1)S(1)}, u32[]{:S(2)}, u32[]{:S(2)}) %all-to-all-start.8) | async-done | bytes 524320 | tf_op jit(solution)/shard_map/all_to_all | solution.py:16
  199.6 1.4 copy-done.4
  201.5 8.3 %all_to_all.60.got_ref = bf16[4,160,256]{2,1,0:T(8,128)(2,1)S(1)} all-to-all(bf16[4,160,256]{2,1,0:T(8,128)(2,1)S(1)} %shard_map.121), channel_id=1, replica_groups=mesh['y'=4,'core'=2,'x'=4,'z'=8] {'x'}, dimensions={0} | all-to-all | bytes 655360 | tf_op jit(solution)/shard_map/all_to_all | solution.py:16
  210.7 6.7 %all-to-all-start.10 = ((bf16[8,160,256]{2,1,0:T(8,128)(2,1)}), bf16[8,160,256]{2,1,0:T(8,128)(2,1)S(1)}, u32[]{:S(2)}, u32[]{:S(2)}) async-start(bf16[8,160,256]{2,1,0:T(8,128)(2,1)} %shard_map.122), calls=%async_computation.10 | async-start | bytes 1310720 | tf_op jit(solution)/shard_map/all_to_all | solution.py:16
  217.9 14.0 %all-to-all-done.10.got_ref = bf16[8,160,256]{2,1,0:T(8,128)(2,1)S(1)} async-done(((bf16[8,160,256]{2,1,0:T(8,128)(2,1)}), bf16[8,160,256]{2,1,0:T(8,128)(2,1)S(1)}, u32[]{:S(2)}, u32[]{:S(2)}) %all-to-all-start.10) | async-done | bytes 655392 | tf_op jit(solution)/shard_map/all_to_all | solution.py:16
  232.8 20.8 %all-reduce.2.cloned.1.call-done.wide_ref = f32[1536,1024]{1,0:T(8,128)} async-done(((f32[1536,1024]{1,0:T(8,128)}), f32[1536,1024]{1,0:T(8,128)}) %all-reduce.2.cloned.1.call-update) | async-done | bytes 6291472 | tf_op jit(solution)/shard_map/psum | solution.py:337
  253.6 2.8 %copy-done.1 = f32[1536,1024]{1,0:T(8,128)S(1)} copy-done((f32[1536,1024]{1,0:T(8,128)S(1)}, f32[1536,1024]{1,0:T(8,128)}, u32[]{:S(2)}) %copy-start.1) | copy-done | bytes 6291480
  256.4 2.0 shard_map.124
  (35 shorter events, 8.2 us)
Async XLA Ops:
  8.0 33.3 %all-gather.5.cloned.1.call-start = ((), (), s32[]{:S(2)}) async-start(), calls=%async_computation.12 | async-start | bytes 1638400 | tf_op jit(solution)/shard_map/all_gather | solution.py:256
  10.5 1.7 copy-start.3
  33.7 33.0 %copy-start.2 = (bf16[16,16,640]{2,1,0:T(8,128)(2,1)}, bf16[16,16,640]{2,1,0:T(8,128)(2,1)S(1)}, u32[]{:S(2)}) copy-start(bf16[16,16,640]{2,1,0:T(8,128)(2,1)S(1)} %all_to_all.55.refs_1_) | copy-start | bytes 983044
  41.3 1.3 copy-start.5
  67.5 15.4 %all-to-all-start.2 = ((bf16[8,128,128]{2,1,0:T(8,128)(2,1)}), bf16[8,128,128]{2,1,0:T(8,128)(2,1)S(1)}, u32[]{:S(2)}, u32[]{:S(2)}) async-start(bf16[8,128,128]{2,1,0:T(8,128)(2,1)} %get-tuple-element.18), calls=%async_computation.2 | async-start | bytes 524288 | tf_op jit(solution)/shard_map/all_to_all | solution.py:16
  72.1 110.3 %all-gather.7.cloned.1.call-start = ((), (), s32[]{:S(2)}) async-start(), calls=%async_computation.13 | async-start | bytes 1638400 | tf_op jit(solution)/shard_map/all_gather | solution.py:265
  82.8 4.7 %copy-start.8 = (s32[1,16]{1,0:T(1,128)S(1)}, s32[1,16]{1,0:T(1,128)}, u32[]{:S(2)}) copy-start(s32[1,16]{1,0:T(1,128)} %param.12) | copy-start | bytes 196
  82.8 4.7 %copy-start.9 = (s32[1,16]{1,0:T(1,128)S(1)}, s32[1,16]{1,0:T(1,128)}, u32[]{:S(2)}) copy-start(s32[1,16]{1,0:T(1,128)} %param.11) | copy-start | bytes 196
  84.0 16.8 %all-to-all-start.3 = ((bf16[4,1056,128]{2,1,0:T(8,128)(2,1)}), bf16[4,1056,128]{2,1,0:T(8,128)(2,1)S(1)}, u32[]{:S(2)}, u32[]{:S(2)}) async-start(bf16[4,1056,128]{2,1,0:T(8,128)(2,1)} %shard_map.114), calls=%async_computation.3 | async-start | bytes 2162688 | tf_op jit(solution)/shard_map/all_to_all | solution.py:16
  100.7 1.9 copy-start.6
  133.8 2.6 copy-start
  136.4 1.9 copy-start.7
  143.7 13.9 %all-to-all-start.6 = ((bf16[4,1056,128]{2,1,0:T(8,128)(2,1)}), bf16[4,1056,128]{2,1,0:T(8,128)(2,1)S(1)}, u32[]{:S(2)}, u32[]{:S(2)}) async-start(bf16[4,1056,128]{2,1,0:T(8,128)(2,1)} %shard_map.118), calls=%async_computation.6 | async-start | bytes 2162688 | tf_op jit(solution)/shard_map/all_to_all | solution.py:16
  147.3 106.4 %all-reduce.2.cloned.1.call-start = ((), (), s32[]{:S(2)}) async-start(), calls=%async_computation.11 | async-start | bytes 12582912 | tf_op jit(solution)/shard_map/psum | solution.py:337
  170.5 29.1 %all-to-all-start.8 = ((bf16[64,32,128]{2,1,0:T(8,128)(2,1)}), bf16[64,32,128]{2,1,0:T(8,128)(2,1)S(1)}, u32[]{:S(2)}, u32[]{:S(2)}) async-start(bf16[64,32,128]{2,1,0:T(8,128)(2,1)} %shard_map.120), calls=%async_computation.8 | async-start | bytes 1048576 | tf_op jit(solution)/shard_map/all_to_all | solution.py:16
  199.5 1.4 copy-start.4
  210.7 21.3 %all-to-all-start.10 = ((bf16[8,160,256]{2,1,0:T(8,128)(2,1)}), bf16[8,160,256]{2,1,0:T(8,128)(2,1)S(1)}, u32[]{:S(2)}, u32[]{:S(2)}) async-start(bf16[8,160,256]{2,1,0:T(8,128)(2,1)} %shard_map.122), calls=%async_computation.10 | async-start | bytes 1310720 | tf_op jit(solution)/shard_map/all_to_all | solution.py:16
  253.6 2.8 %copy-start.1 = (f32[1536,1024]{1,0:T(8,128)S(1)}, f32[1536,1024]{1,0:T(8,128)}, u32[]{:S(2)}) copy-start(f32[1536,1024]{1,0:T(8,128)} %all-reduce.2.cloned.1.call-done.wide_ref) | copy-start | bytes 18874372
Sparse Core Ops, SparseCore 0:
  11.2 30.0 all-gather.4
  150.5 103.1 all-reduce.1
Sparse Core Ops, SparseCore 1:
  75.0 27.0 all-gather.6

commit v6 on v5

--- a/solution.py
+++ b/solution.py
@@ -171,36 +171,26 @@
         for z in range(nz):
             for x in range(nx):
                 at = (x * nz + z) * inner
-                spot = (z * nx + x) * inner
-                out_ref[to, spot : spot + inner, :] = right_sum[at : at + inner, lanes]
-        out_ref[to, full : full + inner, :] = left_sum[:, lanes]
-
-
-def flat_body(outer_ref, right_ref, out_ref):
-    out_ref[...] = dot(outer_ref[...], right_ref[...], 1, 1)
-
-
-def round_body(wide_ref, out_ref):
-    out_ref[...] = wide_ref[...].astype(BF16)
-
-
-def fold_body(nx, nz, got_ref, out_ref):
-    _, rows, _ = out_ref.shape
-    for z in range(nz):
-        block = got_ref[0, z * rows : (z + 1) * rows, :].astype(F32)
-        for x in range(1, nx):
-            block = block + got_ref[x, z * rows : (z + 1) * rows, :].astype(F32)
-        out_ref[z] = block.astype(BF16)
-
-
-def lower_body(ny, nx, nz, inner, pre_ref, left_got, right_got, out_ref):
-    full = nx * nz * inner
+                rows = slice(x * inner, (x + 1) * inner)
+                out_ref[to * nz + z, rows, :] = right_sum[at : at + inner, lanes]
+            out_ref[to * nz + z, nx * inner : (nx + 1) * inner, :] = left_sum[:, lanes]
+
+
+def flat_body(outer_ref, right_ref, *outs):
+    take = outs[0].shape[0]
+    for i, out_ref in enumerate(outs):
+        out_ref[...] = dot(outer_ref[i * take : (i + 1) * take], right_ref[...], 1, 1).astype(BF16)
+
+
+def lower_body(ny, nx, nz, inner, z_ref, pre_ref, got_ref, out_ref):
+    rows = nx * inner
     grad_left = jnp.concatenate(
-        [left_got[x, full : full + inner, :].astype(F32) for x in range(nx)], axis=0
+        [got_ref[x * nz + z_ref[0], rows : rows + inner, :].astype(F32) for x in range(nx)],
+        axis=0,
     )
-    grad_right = right_got[0].astype(F32)
-    for z in range(1, nz):
-        grad_right = grad_right + right_got[z].astype(F32)
+    grad_right = got_ref[0, :rows, :].astype(F32)
+    for i in range(1, nx * nz):
+        grad_right = grad_right + got_ref[i, :rows, :].astype(F32)
     take = grad_left.shape[0] // ny
     for side, grad in enumerate((grad_left, grad_right)):
         _, back = jax.vjp(jax.nn.gelu, pre_ref[side])
@@ -317,37 +307,26 @@
             (left, scores),
         )
         span_loss = lax.dynamic_slice_in_dim(loss, seq_index * own, own, 1)
-        (flat,) = call(
+        flat = call(
             flat_body,
-            [shape((labels * inner, full), F32)],
+            [shape((labels * inner // 2, full), BF16)] * 2,
             (outer, right),
             flops=2 * labels * inner * full * spans,
         )
         flat, slope = lax.optimization_barrier((flat, slope))
         (grad_pay,) = call(
             lambda *refs: back_body(nx, nz, inner, *refs),
-            [shape((nx, full + inner, group), BF16)],
+            [shape((nx * nz, rows + inner, group), BF16)],
             (biaffine, right, slope, outer),
             flops=4 * labels * inner * full * spans,
         )
-        grad_got = exchange(grad_pay, "x")
-        (grad_biaffine,) = call(
-            round_body,
-            [shape((labels * inner, full), BF16)],
-            (lax.psum(flat, ("y", "core")),),
-            room=32,
-        )
-        grad_biaffine = grad_biaffine.reshape(labels, inner, full)
-        (fold_pay,) = call(
-            lambda *refs: fold_body(nx, nz, *refs),
-            [shape((nz, rows, group), BF16)],
-            (grad_got,),
-        )
-        fold_got = exchange(fold_pay, "z")
+        grad_got = exchange(grad_pay, ("x", "z"))
+        grad_biaffine = jnp.concatenate(lax.psum(tuple(flat), ("y", "core")), axis=0).reshape(labels, inner, full)
         (lowered,) = call(
             lambda *refs: lower_body(ny, nx, nz, inner, *refs),
             [shape((ny * CORES * nz, rows // ny, group), BF16)],
-            (pre, grad_got, fold_got),
+            (z_index.reshape(1), pre, grad_got),
+            smem=(0,),
         )
         lowered_got = exchange(lowered, ("y", "core", "z"))
         (grad_parts,) = call(

time: 267 us -> 260 us (0.974)
  waiting for transfers between devices: 93.4 us -> 82.3 us
  other arithmetic: 2.47 us -> 6.32 us
  blocking collectives: 90.1 us -> 93.5 us
  local copies, waits for them, and re-layouts: 14.5 us -> 11.3 us
    all_to_all x5 -> x4, waiting for transfers between devices: 63.7 us -> 54.3 us  [exchange(): return lax.all_to_all(parts, axes, split_axis=0, concat_axis=0, tiled=True)]
    concatenate x0 -> x1, other arithmetic: none -> 3.85 us  [shards(): jnp.concatenate(lax.psum(tuple(flat), ('y', 'core')), axis=0)]
    all_to_all x6, blocking collectives: 90.1 us -> 93.5 us  [exchange(): return lax.all_to_all(parts, axes, split_axis=0, concat_axis=0, tiled=True)]
    unnamed x20 -> x22, local copies, waits for them, and re-layouts: 13.6 us -> 10.4 us
    pallas_call x14 -> x12, Pallas kernels: 19.3 us -> 18.3 us  [call(): pl.pallas_call(body, out_shape=tuple(outs), in_specs=specs, out_specs=tup...]
    all_to_all x5 -> x4, starting transfers between devices: 30.4 us -> 30.6 us  [exchange(): return lax.all_to_all(parts, axes, split_axis=0, concat_axis=0, tiled=True)]
  transfers between devices with their start and end apart: 8 -> 7, of which waited for: 7 -> 5; matrix products, arithmetic and copies ran while one was open for 1% -> 2% of each run, Pallas kernels for 6% -> 1%
where the time goes in v6:
time: 260 us; the launch traced here: 258 us
  blocking collectives  93.5 us (36%)
  waiting for transfers between devices  82.3 us (32%)
  starting transfers between devices  30.7 us (12%)
  Pallas kernels  18.3 us (7%)
  between operations  15.6 us (6%)
  local copies, waits for them, and re-layouts  11.3 us (4%)
  other arithmetic  6.32 us (2%)
    all_to_all x6, blocking collectives, exchange(): return lax.all_to_all(parts, axes, split_axis=0, concat_axis=0, tiled=True)  93.5 us
    all_to_all x4, waiting for transfers between devices, exchange(): return lax.all_to_all(parts, axes, split_axis=0, concat_axis=0, tiled=True)  54.3 us
    all_to_all x4, starting transfers between devices, exchange(): return lax.all_to_all(parts, axes, split_axis=0, concat_axis=0, tiled=True)  30.6 us
    psum x1, waiting for transfers between devices, shards(): lax.psum(tuple(flat), ('y', 'core'))  19.1 us
    pallas_call x12, Pallas kernels, call(): pl.pallas_call(body, out_shape=tuple(outs), in_specs=specs, out_specs=tup...  18.3 us
    unnamed x22, local copies, waits for them, and re-layouts  10.4 us
    all_gather x1, waiting for transfers between devices, shards(): weights = lax.all_gather(side_proj, 'x', axis=0)  7.61 us
  transfers between devices with their start and end apart: 7, of which 5 were waited for; matrix products, arithmetic and copies ran while one was open for 2% of the time, Pallas kernels for 1%

profile of v6, /device:TPU:1, one launch (start us, length us, event | category | flops | bytes accessed | tf_op | source)
XLA Modules:
  0.0 258.1 jit_solution(5393219668219911608)
XLA Ops:
  8.1 1.7 broadcast_select_fusion
  10.5 1.7 copy-done.1
  12.3 0.9 shard_map.111
  13.2 20.5 %all_to_all.50.refs_1_ = bf16[16,16,640]{2,1,0:T(8,128)(2,1)S(1)} all-to-all(bf16[16,16,640]{2,1,0:T(8,128)(2,1)S(1)} %shard_map.111), channel_id=1, replica_groups=mesh['y'=4,'core'=2,'x'=4,'z'=8] {'core','z'}, dimensions={0} | all-to-all | bytes 655360 | tf_op jit(solution)/shard_map/all_to_all | solution.py:16
  33.7 7.6 %all-gather.5.cloned.1.call-done = bf16[640,1024]{1,0:T(8,128)(2,1)} async-done(((bf16[160,1024]{1,0:T(8,128)(2,1)}), bf16[640,1024]{1,0:T(8,128)(2,1)}) %all-gather.5.cloned.1.call-update) | async-done | bytes 1310736 | tf_op jit(solution)/shard_map/all_gather | solution.py:246
  41.3 1.3 copy-done.3
  43.3 23.4 %all_to_all.51.refs_0_ = bf16[16,128,128]{2,1,0:T(8,128)(2,1)S(1)} all-to-all(bf16[16,128,128]{2,1,0:T(8,128)(2,1)S(1)} %shard_map.112), channel_id=1, replica_groups=mesh['y'=4,'core'=2,'x'=4,'z'=8] {'core','z'}, dimensions={0} | all-to-all | bytes 1048576 | tf_op jit(solution)/shard_map/all_to_all | solution.py:16
  66.8 15.2 %all_to_all.52.refs_1_ = bf16[8,128,128]{2,1,0:T(8,128)(2,1)S(1)} all-to-all(bf16[8,128,128]{2,1,0:T(8,128)(2,1)S(1)} %get-tuple-element.21), channel_id=1, replica_groups=mesh['y'=4,'core'=2,'x'=4,'z'=8] {'z'}, dimensions={0} | all-to-all | bytes 524288 | tf_op jit(solution)/shard_map/all_to_all | solution.py:16
  82.0 1.1 shard_map.114
  83.1 3.5 %all-to-all-start.3 = ((bf16[4,1056,128]{2,1,0:T(8,128)(2,1)}), bf16[4,1056,128]{2,1,0:T(8,128)(2,1)S(1)}, u32[]{:S(2)}, u32[]{:S(2)}) async-start(bf16[4,1056,128]{2,1,0:T(8,128)(2,1)} %shard_map.114), calls=%async_computation.3 | async-start | bytes 2162688 | tf_op jit(solution)/shard_map/all_to_all | solution.py:16
  87.0 12.9 %all-to-all-done.3.refs_1_ = bf16[4,1056,128]{2,1,0:T(8,128)(2,1)S(1)} async-done(((bf16[4,1056,128]{2,1,0:T(8,128)(2,1)}), bf16[4,1056,128]{2,1,0:T(8,128)(2,1)S(1)}, u32[]{:S(2)}, u32[]{:S(2)}) %all-to-all-start.3) | async-done | bytes 1081376 | tf_op jit(solution)/shard_map/all_to_all | solution.py:16
  99.9 1.9 copy-done.4
  101.8 2.9 %shard_map.115 = (f32[32,8,128]{2,1,0:T(8,128)S(1)}, f32[32,512]{1,0:T(8,128)S(1)}, bf16[1024,512]{1,0:T(8,128)(2,1)S(1)}) custom-call(bf16[48,32,1024]{2,1,0:T(8,128)(2,1)S(1)} %copy-done.4, bf16[4,1056,128]{2,1,0:T(8,128)(2,1)S(1)} %all-to-all-done.3.refs_1_, f32[4,8,128]{2,1,0:T(8,128)S(1)} %dynamic_update_slice.3.refs_2_), custom_call_target="tpu_custom_call" | custom-call | flops 1610612736 | bytes 5488640 | tf_op jit(solution)/shard_map/pallas_call | solution.py:26
  104.6 1.0 copy-done.6
  105.6 13.3 %all_to_all.53 = f32[32,8,128]{2,1,0:T(8,128)S(1)} all-to-all(f32[32,8,128]{2,1,0:T(8,128)S(1)} %get-tuple-element.23), channel_id=1, replica_groups=mesh['y'=4,'core'=2,'x'=4,'z'=8] {'x','z'}, dimensions={0} | all-to-all | bytes 262144 | tf_op jit(solution)/shard_map/all_to_all | solution.py:16
  119.0 12.7 %all_to_all.54.refs_1_ = f32[32,8,128]{2,1,0:T(8,128)S(1)} all-to-all(f32[32,8,128]{2,1,0:T(8,128)S(1)} %broadcast_in_dim.5), channel_id=1, replica_groups=mesh['y'=4,'core'=2,'x'=4,'z'=8] {'x','z'}, dimensions={0} | all-to-all | bytes 262144 | tf_op jit(solution)/shard_map/all_to_all | solution.py:16
  132.1 1.2 copy-done.7
  133.3 3.4 %shard_map.117 = (bf16[768,1024]{1,0:T(8,128)(2,1)}, bf16[768,1024]{1,0:T(8,128)(2,1)}) custom-call(bf16[1536,512]{1,0:T(8,128)(2,1)S(1)} %get-tuple-element.27.outer_ref.refs_3_, bf16[1024,512]{1,0:T(8,128)(2,1)S(1)} %copy-done.7), custom_call_target="tpu_custom_call" | custom-call | flops 1610612736 | bytes 5767168 | tf_op jit(solution)/shard_map/pallas_call | solution.py:26
  136.7 1.9 copy-done.5
  138.6 5.5 %shard_map.118 = bf16[32,160,128]{2,1,0:T(8,128)(2,1)} custom-call(bf16[48,32,1024]{2,1,0:T(8,128)(2,1)S(1)} %copy-done.5, bf16[1024,512]{1,0:T(8,128)(2,1)S(1)} %copy-done.8, f32[48,512]{1,0:T(8,128)S(1)} %get-tuple-element.31.refs_2_, bf16[1536,512]{1,0:T(8,128)(2,1)S(1)} %get-tuple-element.27.outer_ref.refs_3_), custom_call_target="tpu_custom_call" | custom-call | flops 3221225472 | bytes 7176192 | tf_op jit(solution)/shard_map/pallas_call | solution.py:26
  144.1 4.0 %all-to-all-start.6 = ((bf16[32,160,128]{2,1,0:T(8,128)(2,1)}), bf16[32,160,128]{2,1,0:T(8,128)(2,1)S(1)}, u32[]{:S(2)}, u32[]{:S(2)}) async-start(bf16[32,160,128]{2,1,0:T(8,128)(2,1)} %shard_map.118), calls=%async_computation.6 | async-start | bytes 2621440 | tf_op jit(solution)/shard_map/all_to_all | solution.py:16
  149.4 24.4 %all-to-all-done.6.refs_2_ = bf16[32,160,128]{2,1,0:T(8,128)(2,1)S(1)} async-done(((bf16[32,160,128]{2,1,0:T(8,128)(2,1)}), bf16[32,160,128]{2,1,0:T(8,128)(2,1)S(1)}, u32[]{:S(2)}, u32[]{:S(2)}) %all-to-all-start.6) | async-done | bytes 1310752 | tf_op jit(solution)/shard_map/all_to_all | solution.py:16
  173.8 1.0 shard_map.119
  174.8 16.1 %all-to-all-start.7 = ((bf16[64,32,128]{2,1,0:T(8,128)(2,1)}), bf16[64,32,128]{2,1,0:T(8,128)(2,1)S(1)}, u32[]{:S(2)}, u32[]{:S(2)}) async-start(bf16[64,32,128]{2,1,0:T(8,128)(2,1)} %shard_map.119), calls=%async_computation.7 | async-start | bytes 1048576 | tf_op jit(solution)/shard_map/all_to_all | solution.py:16
  191.0 17.1 %all-to-all-done.7.refs_0_ = bf16[64,32,128]{2,1,0:T(8,128)(2,1)S(1)} async-done(((bf16[64,32,128]{2,1,0:T(8,128)(2,1)}), bf16[64,32,128]{2,1,0:T(8,128)(2,1)S(1)}, u32[]{:S(2)}, u32[]{:S(2)}) %all-to-all-start.7) | async-done | bytes 524320 | tf_op jit(solution)/shard_map/all_to_all | solution.py:16
  208.0 1.3 copy-done.2
  209.9 8.3 %all_to_all.55.got_ref = bf16[4,160,256]{2,1,0:T(8,128)(2,1)S(1)} all-to-all(bf16[4,160,256]{2,1,0:T(8,128)(2,1)S(1)} %shard_map.120), channel_id=1, replica_groups=mesh['y'=4,'core'=2,'x'=4,'z'=8] {'x'}, dimensions={0} | all-to-all | bytes 655360 | tf_op jit(solution)/shard_map/all_to_all | solution.py:16
  218.3 0.9 shard_map.121
  219.2 7.0 %all-to-all-start.9 = ((bf16[8,160,256]{2,1,0:T(8,128)(2,1)}), bf16[8,160,256]{2,1,0:T(8,128)(2,1)S(1)}, u32[]{:S(2)}, u32[]{:S(2)}) async-start(bf16[8,160,256]{2,1,0:T(8,128)(2,1)} %shard_map.121), calls=%async_computation.9 | async-start | bytes 1310720 | tf_op jit(solution)/shard_map/all_to_all | solution.py:16
  226.8 19.1 %all-reduce.3.cloned.1.call-done = (bf16[768,1024]{1,0:T(8,128)(2,1)}, bf16[768,1024]{1,0:T(8,128)(2,1)}) async-done(((bf16[768,1024]{1,0:T(8,128)(2,1)}, bf16[768,1024]{1,0:T(8,128)(2,1)}), (bf16[768,1024]{1,0:T(8,128)(2,1)}, bf16[768,1024]{1,0:T(8,128)(2,1)})) %all-reduce.3.cloned.1.call-update) | async-done | bytes 3145744 | tf_op jit(solution)/shard_map/psum | solution.py:324
  245.9 3.9 %pad_maximum_fusion = bf16[1536,1024]{1,0:T(8,128)(2,1)} fusion(bf16[768,1024]{1,0:T(8,128)(2,1)} %get-tuple-element.36, bf16[768,1024]{1,0:T(8,128)(2,1)} %get-tuple-element.37), kind=kLoop, calls=%fused_computation | loop fusion | flops 6291456 | bytes 6291456 | tf_op jit(solution)/shard_map/concatenate | solution.py:324
  249.7 0.9 shard_map.122
  (34 shorter events, 4.7 us)
Async XLA Ops:
  8.0 33.3 %all-gather.5.cloned.1.call-start = ((), (), s32[]{:S(2)}) async-start(), calls=%async_computation.10 | async-start | bytes 1638400 | tf_op jit(solution)/shard_map/all_gather | solution.py:246
  10.5 1.7 copy-start.1
  33.7 33.0 %copy-start = (bf16[16,16,640]{2,1,0:T(8,128)(2,1)}, bf16[16,16,640]{2,1,0:T(8,128)(2,1)S(1)}, u32[]{:S(2)}) copy-start(bf16[16,16,640]{2,1,0:T(8,128)(2,1)S(1)} %all_to_all.50.refs_1_) | copy-start | bytes 983044
  41.3 1.3 copy-start.3
  82.0 4.7 %copy-start.9 = (s32[1,16]{1,0:T(1,128)S(1)}, s32[1,16]{1,0:T(1,128)}, u32[]{:S(2)}) copy-start(s32[1,16]{1,0:T(1,128)} %param.12) | copy-start | bytes 196
  82.0 4.7 %copy-start.10 = (s32[1,16]{1,0:T(1,128)S(1)}, s32[1,16]{1,0:T(1,128)}, u32[]{:S(2)}) copy-start(s32[1,16]{1,0:T(1,128)} %param.11) | copy-start | bytes 196
  83.1 16.8 %all-to-all-start.3 = ((bf16[4,1056,128]{2,1,0:T(8,128)(2,1)}), bf16[4,1056,128]{2,1,0:T(8,128)(2,1)S(1)}, u32[]{:S(2)}, u32[]{:S(2)}) async-start(bf16[4,1056,128]{2,1,0:T(8,128)(2,1)} %shard_map.114), calls=%async_computation.3 | async-start | bytes 2162688 | tf_op jit(solution)/shard_map/all_to_all | solution.py:16
  99.9 1.9 copy-start.4
  104.6 1.0 copy-start.6
  132.1 1.2 copy-start.7
  133.3 3.4 %copy-start.8 = (bf16[1024,512]{1,0:T(8,128)(2,1)S(1)}, bf16[1024,512]{1,0:T(8,128)(2,1)}, u32[]{:S(2)}) copy-start(bf16[1024,512]{1,0:T(8,128)(2,1)} %copy-done.6) | copy-start | bytes 3145732
  136.7 1.9 copy-start.5
  144.1 29.7 %all-to-all-start.6 = ((bf16[32,160,128]{2,1,0:T(8,128)(2,1)}), bf16[32,160,128]{2,1,0:T(8,128)(2,1)S(1)}, u32[]{:S(2)}, u32[]{:S(2)}) async-start(bf16[32,160,128]{2,1,0:T(8,128)(2,1)} %shard_map.118), calls=%async_computation.6 | async-start | bytes 2621440 | tf_op jit(solution)/shard_map/all_to_all | solution.py:16
  148.1 42.9 %all-gather.7.cloned.1.call-start = ((), (), s32[]{:S(2)}) async-start(), calls=%async_computation.11 | async-start | bytes 1638400 | tf_op jit(solution)/shard_map/all_gather | solution.py:255
  148.6 97.2 %all-reduce.3.cloned.1.call-start = ((), (), s32[]{:S(2)}) async-start(), calls=%async_computation.12 | async-start | bytes 6291456 | tf_op jit(solution)/shard_map/psum | solution.py:324
  174.8 33.2 %all-to-all-start.7 = ((bf16[64,32,128]{2,1,0:T(8,128)(2,1)}), bf16[64,32,128]{2,1,0:T(8,128)(2,1)S(1)}, u32[]{:S(2)}, u32[]{:S(2)}) async-start(bf16[64,32,128]{2,1,0:T(8,128)(2,1)} %shard_map.119), calls=%async_computation.7 | async-start | bytes 1048576 | tf_op jit(solution)/shard_map/all_to_all | solution.py:16
  208.0 1.3 copy-start.2
  219.2 30.6 %all-to-all-start.9 = ((bf16[8,160,256]{2,1,0:T(8,128)(2,1)}), bf16[8,160,256]{2,1,0:T(8,128)(2,1)S(1)}, u32[]{:S(2)}, u32[]{:S(2)}) async-start(bf16[8,160,256]{2,1,0:T(8,128)(2,1)} %shard_map.121), calls=%async_computation.9 | async-start | bytes 1310720 | tf_op jit(solution)/shard_map/all_to_all | solution.py:16
Sparse Core Ops, SparseCore 0:
  11.2 30.0 all-gather.4
  152.5 93.3 all-reduce.2
Sparse Core Ops, SparseCore 1:
  150.9 37.8 all-gather.6

commit v7 on v6

--- a/solution.py
+++ b/solution.py
@@ -297,6 +297,7 @@
         score_sum = jnp.sum(score_got, axis=0)
         scores = exchange(jnp.broadcast_to(score_sum[None], score_got.shape), ("x", "z"))
 
+        scores, all_pieces = lax.optimization_barrier((scores, all_pieces))
         outer, loss, slope = call(
             lambda *refs: slope_body(nx, nz, inner, own, labels, *refs),
             [

time: 260 us -> 253 us (0.973)
  starting transfers between devices: 30.7 us -> 27.3 us
  blocking collectives: 93.5 us -> 90.4 us
    all_to_all x4 -> x5, waiting for transfers between devices: 54.3 us -> 61.1 us  [exchange(): return lax.all_to_all(parts, axes, split_axis=0, concat_axis=0, tiled=True)]
    psum x1, waiting for transfers between devices: 19.1 us -> 13.5 us  [shards(): lax.psum(tuple(flat), ('y', 'core'))]
    all_to_all x4 -> x5, starting transfers between devices: 30.6 us -> 27.2 us  [exchange(): return lax.all_to_all(parts, axes, split_axis=0, concat_axis=0, tiled=True)]
    all_to_all x6 -> x5, blocking collectives: 93.5 us -> 90.4 us  [exchange(): return lax.all_to_all(parts, axes, split_axis=0, concat_axis=0, tiled=True)]
    unnamed x22 -> x20, local copies, waits for them, and re-layouts: 10.4 us -> 8.26 us
  transfers between devices with their start and end apart: 7 -> 8, of which waited for: 5 -> 6; matrix products, arithmetic and copies ran while one was open for 2% -> 2% of each run, Pallas kernels for 1% -> 3%
where the time goes in v7:
time: 253 us; the launch traced here: 251 us
  blocking collectives  90.4 us (36%)
  waiting for transfers between devices  83.5 us (33%)
  starting transfers between devices  27.3 us (11%)
  Pallas kernels  18.3 us (7%)
  between operations  15.6 us (6%)
  local copies, waits for them, and re-layouts  9.83 us (4%)
  other arithmetic  6.32 us (2%)
    all_to_all x5, blocking collectives, exchange(): return lax.all_to_all(parts, axes, split_axis=0, concat_axis=0, tiled=True)  90.4 us
    all_to_all x5, waiting for transfers between devices, exchange(): return lax.all_to_all(parts, axes, split_axis=0, concat_axis=0, tiled=True)  61.1 us
    all_to_all x5, starting transfers between devices, exchange(): return lax.all_to_all(parts, axes, split_axis=0, concat_axis=0, tiled=True)  27.2 us
    pallas_call x12, Pallas kernels, call(): pl.pallas_call(body, out_shape=tuple(outs), in_specs=specs, out_specs=tup...  18.3 us
    psum x1, waiting for transfers between devices, shards(): lax.psum(tuple(flat), ('y', 'core'))  13.5 us
    unnamed x20, local copies, waits for them, and re-layouts  8.26 us
    all_gather x1, waiting for transfers between devices, shards(): weights = lax.all_gather(side_proj, 'x', axis=0)  7.61 us
  transfers between devices with their start and end apart: 8, of which 6 were waited for; matrix products, arithmetic and copies ran while one was open for 2% of the time, Pallas kernels for 3%

profile of v7, /device:TPU:1, one launch (start us, length us, event | category | flops | bytes accessed | tf_op | source)
XLA Modules:
  0.0 251.2 jit_solution(17321329253401722541)
XLA Ops:
  8.1 1.7 broadcast_select_fusion
  10.5 1.7 copy-done.1
  12.3 0.9 shard_map.111
  13.2 20.5 %all_to_all.50.refs_1_ = bf16[16,16,640]{2,1,0:T(8,128)(2,1)S(1)} all-to-all(bf16[16,16,640]{2,1,0:T(8,128)(2,1)S(1)} %shard_map.111), channel_id=1, replica_groups=mesh['y'=4,'core'=2,'x'=4,'z'=8] {'core','z'}, dimensions={0} | all-to-all | bytes 655360 | tf_op jit(solution)/shard_map/all_to_all | solution.py:16
  33.7 7.6 %all-gather.5.cloned.1.call-done = bf16[640,1024]{1,0:T(8,128)(2,1)} async-done(((bf16[160,1024]{1,0:T(8,128)(2,1)}), bf16[640,1024]{1,0:T(8,128)(2,1)}) %all-gather.5.cloned.1.call-update) | async-done | bytes 1310736 | tf_op jit(solution)/shard_map/all_gather | solution.py:246
  41.3 1.3 copy-done.3
  42.6 1.4 shard_map.112
  44.0 8.9 %all-to-all-start.1 = ((bf16[16,128,128]{2,1,0:T(8,128)(2,1)}), bf16[16,128,128]{2,1,0:T(8,128)(2,1)S(1)}, u32[]{:S(2)}, u32[]{:S(2)}) async-start(bf16[16,128,128]{2,1,0:T(8,128)(2,1)} %shard_map.112), calls=%async_computation.1 | async-start | bytes 1048576 | tf_op jit(solution)/shard_map/all_to_all | solution.py:16
  53.5 14.2 %all-to-all-done.1.refs_0_ = bf16[16,128,128]{2,1,0:T(8,128)(2,1)S(1)} async-done(((bf16[16,128,128]{2,1,0:T(8,128)(2,1)}), bf16[16,128,128]{2,1,0:T(8,128)(2,1)S(1)}, u32[]{:S(2)}, u32[]{:S(2)}) %all-to-all-start.1) | async-done | bytes 524320 | tf_op jit(solution)/shard_map/all_to_all | solution.py:16
  67.8 15.2 %all_to_all.51.refs_1_ = bf16[8,128,128]{2,1,0:T(8,128)(2,1)S(1)} all-to-all(bf16[8,128,128]{2,1,0:T(8,128)(2,1)S(1)} %get-tuple-element.23), channel_id=1, replica_groups=mesh['y'=4,'core'=2,'x'=4,'z'=8] {'z'}, dimensions={0} | all-to-all | bytes 524288 | tf_op jit(solution)/shard_map/all_to_all | solution.py:16
  83.0 1.1 shard_map.114
  84.1 3.5 %all-to-all-start.3 = ((bf16[4,1056,128]{2,1,0:T(8,128)(2,1)}), bf16[4,1056,128]{2,1,0:T(8,128)(2,1)S(1)}, u32[]{:S(2)}, u32[]{:S(2)}) async-start(bf16[4,1056,128]{2,1,0:T(8,128)(2,1)} %shard_map.114), calls=%async_computation.3 | async-start | bytes 2162688 | tf_op jit(solution)/shard_map/all_to_all | solution.py:16
  88.0 12.9 %all-to-all-done.3.refs_1_ = bf16[4,1056,128]{2,1,0:T(8,128)(2,1)S(1)} async-done(((bf16[4,1056,128]{2,1,0:T(8,128)(2,1)}), bf16[4,1056,128]{2,1,0:T(8,128)(2,1)S(1)}, u32[]{:S(2)}, u32[]{:S(2)}) %all-to-all-start.3) | async-done | bytes 1081376 | tf_op jit(solution)/shard_map/all_to_all | solution.py:16
  100.9 1.9 copy-done.4
  102.7 2.9 %shard_map.115 = (f32[32,8,128]{2,1,0:T(8,128)S(1)}, f32[32,512]{1,0:T(8,128)S(1)}, bf16[1024,512]{1,0:T(8,128)(2,1)S(1)}) custom-call(bf16[48,32,1024]{2,1,0:T(8,128)(2,1)S(1)} %copy-done.4, bf16[4,1056,128]{2,1,0:T(8,128)(2,1)S(1)} %all-to-all-done.3.refs_1_, f32[4,8,128]{2,1,0:T(8,128)S(1)} %dynamic_update_slice.3.refs_2_), custom_call_target="tpu_custom_call" | custom-call | flops 1610612736 | bytes 5488640 | tf_op jit(solution)/shard_map/pallas_call | solution.py:26
  105.6 13.6 %all_to_all.52 = f32[32,8,128]{2,1,0:T(8,128)S(1)} all-to-all(f32[32,8,128]{2,1,0:T(8,128)S(1)} %get-tuple-element.25), channel_id=1, replica_groups=mesh['y'=4,'core'=2,'x'=4,'z'=8] {'x','z'}, dimensions={0} | all-to-all | bytes 262144 | tf_op jit(solution)/shard_map/all_to_all | solution.py:16
  119.9 3.9 %all-to-all-start.5 = ((f32[32,8,128]{2,1,0:T(8,128)}), f32[32,8,128]{2,1,0:T(8,128)S(1)}, u32[]{:S(2)}, u32[]{:S(2)}) async-start(f32[32,8,128]{2,1,0:T(8,128)} %broadcast_in_dim.5), calls=%async_computation.5 | async-start | bytes 262144 | tf_op jit(solution)/shard_map/all_to_all | solution.py:16
  123.8 9.1 %all-to-all-done.5.refs_1_ = f32[32,8,128]{2,1,0:T(8,128)S(1)} async-done(((f32[32,8,128]{2,1,0:T(8,128)}), f32[32,8,128]{2,1,0:T(8,128)S(1)}, u32[]{:S(2)}, u32[]{:S(2)}) %all-to-all-start.5) | async-done | bytes 131104 | tf_op jit(solution)/shard_map/all_to_all | solution.py:16
  133.2 3.4 %shard_map.117 = (bf16[768,1024]{1,0:T(8,128)(2,1)}, bf16[768,1024]{1,0:T(8,128)(2,1)}) custom-call(bf16[1536,512]{1,0:T(8,128)(2,1)S(1)} %get-tuple-element.30.outer_ref.refs_3_, bf16[1024,512]{1,0:T(8,128)(2,1)S(1)} %get-tuple-element.29.right_ref.refs_1_), custom_call_target="tpu_custom_call" | custom-call | flops 1610612736 | bytes 5767168 | tf_op jit(solution)/shard_map/pallas_call | solution.py:26
  136.6 1.9 copy-done.5
  138.5 1.4 copy-done.7
  139.9 5.5 %shard_map.118 = bf16[32,160,128]{2,1,0:T(8,128)(2,1)} custom-call(bf16[48,32,1024]{2,1,0:T(8,128)(2,1)S(1)} %copy-done.5, bf16[1024,512]{1,0:T(8,128)(2,1)S(1)} %get-tuple-element.29.right_ref.refs_1_, f32[48,512]{1,0:T(8,128)S(1)} %get-tuple-element.34.refs_2_, bf16[1536,512]{1,0:T(8,128)(2,1)S(1)} %copy-done.7), custom_call_target="tpu_custom_call" | custom-call | flops 3221225472 | bytes 7176192 | tf_op jit(solution)/shard_map/pallas_call | solution.py:26
  145.4 4.0 %all-to-all-start.6 = ((bf16[32,160,128]{2,1,0:T(8,128)(2,1)}), bf16[32,160,128]{2,1,0:T(8,128)(2,1)S(1)}, u32[]{:S(2)}, u32[]{:S(2)}) async-start(bf16[32,160,128]{2,1,0:T(8,128)(2,1)} %shard_map.118), calls=%async_computation.6 | async-start | bytes 2621440 | tf_op jit(solution)/shard_map/all_to_all | solution.py:16
  149.4 0.7 all-reduce.3.cloned.1.call-update
  150.2 24.9 %all-to-all-done.6.refs_2_ = bf16[32,160,128]{2,1,0:T(8,128)(2,1)S(1)} async-done(((bf16[32,160,128]{2,1,0:T(8,128)(2,1)}), bf16[32,160,128]{2,1,0:T(8,128)(2,1)S(1)}, u32[]{:S(2)}, u32[]{:S(2)}) %all-to-all-start.6) | async-done | bytes 1310752 | tf_op jit(solution)/shard_map/all_to_all | solution.py:16
  175.3 32.8 %all_to_all.53.refs_0_ = bf16[64,32,128]{2,1,0:T(8,128)(2,1)S(1)} all-to-all(bf16[64,32,128]{2,1,0:T(8,128)(2,1)S(1)} %shard_map.119), channel_id=1, replica_groups=mesh['y'=4,'core'=2,'x'=4,'z'=8] {'y','core','z'}, dimensions={0} | all-to-all | bytes 1048576 | tf_op jit(solution)/shard_map/all_to_all | solution.py:16
  208.7 8.3 %all_to_all.54.got_ref = bf16[4,160,256]{2,1,0:T(8,128)(2,1)S(1)} all-to-all(bf16[4,160,256]{2,1,0:T(8,128)(2,1)S(1)} %shard_map.120), channel_id=1, replica_groups=mesh['y'=4,'core'=2,'x'=4,'z'=8] {'x'}, dimensions={0} | all-to-all | bytes 655360 | tf_op jit(solution)/shard_map/all_to_all | solution.py:16
  217.0 0.9 shard_map.121
  217.9 7.0 %all-to-all-start.9 = ((bf16[8,160,256]{2,1,0:T(8,128)(2,1)}), bf16[8,160,256]{2,1,0:T(8,128)(2,1)S(1)}, u32[]{:S(2)}, u32[]{:S(2)}) async-start(bf16[8,160,256]{2,1,0:T(8,128)(2,1)} %shard_map.121), calls=%async_computation.9 | async-start | bytes 1310720 | tf_op jit(solution)/shard_map/all_to_all | solution.py:16
  225.5 13.5 %all-reduce.3.cloned.1.call-done = (bf16[768,1024]{1,0:T(8,128)(2,1)}, bf16[768,1024]{1,0:T(8,128)(2,1)}) async-done(((bf16[768,1024]{1,0:T(8,128)(2,1)}, bf16[768,1024]{1,0:T(8,128)(2,1)}), (bf16[768,1024]{1,0:T(8,128)(2,1)}, bf16[768,1024]{1,0:T(8,128)(2,1)})) %all-reduce.3.cloned.1.call-update) | async-done | bytes 3145744 | tf_op jit(solution)/shard_map/psum | solution.py:325
  239.0 3.9 %pad_maximum_fusion = bf16[1536,1024]{1,0:T(8,128)(2,1)} fusion(bf16[768,1024]{1,0:T(8,128)(2,1)} %get-tuple-element.40, bf16[768,1024]{1,0:T(8,128)(2,1)} %get-tuple-element.41), kind=kLoop, calls=%fused_computation | loop fusion | flops 6291456 | bytes 6291456 | tf_op jit(solution)/shard_map/concatenate | solution.py:325
  242.9 0.9 shard_map.122
  (33 shorter events, 4.3 us)
Async XLA Ops:
  8.0 33.3 %all-gather.5.cloned.1.call-start = ((), (), s32[]{:S(2)}) async-start(), calls=%async_computation.10 | async-start | bytes 1638400 | tf_op jit(solution)/shard_map/all_gather | solution.py:246
  10.5 1.7 copy-start.1
  33.7 10.4 %copy-start = (bf16[16,16,640]{2,1,0:T(8,128)(2,1)}, bf16[16,16,640]{2,1,0:T(8,128)(2,1)S(1)}, u32[]{:S(2)}) copy-start(bf16[16,16,640]{2,1,0:T(8,128)(2,1)S(1)} %all_to_all.50.refs_1_) | copy-start | bytes 983044
  41.3 1.3 copy-start.3
  44.0 23.7 %all-to-all-start.1 = ((bf16[16,128,128]{2,1,0:T(8,128)(2,1)}), bf16[16,128,128]{2,1,0:T(8,128)(2,1)S(1)}, u32[]{:S(2)}, u32[]{:S(2)}) async-start(bf16[16,128,128]{2,1,0:T(8,128)(2,1)} %shard_map.112), calls=%async_computation.1 | async-start | bytes 1048576 | tf_op jit(solution)/shard_map/all_to_all | solution.py:16
  52.9 70.8 %all-gather.7.cloned.1.call-start = ((), (), s32[]{:S(2)}) async-start(), calls=%async_computation.11 | async-start | bytes 1638400 | tf_op jit(solution)/shard_map/all_gather | solution.py:255
  83.0 4.7 %copy-start.8 = (s32[1,16]{1,0:T(1,128)S(1)}, s32[1,16]{1,0:T(1,128)}, u32[]{:S(2)}) copy-start(s32[1,16]{1,0:T(1,128)} %param.12) | copy-start | bytes 196
  83.0 4.7 %copy-start.9 = (s32[1,16]{1,0:T(1,128)S(1)}, s32[1,16]{1,0:T(1,128)}, u32[]{:S(2)}) copy-start(s32[1,16]{1,0:T(1,128)} %param.11) | copy-start | bytes 196
  84.1 16.8 %all-to-all-start.3 = ((bf16[4,1056,128]{2,1,0:T(8,128)(2,1)}), bf16[4,1056,128]{2,1,0:T(8,128)(2,1)S(1)}, u32[]{:S(2)}, u32[]{:S(2)}) async-start(bf16[4,1056,128]{2,1,0:T(8,128)(2,1)} %shard_map.114), calls=%async_computation.3 | async-start | bytes 2162688 | tf_op jit(solution)/shard_map/all_to_all | solution.py:16
  100.9 1.9 copy-start.4
  119.9 13.0 %all-to-all-start.5 = ((f32[32,8,128]{2,1,0:T(8,128)}), f32[32,8,128]{2,1,0:T(8,128)S(1)}, u32[]{:S(2)}, u32[]{:S(2)}) async-start(f32[32,8,128]{2,1,0:T(8,128)} %broadcast_in_dim.5), calls=%async_computation.5 | async-start | bytes 262144 | tf_op jit(solution)/shard_map/all_to_all | solution.py:16
  133.2 3.4 %copy-start.6 = (bf16[1536,512]{1,0:T(8,128)(2,1)}, bf16[1536,512]{1,0:T(8,128)(2,1)S(1)}, u32[]{:S(2)}) copy-start(bf16[1536,512]{1,0:T(8,128)(2,1)S(1)} %get-tuple-element.30.outer_ref.refs_3_) | copy-start | bytes 4718596
  136.6 1.9 copy-start.5
  138.5 1.4 copy-start.7
  145.4 29.6 %all-to-all-start.6 = ((bf16[32,160,128]{2,1,0:T(8,128)(2,1)}), bf16[32,160,128]{2,1,0:T(8,128)(2,1)S(1)}, u32[]{:S(2)}, u32[]{:S(2)}) async-start(bf16[32,160,128]{2,1,0:T(8,128)(2,1)} %shard_map.118), calls=%async_computation.6 | async-start | bytes 2621440 | tf_op jit(solution)/shard_map/all_to_all | solution.py:16
  149.4 89.6 %all-reduce.3.cloned.1.call-start = ((), (), s32[]{:S(2)}) async-start(), calls=%async_computation.12 | async-start | bytes 6291456 | tf_op jit(solution)/shard_map/psum | solution.py:325
  150.1 58.0 %copy-start.2 = (bf16[64,16,640]{2,1,0:T(8,128)(2,1)S(1)}, bf16[64,16,640]{2,1,0:T(8,128)(2,1)}, u32[]{:S(2)}) copy-start(bf16[64,16,640]{2,1,0:T(8,128)(2,1)} %all-gather.7.cloned.1.call-done) | copy-start | bytes 3932164
  217.9 25.0 %all-to-all-start.9 = ((bf16[8,160,256]{2,1,0:T(8,128)(2,1)}), bf16[8,160,256]{2,1,0:T(8,128)(2,1)S(1)}, u32[]{:S(2)}, u32[]{:S(2)}) async-start(bf16[8,160,256]{2,1,0:T(8,128)(2,1)} %shard_map.121), calls=%async_computation.9 | async-start | bytes 1310720 | tf_op jit(solution)/shard_map/all_to_all | solution.py:16
Sparse Core Ops, SparseCore 0:
  11.2 30.0 all-gather.4
  152.7 86.2 all-reduce.2
Sparse Core Ops, SparseCore 1:
  55.8 26.2 all-gather.6
